TPU v7x, 512 devices: a whole 4x4x16 slice. The times are simulated.
512 devices in a mesh: row: 32 (over z, x_hi), rep: 16 (over x_lo, y, core).
Axes of the slice: x: 4 (x_hi: 2, x_lo: 2; x = x_hi * 2 + x_lo), y: 4, z: 16, core: 2. Of those that a mesh axis runs over, the one named last changes fastest.
Arguments:
- features: float32 [32768, 512], P(('row', 'rep')), may hold values from -6 to 6
- weight: float32 [512, 512], replicated, may hold values from -0.25 to 0.25
- cotangent: float32 [32768, 512], P(('row', 'rep')), may hold values from -6 to 6
- tile_mask: int32 [256, 256], P('row', 'rep'), may hold values from 0 to 1
- row_codes: int32 [2, 32768], P(None, 'row'), may hold values from 1 to 32767
- col_codes: int32 [2, 32768], P(None, 'rep'), may hold values from 1 to 32767
Outputs:
- activated: float32 [32768, 512], P(('row', 'rep'))
- grad_input: float32 [32768, 512], P(('row', 'rep'))
All inputs are finite; a program needn't handle non-finite values.
Results may differ from a plain program's by a relative error of at most 0.0031.
Values may be sent and summed in bfloat16 or wider, within the bound.
No kernel may reach another device: no remote copies, remote signals or barrier semaphores. Data moves between devices by JAX's collectives and lax.ppermute only.
A program may use at most 64 MiB of HBM per device.

v0:
```python
import jax
import jax.numpy as jnp
from jax import lax
from jax.sharding import PartitionSpec as P

HIGHEST = lax.Precision.HIGHEST
hash_prime = 65521


def build_adjacency(tile_mask, row_codes, col_codes):
    row_tiles, col_tiles = tile_mask.shape
    rows_block = row_codes.shape[1]
    columns = col_codes.shape[1]
    tile_side = rows_block // row_tiles
    rep_index = lax.axis_index("rep")
    rep_count = lax.axis_size("rep")
    per_mille = 10 + 20 * rep_index // max(rep_count - 1, 1)
    threshold = per_mille * hash_prime // 1000
    first_tiles = row_codes[0].reshape(row_tiles, tile_side)
    second_tiles = row_codes[1].reshape(row_tiles, tile_side)

    def one_tile(operands):
        first_code, second_code, mask_row = operands
        hashed = (
            first_code[:, None] * col_codes[0][None, :]
            + second_code[:, None] * col_codes[1][None, :]
        ) % hash_prime
        kept_cells = (hashed < threshold).astype(jnp.int32).reshape(tile_side, col_tiles, tile_side)
        kept_cells = kept_cells * mask_row[None, :, None]
        return kept_cells.reshape(tile_side, columns).astype(jnp.bfloat16)

    built_rows = lax.map(one_tile, (first_tiles, second_tiles, tile_mask))
    return built_rows.reshape(rows_block, columns)


def times_transpose(left, weight):
    return lax.dot_general(
        left,
        weight,
        (((1,), (1,)), ((), ())),
        precision=HIGHEST,
        preferred_element_type=jnp.float32,
    )


def per_device(features, weight, cotangent, tile_mask, row_codes, col_codes):
    adjacency = build_adjacency(tile_mask, row_codes, col_codes)
    degree_part = jnp.sum(adjacency, axis=1, dtype=jnp.float32)
    features_low = features.astype(jnp.bfloat16)
    column_block = adjacency
    aggregate = jnp.dot(
        column_block,
        lax.all_gather(features_low, "row", axis=0, tiled=True),
        preferred_element_type=jnp.float32,
    )
    block_sum, degree = (
        lax.psum_scatter(aggregate, "rep", scatter_dimension=0, tiled=True),
        lax.psum_scatter(degree_part, "rep", scatter_dimension=0, tiled=True),
    )
    row_scale = lax.rsqrt(1.0 + degree)[:, None]
    hidden = (features + block_sum) * row_scale
    pre_act = jnp.dot(hidden, weight, precision=HIGHEST, preferred_element_type=jnp.float32)
    activated = jax.nn.softplus(pre_act)
    pulled = cotangent * jax.nn.sigmoid(pre_act) * row_scale
    pulled_block = lax.all_gather(pulled.astype(jnp.bfloat16), "rep", axis=0, tiled=True)
    column_block = adjacency
    back_sum = lax.psum_scatter(
        lax.dot_general(
            column_block, pulled_block, (((0,), (0,)), ((), ())), preferred_element_type=jnp.float32
        ),
        "row",
        scatter_dimension=0,
        tiled=True,
    )
    grad_input = times_transpose(pulled + back_sum, weight)
    return (activated, grad_input)


def solution(mesh):
    in_specs = (
        P(("row", "rep"), None),
        P(),
        P(("row", "rep"), None),
        P("row", "rep"),
        P(None, "row"),
        P(None, "rep"),
    )
    out_specs = (P(("row", "rep"), None), P(("row", "rep"), None))
    return jax.shard_map(
        per_device, mesh=mesh, in_specs=in_specs, out_specs=out_specs, check_vma=False
    )
```

profile of v0, /device:TPU:8, one launch (start us, length us, event | category | flops | bytes accessed | tf_op | source)
XLA Modules:
  0.0 981.4 jit_solution(12139800078560651348)
XLA Ops:
  7.2 1.6 convert_element_type.27
  9.0 0.8 fusion.17
  9.8 25.4 %while.12 = (s32[]{:T(128)}, bf16[8,128,2048]{2,1,0:T(8,128)(2,1)}, s32[8,128]{1,0:T(8,128)S(1)}, s32[2,2048]{1,0:T(2,128)}, s32[8,128]{1,0:T(8,128)S(1)}, /*index=5*/s32[]{:T(128)}, s32[8,16]{1,0:T(8,128)}, s32[]{:T(128)}) while((s32[]{:T(128)}, bf16[8,128,2048]{2,1,0:T(8,128)(2,1)}, s32[8,128]{1,0:T(8,128)S(1)}, s32[2,2048]{1,0:T(2,128)}, ...), condition=%wide.region_1.2_spmd, body=%wide.region_0.1_spmd.sunk | while | flops 3145730 | bytes 594205 | solution.py:32
  9.8 0.7 fusion.30
  10.5 0.1 broadcast_bitcast_fusion.2
  10.6 0.8 fusion.31
  11.4 1.6 fusion.33
  13.0 0.7 fusion.30
  13.7 0.1 broadcast_bitcast_fusion.2
  13.7 0.8 fusion.31
  14.6 1.6 fusion.33
  16.1 0.7 fusion.30
  16.8 0.1 broadcast_bitcast_fusion.2
  16.9 0.8 fusion.31
  17.7 1.6 fusion.33
  19.3 0.7 fusion.30
  20.0 0.1 broadcast_bitcast_fusion.2
  20.1 0.8 fusion.31
  20.9 1.6 fusion.33
  22.5 0.7 fusion.30
  23.2 0.1 broadcast_bitcast_fusion.2
  23.2 0.8 fusion.31
  24.0 1.6 fusion.33
  25.6 0.7 fusion.30
  26.3 0.1 broadcast_bitcast_fusion.2
  26.4 0.8 fusion.31
  27.2 1.6 fusion.33
  28.8 0.7 fusion.30
  29.5 0.1 broadcast_bitcast_fusion.2
  29.6 0.8 fusion.31
  30.4 1.6 fusion.33
  31.9 0.7 fusion.30
  32.6 0.1 broadcast_bitcast_fusion.2
  32.7 0.8 fusion.31
  33.5 1.6 fusion.33
  35.1 131.1 %all-gather.3.cloned.1.call-done = bf16[2048,512]{1,0:T(8,128)(2,1)} async-done(((bf16[64,512]{1,0:T(8,128)(2,1)}), bf16[2048,512]{1,0:T(8,128)(2,1)}) %all-gather.3.cloned.1.call-update) | async-done | bytes 2097168 | tf_op jit(solution)/shard_map/all_gather | solution.py:53
  166.2 6.5 fusion.18
  172.8 1.3 dynamic-slice
  174.8 2.8 convert_reduce_fusion
  177.6 23.4 %all-reduce = f32[1024]{0:T(1024)S(1)} all-reduce(f32[1024]{0:T(1024)S(1)} %bitcast.35), channel_id=3, replica_groups=mesh['row'=32,'rep'=16] {'rep'}, use_global_device_ids=true, to_apply=%region_4.5.clone | all-reduce | flops 1024 | bytes 8192
  200.9 0.1 fusion.14
  201.0 33.3 %reduce-scatter.3.cloned.1.call-done = f32[64,512]{1,0:T(8,128)} async-done(((f32[1024,512]{1,0:T(8,128)}), f32[64,512]{1,0:T(8,128)}) %reduce-scatter.3.cloned.1.call-update) | async-done | bytes 131088 | tf_op jit(solution)/shard_map/reduce_scatter | solution.py:57
  234.3 2.4 fusion.15
  236.8 0.0 reduce-scatter.5.cloned.1.call-start
  236.8 42.6 %all-gather.5.cloned.1.call-done = bf16[1024,512]{1,0:T(8,128)(2,1)} async-done(((bf16[64,512]{1,0:T(8,128)(2,1)}), bf16[1024,512]{1,0:T(8,128)(2,1)}) %all-gather.5.cloned.1.call-update) | async-done | bytes 1048592 | tf_op jit(solution)/shard_map/all_gather | solution.py:65
  279.4 6.8 fusion.19
  286.2 686.0 %reduce-scatter.5.cloned.1.call-done = f32[64,512]{1,0:T(8,128)} async-done(((f32[2048,512]{1,0:T(8,128)}), f32[64,512]{1,0:T(8,128)}) %reduce-scatter.5.cloned.1.call-update) | async-done | bytes 131088 | tf_op jit(solution)/shard_map/reduce_scatter | solution.py:67
  972.2 2.7 fusion.8
  (22 shorter events, 0.2 us)
Async XLA Ops:
  7.2 227.1 %copy-start = (f32[512,512]{1,0:T(8,128)S(1)}, f32[512,512]{1,0:T(8,128)}, u32[]{:S(2)}) copy-start(f32[512,512]{1,0:T(8,128)} %param.9) | copy-start | bytes 3145732
  7.2 159.1 %all-gather.3.cloned.1.call-start = ((), (), s32[]{:S(2)}) async-start(), calls=%async_computation.2 | async-start | bytes 2162688 | tf_op jit(solution)/shard_map/all_gather | solution.py:53
  8.9 225.4 %reduce-scatter.3.cloned.1.call-start = ((), (), s32[]{:S(2)}) async-start(), calls=%async_computation.3 | async-start | bytes 2228224 | tf_op jit(solution)/shard_map/reduce_scatter | solution.py:57
  172.7 61.6 %copy-start.1 = (f32[64,512]{1,0:T(8,128)S(1)}, f32[64,512]{1,0:T(8,128)}, u32[]{:S(2)}) copy-start(f32[64,512]{1,0:T(8,128)} %param.10) | copy-start | bytes 393220
  172.7 61.6 %copy-start.2 = (f32[64,512]{1,0:T(8,128)S(1)}, f32[64,512]{1,0:T(8,128)}, u32[]{:S(2)}) copy-start(f32[64,512]{1,0:T(8,128)} %param.8) | copy-start | bytes 393220
  172.8 106.6 %all-gather.5.cloned.1.call-start = ((), (), s32[]{:S(2)}) async-start(), calls=%async_computation.4 | async-start | bytes 1114112 | tf_op jit(solution)/shard_map/all_gather | solution.py:65
  236.8 735.4 %reduce-scatter.5.cloned.1.call-start = ((), (), s32[]{:S(2)}) async-start(), calls=%async_computation.5 | async-start | bytes 4325376 | tf_op jit(solution)/shard_map/reduce_scatter | solution.py:67
Sparse Core Ops, SparseCore 0:
  11.7 154.4 all-gather.2
  172.9 61.3 reduce-scatter.2
  237.0 42.3 all-gather.4
  286.3 685.8 reduce-scatter.4
where the time goes:
time: 984 us; the launch traced here: 981 us
  waiting for transfers between devices  893 us (91%)
  blocking collectives  23.4 us (2%)
  matrix products  18.4 us (2%)
  other arithmetic  17.2 us (2%)
  local copies, waits for them, and re-layouts  14.7 us (1%)
  between operations  14.5 us (1%)
    reduce_scatter x1, waiting for transfers between devices, per_device(): lax.psum_scatter(lax.dot_general(column_block, pulled_block, (((0,), (0,)...  686 us
    all_gather x1, waiting for transfers between devices, per_device(): lax.all_gather(features_low, 'row', axis=0, tiled=True)  131 us
    all_gather x1, waiting for transfers between devices, per_device(): lax.all_gather(pulled.astype(jnp.bfloat16), 'rep', axis=0, tiled=True)  42.6 us
    reduce_scatter x1, waiting for transfers between devices, per_device(): lax.psum_scatter(aggregate, 'rep', scatter_dimension=0, tiled=True)  33.3 us
    unnamed x1, blocking collectives  23.4 us
  transfers between devices with their start and end apart: 4, of which 4 were waited for; matrix products, arithmetic and copies ran while one was open for 3% of the time, Pallas kernels for 0%

commit v1 on v0

v1 whole, which is shorter than its diff:
```python
import jax
import jax.numpy as jnp
from jax import lax
from jax.experimental import pallas as pl
from jax.experimental.pallas import tpu as pltpu
from jax.sharding import Mesh, PartitionSpec as P

HIGHEST = lax.Precision.HIGHEST
hash_prime = 65521
N_Z_HI, N_Z_LO, N_X_HI, N_X_LO, N_Y, N_CORE = 4, 4, 2, 2, 4, 2
N_Z = N_Z_HI * N_Z_LO
N_XY = N_X_HI * N_X_LO * N_Y
RPD = 64
F = 512
R = N_XY * RPD
COLS = N_CORE * N_Z * RPD
DIGITS = 16
AXES = ("zh", "zl", "xh", "xl", "y", "c")
XY = ("xh", "xl", "y")


def centred(value):
    residue = value % hash_prime
    return jnp.where(residue > hash_prime // 2, residue - hash_prime, residue)


def two_digits(value):
    high = (value + 128) >> 8
    return value - (high << 8), high << 8


def row_digits(first_code, second_code):
    digits = []
    for code in (first_code, second_code):
        digits.extend(two_digits(code))
        digits.extend(two_digits(centred(code << 8)))
    digits.extend(two_digits(centred((first_code + second_code) << 14)))
    digits.extend([jnp.zeros_like(first_code)] * (DIGITS - len(digits)))
    return jnp.stack(digits, axis=-1).astype(jnp.bfloat16)


def column_digits(first_code, second_code):
    digits = []
    for code in (first_code, second_code):
        low, high = two_digits(code - 16384)
        digits.extend((low, low, high >> 8, high >> 8))
    digits.extend([jnp.ones_like(first_code)] * 2)
    digits.extend([jnp.zeros_like(first_code)] * (DIGITS - len(digits)))
    return jnp.stack(digits, axis=0).astype(jnp.bfloat16)


def adjacency_kernel(left_ref, right_ref, limit_ref, adjacency_ref, degree_ref):
    value = jnp.dot(left_ref[...], right_ref[...], preferred_element_type=jnp.float32)
    residue = value - jnp.round(value * (1.0 / hash_prime)) * float(hash_prime)
    kept = jnp.logical_and(residue >= 0.0, residue < limit_ref[0])
    kept = jnp.where(kept, 1.0, 0.0)
    adjacency_ref[...] = kept.astype(jnp.bfloat16)
    degree_ref[...] = jnp.broadcast_to(jnp.sum(kept, axis=1, keepdims=True), degree_ref.shape)


def build_adjacency(left, right, limit):
    return pl.pallas_call(
        adjacency_kernel,
        grid=(N_XY,),
        in_specs=[
            pl.BlockSpec((RPD, DIGITS), lambda k: (k, 0)),
            pl.BlockSpec((DIGITS, COLS), lambda k: (0, 0)),
            pl.BlockSpec((1, 1, COLS), lambda k: (k, 0, 0)),
        ],
        out_specs=[
            pl.BlockSpec((RPD, COLS), lambda k: (k, 0)),
            pl.BlockSpec((RPD, 128), lambda k: (k, 0)),
        ],
        out_shape=[
            jax.ShapeDtypeStruct((R, COLS), jnp.bfloat16),
            jax.ShapeDtypeStruct((R, 128), jnp.float32),
        ],
        cost_estimate=pl.CostEstimate(flops=2 * R * COLS * DIGITS, bytes_accessed=2 * R * COLS, transcendentals=0),
    )(left, right, limit)


def to_other_core(values):
    return lax.ppermute(values, "c", [(0, 1), (1, 0)])


def exchange(values, axis):
    return lax.all_to_all(values, axis, 0, 0, tiled=True)


def to_all(values, axis, count):
    return exchange(jnp.broadcast_to(values[None], (count,) + values.shape).reshape(-1, values.shape[1]), axis)


def per_device(features, weight, cotangent, tile_mask, row_codes, col_codes):
    x_hi, core = lax.axis_index("xh"), lax.axis_index("c")
    subset = (lax.axis_index("xl") * N_Y + lax.axis_index("y")) * N_CORE + core

    own_rows = lax.dynamic_index_in_dim(row_codes.reshape(2, N_XY // 2, N_CORE, RPD), core, 2, False)
    own_columns = lax.dynamic_index_in_dim(col_codes.reshape(2, N_Z_HI, N_Z_LO, N_X_HI, RPD), x_hi, 3, False)
    own_columns = own_columns.transpose(0, 2, 1, 3)
    own_mask = tile_mask.reshape(N_XY // 2, N_Z_HI, N_Z_LO).transpose(0, 2, 1)
    sizes = (own_rows.size, own_columns.size, own_mask.size)
    small = jnp.concatenate([own_rows.reshape(-1), own_columns.reshape(-1), own_mask.reshape(-1)])
    small = lax.all_gather(small, ("xh", "c"), axis=0).reshape(N_X_HI, N_CORE, -1)
    rows_all = lax.dynamic_index_in_dim(small[:, :, : sizes[0]], core, 1, False)
    rows_all = rows_all.reshape(N_X_HI, 2, N_XY // 2, RPD).transpose(1, 0, 2, 3).reshape(2, R)
    columns_all = lax.dynamic_index_in_dim(small[:, :, sizes[0] : sizes[0] + sizes[1]], x_hi, 0, False)
    columns_all = columns_all.reshape(N_CORE, 2, N_Z * RPD)
    mask_all = small[:, :, sizes[0] + sizes[1] :].reshape(N_X_HI, N_CORE, N_XY // 2, N_Z)
    mask_all = mask_all.transpose(1, 0, 2, 3).reshape(N_CORE, N_XY, N_Z)

    def own_first(values):
        return jnp.where(core == 0, values, values[::-1])

    columns_all = own_first(columns_all).transpose(1, 0, 2).reshape(2, COLS)
    mask_all = own_first(mask_all)
    subsets = jnp.stack([subset, subset ^ 1])
    threshold = (10 + 20 * subsets // 15) * hash_prime // 1000
    limit = (mask_all * threshold[:, None, None]).transpose(1, 0, 2).astype(jnp.float32)
    limit = jnp.repeat(limit.reshape(N_XY, N_CORE * N_Z), RPD, axis=1).reshape(N_XY, 1, COLS)
    left = row_digits(rows_all[0], rows_all[1])
    right = column_digits(columns_all[0], columns_all[1])

    gathered = lax.all_gather(features.astype(jnp.bfloat16), "zh", axis=0, tiled=True)
    gathered = to_all(gathered, "zl", N_Z_LO)
    other = to_other_core(gathered)
    adjacency, degree = build_adjacency(left, right, limit)
    half = COLS // 2
    aggregate = jnp.dot(adjacency[:, :half], gathered, preferred_element_type=jnp.float32)
    aggregate += jnp.dot(adjacency[:, half:], other, preferred_element_type=jnp.float32)
    sent = jnp.concatenate([aggregate, degree], axis=1).astype(jnp.float16)
    arrived = exchange(sent, XY).reshape(N_XY, RPD, F + 128).astype(jnp.float32).sum(axis=0)

    row_scale = lax.rsqrt(1.0 + arrived[:, F : F + 1])
    hidden = (features + arrived[:, :F]) * row_scale
    pre_act = jnp.dot(hidden, weight, precision=HIGHEST, preferred_element_type=jnp.float32)
    activated = jax.nn.softplus(pre_act)
    pulled = cotangent * jax.nn.sigmoid(pre_act) * row_scale

    pulled_block = to_all(pulled.astype(jnp.bfloat16), XY, N_XY)
    contract = (((0,), (0,)), ((), ()))
    term_other = lax.dot_general(adjacency[:, half:], pulled_block, contract, preferred_element_type=jnp.float32)
    from_other = to_other_core(term_other)
    term = lax.dot_general(adjacency[:, :half], pulled_block, contract, preferred_element_type=jnp.float32)
    term = (term + from_other).astype(jnp.bfloat16)
    term = exchange(term, "zl").reshape(N_Z_LO, N_Z_HI * RPD, F).astype(jnp.float32).sum(axis=0)
    term = exchange(term.astype(jnp.bfloat16), "zh").reshape(N_Z_HI, RPD, F).astype(jnp.float32).sum(axis=0)
    grad_input = lax.dot_general(
        pulled + term, weight, (((1,), (1,)), ((), ())), precision=HIGHEST, preferred_element_type=jnp.float32
    )
    return (activated, grad_input)


def solution(mesh):
    inner = Mesh(mesh.devices.reshape(N_Z_HI, N_Z_LO, N_X_HI, N_X_LO, N_Y, N_CORE), AXES)
    row, rep = ("zh", "zl", "xh"), ("xl", "y", "c")
    in_specs = (
        P(row + rep, None),
        P(),
        P(row + rep, None),
        P(row, rep),
        P(None, row),
        P(None, rep),
    )
    out_specs = (P(row + rep, None), P(row + rep, None))
    return jax.shard_map(per_device, mesh=inner, in_specs=in_specs, out_specs=out_specs, check_vma=False)
```

time: 984 us -> 194 us (0.20)
  the two profiles are of different devices: /device:TPU:8 before, /device:TPU:32 now
where the time goes in v1:
time: 194 us; the launch traced here: 193 us
  blocking collectives  138 us (71%)
  waiting for transfers between devices  15.6 us (8%)
  Pallas kernels  10.5 us (5%)
  matrix products  10.1 us (5%)
  starting transfers between devices  8.41 us (4%)
  local copies, waits for them, and re-layouts  5.98 us (3%)
  other arithmetic  3.5 us (2%)
    all_to_all x4, blocking collectives, exchange(): return lax.all_to_all(values, axis, 0, 0, tiled=True)  105 us
    all_gather x1, blocking collectives, per_device(): lax.all_gather(features.astype(jnp.bfloat16), 'zh', axis=0, tiled=True)  26 us
    all_to_all x1, waiting for transfers between devices, exchange(): return lax.all_to_all(values, axis, 0, 0, tiled=True)  11.5 us
    pallas_call x1, Pallas kernels, build_adjacency(): pl.pallas_call(adjacency_kernel, grid=(N_XY,), in_specs=[pl.BlockSpec((RP...  10.5 us
    all_gather x1, blocking collectives, per_device(): lax.all_gather(small, ('xh', 'c'), axis=0).reshape(N_X_HI, N_CORE, -1)  6.74 us
    all_to_all x1, starting transfers between devices, exchange(): return lax.all_to_all(values, axis, 0, 0, tiled=True)  4.58 us
    ppermute x2, waiting for transfers between devices, to_other_core(): return lax.ppermute(values, 'c', [(0, 1), (1, 0)])  4.13 us
  transfers between devices with their start and end apart: 3, of which 2 were waited for; matrix products, arithmetic and copies ran while one was open for 5% of the time, Pallas kernels for 5%

profile of v1, /device:TPU:32, one launch (start us, length us, event | category | flops | bytes accessed | tf_op | source)
XLA Modules:
  0.0 192.9 jit_solution(4855845254187341187)
XLA Ops:
  0.7 1.0 convert_element_type.29
  1.7 26.0 %all_gather.11 = bf16[256,512]{1,0:T(8,128)(2,1)S(1)} all-gather(bf16[64,512]{1,0:T(8,128)(2,1)S(1)} %convert_element_type.29), channel_id=1, replica_groups=mesh['zh'=4,'zl'=4,'xh'=2,'xl'=2,'y'=4,'c'=2] {'zh'}, dimensions={0}, use_global_device_ids=true | all-gather | bytes 327680 | tf_op jit(solution)/shard_map/all_gather | solution.py:124
  27.7 1.1 broadcast_in_dim.7
  28.7 4.6 %all-to-all-start = ((bf16[4,256,512]{2,1,0:T(8,128)(2,1)}), bf16[4,256,512]{2,1,0:T(8,128)(2,1)S(1)}, u32[]{:S(2)}, u32[]{:S(2)}) async-start(bf16[4,256,512]{2,1,0:T(8,128)(2,1)} %broadcast_in_dim.7), calls=%async_computation | async-start | bytes 2097152 | tf_op jit(solution)/shard_map/all_to_all | solution.py:87
  33.3 0.1 copy.53
  33.4 0.1 copy.54
  33.5 0.1 reshape.442
  33.6 0.1 reshape.437
  33.7 0.1 reshape.438
  33.8 0.1 reshape.439
  34.0 0.1 reshape.440
  34.1 6.7 %all-gather.1 = s32[4,1,3200]{2,1,0:T(1,128)S(1)} all-gather(s32[1,1,3200]{2,1,0:T(1,128)S(1)} %reshape.455), channel_id=2, replica_groups=mesh['zh'=4,'zl'=4,'xh'=2,'xl'=2,'y'=4,'c'=2] {'xh','c'}, dimensions={0}, use_global_device_ids=true | all-gather | bytes 64000 | tf_op jit(solution)/shard_map/all_gather | solution.py:104
  40.8 0.1 reduce.3
  41.0 0.1 reshape.446
  41.1 0.1 and_select_fusion.3
  41.2 0.1 fusion.22
  41.3 0.1 reshape.448
  41.4 0.1 reshape.444
  41.5 0.1 squeeze.20
  41.6 0.1 squeeze.19
  41.7 0.2 rev.6
  42.0 11.5 %all-to-all-done = bf16[4,256,512]{2,1,0:T(8,128)(2,1)S(1)} async-done(((bf16[4,256,512]{2,1,0:T(8,128)(2,1)}), bf16[4,256,512]{2,1,0:T(8,128)(2,1)S(1)}, u32[]{:S(2)}, u32[]{:S(2)}) %all-to-all-start) | async-done | bytes 1048608 | tf_op jit(solution)/shard_map/all_to_all | solution.py:87
  53.5 1.9 collective-permute-start
  55.4 0.1 fusion.31
  55.6 0.1 stack.24
  55.7 0.8 copy.57.left_ref
  56.6 0.1 broadcast_in_dim.6
  56.7 0.8 reshape_reshape.3.limit_ref
  57.6 1.4 stack.56.right_ref
  58.9 10.5 %shard_map.77 = (bf16[1024,2048]{1,0:T(8,128)(2,1)}, f32[1024,128]{1,0:T(8,128)}) custom-call(bf16[1024,16]{1,0:T(8,128)(2,1)} %copy.57.left_ref, bf16[16,2048]{1,0:T(8,128)(2,1)} %stack.56.right_ref, f32[16,1,2048]{2,1,0:T(1,128)} %reshape_reshape.3.limit_ref), custom_call_target="tpu_custom_call" | custom-call | flops 67108864 | bytes 4194304 | tf_op jit(solution)/shard_map/pallas_call | solution.py:62
  69.5 1.1 convert.80
  70.6 3.0 %fusion.6 = f32[1024,512]{1,0:T(8,128)S(1)} fusion(bf16[1024,512]{1,0:T(8,128)(2,1)S(1)} %bitcast.56, bf16[1024,2048]{1,0:T(8,128)(2,1)} %get-tuple-element.4), kind=kOutput, calls=%fused_computation.9 | convolution fusion | flops 1073741824 | bytes 5242880 | tf_op jit(solution)/shard_map/dot_general | solution.py:129
  73.6 1.2 add_convert_fusion.1
  74.8 0.4 pad_maximum_fusion
  75.2 27.4 %all_to_all.42 = f16[16,64,640]{2,1,0:T(8,128)(2,1)S(1)} all-to-all(f16[16,64,640]{2,1,0:T(8,128)(2,1)S(1)} %pad_maximum_fusion), channel_id=1, replica_groups=mesh['zh'=4,'zl'=4,'xh'=2,'xl'=2,'y'=4,'c'=2] {'xh','xl','y'}, dimensions={0} | all-to-all | bytes 2621440 | tf_op jit(solution)/shard_map/all_to_all | solution.py:87
  102.6 0.2 convert_reduce_fusion
  102.8 0.1 fusion.19
  102.9 1.5 fusion.32
  104.4 0.1 broadcast_in_dim.8
  104.5 20.1 %all_to_all.43 = bf16[16,64,512]{2,1,0:T(8,128)(2,1)S(1)} all-to-all(bf16[16,64,512]{2,1,0:T(8,128)(2,1)S(1)} %broadcast_in_dim.8), channel_id=1, replica_groups=mesh['zh'=4,'zl'=4,'xh'=2,'xl'=2,'y'=4,'c'=2] {'xh','xl','y'}, dimensions={0} | all-to-all | bytes 2097152 | tf_op jit(solution)/shard_map/all_to_all | solution.py:87
  124.6 1.3 fusion
  125.9 1.9 collective-permute-start.1
  127.8 4.1 %collective-permute-done.1 = f32[1024,512]{1,0:T(8,128)S(1)} collective-permute-done((f32[1024,512]{1,0:T(8,128)S(1)}, f32[1024,512]{1,0:T(8,128)S(1)}, u32[]{:S(2)}, u32[]{:S(2)}) %collective-permute-start.1) | collective-permute-done | bytes 2097184 | tf_op jit(solution)/shard_map/ppermute | solution.py:83
  132.0 1.3 add_convert_fusion
  133.2 30.2 %all_to_all.44 = bf16[4,256,512]{2,1,0:T(8,128)(2,1)S(1)} all-to-all(bf16[4,256,512]{2,1,0:T(8,128)(2,1)S(1)} %bitcast.60), channel_id=1, replica_groups=mesh['zh'=4,'zl'=4,'xh'=2,'xl'=2,'y'=4,'c'=2] {'zl'}, dimensions={0} | all-to-all | bytes 2097152 | tf_op jit(solution)/shard_map/all_to_all | solution.py:87
  163.5 0.2 reduce_sum.31
  163.7 27.3 %all_to_all.45 = bf16[4,64,512]{2,1,0:T(8,128)(2,1)S(1)} all-to-all(bf16[4,64,512]{2,1,0:T(8,128)(2,1)S(1)} %bitcast.54), channel_id=1, replica_groups=mesh['zh'=4,'zl'=4,'xh'=2,'xl'=2,'y'=4,'c'=2] {'zh'}, dimensions={0} | all-to-all | bytes 524288 | tf_op jit(solution)/shard_map/all_to_all | solution.py:87
  191.1 1.8 fusion.15
  (43 shorter events, 0.4 us)
Async XLA Ops:
  0.6 102.3 %copy-start = (f32[512,512]{1,0:T(8,128)S(1)}, f32[512,512]{1,0:T(8,128)}, u32[]{:S(2)}) copy-start(f32[512,512]{1,0:T(8,128)} %param.7) | copy-start | bytes 3145732
  0.6 32.7 %copy-start.5 = (s32[8,16]{1,0:T(8,128)S(1)}, s32[8,16]{1,0:T(8,128)}, u32[]{:S(2)}) copy-start(s32[8,16]{1,0:T(8,128)} %param.9) | copy-start | bytes 1540
  0.7 33.0 %copy-start.4 = (s32[2,1024]{1,0:T(2,128)S(1)}, s32[2,1024]{1,0:T(2,128)}, u32[]{:S(2)}) copy-start(s32[2,1024]{1,0:T(2,128)} %param.10) | copy-start | bytes 24580
  0.7 33.2 %copy-start.3 = (s32[2,2048]{1,0:T(2,128)S(1)}, s32[2,2048]{1,0:T(2,128)}, u32[]{:S(2)}) copy-start(s32[2,2048]{1,0:T(2,128)} %param.11) | copy-start | bytes 49156
  28.7 24.8 %all-to-all-start = ((bf16[4,256,512]{2,1,0:T(8,128)(2,1)}), bf16[4,256,512]{2,1,0:T(8,128)(2,1)S(1)}, u32[]{:S(2)}, u32[]{:S(2)}) async-start(bf16[4,256,512]{2,1,0:T(8,128)(2,1)} %broadcast_in_dim.7), calls=%async_computation | async-start | bytes 2097152 | tf_op jit(solution)/shard_map/all_to_all | solution.py:87
  53.5 20.1 %collective-permute-start = (bf16[1024,512]{1,0:T(8,128)(2,1)S(1)}, bf16[1024,512]{1,0:T(8,128)(2,1)S(1)}, u32[]{:S(2)}, u32[]{:S(2)}) collective-permute-start(bf16[1024,512]{1,0:T(8,128)(2,1)S(1)} %bitcast.55), channel_id=1, source_target_pairs={{0,1},{1,0},{2,3},{3,2},{4,5},{5,4},{6,7},{7,6},{8,9},{9,8},{10,11... | collective-permute-start | bytes 3145736 | tf_op jit(solution)/shard_map/ppermute | solution.py:83
  70.6 3.0 %copy-start.6 = (bf16[1024,2048]{1,0:T(8,128)(2,1)S(1)}, bf16[1024,2048]{1,0:T(8,128)(2,1)}, u32[]{:S(2)}) copy-start(bf16[1024,2048]{1,0:T(8,128)(2,1)} %get-tuple-element.4) | copy-start | bytes 12582916
  75.2 27.7 %copy-start.1 = (f32[64,512]{1,0:T(8,128)S(1)}, f32[64,512]{1,0:T(8,128)}, u32[]{:S(2)}) copy-start(f32[64,512]{1,0:T(8,128)} %param.8) | copy-start | bytes 393220
  75.2 27.7 %copy-start.2 = (f32[64,512]{1,0:T(8,128)S(1)}, f32[64,512]{1,0:T(8,128)}, u32[]{:S(2)}) copy-start(f32[64,512]{1,0:T(8,128)} %param.6) | copy-start | bytes 393220
  125.9 6.1 %collective-permute-start.1 = (f32[1024,512]{1,0:T(8,128)S(1)}, f32[1024,512]{1,0:T(8,128)S(1)}, u32[]{:S(2)}, u32[]{:S(2)}) collective-permute-start(f32[1024,512]{1,0:T(8,128)S(1)} %fusion), channel_id=1, source_target_pairs={{0,1},{1,0},{2,3},{3,2},{4,5},{5,4},{6,7},{7,6},{8,9},{9,8},{10,11... | collective-permute-start | bytes 6291464 | tf_op jit(solution)/shard_map/ppermute | solution.py:83

commit v2 on v1

v2 whole, which is shorter than its diff:
```python
import jax
import jax.numpy as jnp
from jax import lax
from jax.experimental import pallas as pl
from jax.experimental.pallas import tpu as pltpu
from jax.sharding import Mesh, PartitionSpec as P

HIGH = lax.Precision.HIGH
hash_prime = 65521
N_Z_HI, N_Z_LO, N_X_HI, N_X_LO, N_Y, N_CORE = 4, 4, 2, 2, 4, 2
N_Z = N_Z_HI * N_Z_LO
N_XY = N_X_HI * N_X_LO * N_Y
N_REP = N_X_LO * N_Y * N_CORE
RPD = 64
F = 512
R = N_XY * RPD
COLS = N_CORE * N_Z * RPD
HALF = COLS // 2
BLOCK = N_Z_HI * RPD
DIGITS = 16
AXES = ("zh", "zl", "xh", "xl", "y", "c")
Z = ("zh", "zl")
XY = ("xh", "xl", "y")


def centred(value):
    return value - jnp.round(value * (1.0 / hash_prime)) * float(hash_prime)


def two_digits(value):
    high = jnp.floor((value + 128.0) * (1.0 / 256.0))
    return value - 256.0 * high, high


def stack_rows(rows, width):
    row_index = lax.broadcasted_iota(jnp.int32, (DIGITS, width), 0)
    stacked = jnp.zeros((DIGITS, width), jnp.float32)
    for k, row in enumerate(rows):
        stacked = jnp.where(row_index == k, row, stacked)
    return stacked.astype(jnp.bfloat16)


def row_digits(first_code, second_code):
    digits = []
    for code in (first_code, second_code):
        for value in (code, centred(code * 256.0)):
            low, high = two_digits(value)
            digits.extend((low, 256.0 * high))
    low, high = two_digits(centred(centred((first_code + second_code) * 128.0) * 128.0))
    return digits + [low, 256.0 * high]


def column_digits(first_code, second_code):
    digits = []
    for code in (first_code, second_code):
        low, high = two_digits(code - 16384.0)
        digits.extend((low, low, high, high))
    return digits + [jnp.ones_like(first_code)] * 2


def adjacency_kernel(threshold_ref, rows_ref, columns_ref, mask_ref, adjacency_ref, degree_ref, left_ref):
    rows = rows_ref[...].astype(jnp.float32)
    columns = columns_ref[...].astype(jnp.float32)
    left_ref[...] = stack_rows(row_digits(rows[:1], rows[1:]), R)
    right = stack_rows(column_digits(columns[:1], columns[1:]), HALF)
    groups = (N_Z, HALF)
    spread = lax.broadcasted_iota(jnp.int32, groups, 0) == lax.broadcasted_iota(jnp.int32, groups, 1) // RPD
    spread = jnp.where(spread, 1.0, 0.0).astype(jnp.bfloat16)
    mask = mask_ref[...].astype(jnp.float32).astype(jnp.bfloat16)
    limit = jnp.dot(mask, spread, preferred_element_type=jnp.float32) * threshold_ref[0].astype(jnp.float32)
    ones = jnp.ones((8, HALF), jnp.bfloat16)
    for pair in range(N_XY // 2):
        at = pl.ds(2 * RPD * pair, 2 * RPD)
        contract = (((0,), (0,)), ((), ()))
        value = lax.dot_general(left_ref[:, at], right, contract, preferred_element_type=jnp.float32)
        nearest = jnp.round(value * (1.0 / hash_prime))
        residue = value - nearest * float(hash_prime)
        kept = []
        for k in range(2):
            part = residue[k * RPD : (k + 1) * RPD]
            inside = jnp.logical_and(part >= 0.0, part < limit[2 * pair + k][None, :])
            kept.append(jnp.where(inside, 1.0, 0.0))
        low = jnp.concatenate(kept, axis=0).astype(jnp.bfloat16)
        adjacency_ref[at, :] = low
        contract = (((1,), (1,)), ((), ()))
        degree_ref[:, at] = lax.dot_general(ones, low, contract, preferred_element_type=jnp.float32)


def build_adjacency(threshold, rows, columns, mask):
    vmem = pl.BlockSpec(memory_space=pltpu.VMEM)
    return pl.pallas_call(
        adjacency_kernel,
        in_specs=[pl.BlockSpec(memory_space=pltpu.SMEM), vmem, vmem, vmem],
        out_specs=[vmem, vmem],
        out_shape=[
            jax.ShapeDtypeStruct((R, HALF), jnp.bfloat16),
            jax.ShapeDtypeStruct((8, R), jnp.float32),
        ],
        scratch_shapes=[pltpu.VMEM((DIGITS, R), jnp.bfloat16)],
        compiler_params=pltpu.CompilerParams(vmem_limit_bytes=32 * 1024 * 1024),
        cost_estimate=pl.CostEstimate(flops=2 * R * HALF * 16, bytes_accessed=2 * R * HALF, transcendentals=0),
    )(threshold, rows, columns, mask)


def to_other_core(values):
    return lax.ppermute(values, "c", [(0, 1), (1, 0)])


def along_z(values, step):
    return lax.ppermute(values, Z, [(z, (z + step) % N_Z) for z in range(N_Z)])


def exchange(values, axis):
    return lax.all_to_all(values, axis, 0, 0, tiled=True)


def to_all(values, axis, count):
    return exchange(jnp.broadcast_to(values[None], (count,) + values.shape).reshape(-1, values.shape[1]), axis)


def per_device(features, weight, cotangent, tile_mask, row_codes, col_codes):
    x_hi, z_lo, core = lax.axis_index("xh"), lax.axis_index("zl"), lax.axis_index("c")
    subset = (lax.axis_index("xl") * N_Y + lax.axis_index("y")) * N_CORE + core

    def by_class(values):
        twice = jnp.concatenate([values, values], axis=1)
        turned = lax.dynamic_slice_in_dim(twice, z_lo, N_Z_LO, 1)
        return jnp.concatenate([turned[:, :2], turned[:, 3:], turned[:, 2:3]], axis=1)

    own_rows = lax.dynamic_index_in_dim(row_codes.reshape(2, N_XY // 2, N_CORE, RPD), core, 2, False)
    own_columns = lax.dynamic_index_in_dim(col_codes.reshape(2, N_Z_HI, N_Z_LO, N_X_HI, RPD), x_hi, 3, False)
    own_columns = by_class(own_columns.transpose(0, 2, 1, 3))
    own_mask = by_class(tile_mask.reshape(N_XY // 2, N_Z_HI, N_Z_LO).transpose(0, 2, 1))
    sizes = (own_rows.size, own_columns.size, own_mask.size)
    small = jnp.concatenate([own_rows.reshape(-1), own_columns.reshape(-1), own_mask.reshape(-1)])
    small = lax.all_gather(small, ("xh", "c"), axis=0).reshape(N_X_HI, N_CORE, -1)
    small = jnp.where(core == 0, small, small[:, ::-1])
    rows, other_rows = (
        small[:, k, : sizes[0]].reshape(N_X_HI, 2, R // 2).transpose(1, 0, 2).reshape(2, R) for k in range(N_CORE)
    )
    columns = lax.dynamic_index_in_dim(small[:, :, sizes[0] : sizes[0] + sizes[1]], x_hi, 0, False)
    columns = columns.reshape(N_CORE, 2, HALF)
    mask = small[:, :, sizes[0] + sizes[1] :].reshape(N_X_HI, N_CORE, N_XY // 2, N_Z)
    mask = mask.transpose(1, 0, 2, 3).reshape(N_CORE, N_XY, N_Z)
    thresholds = [
        ((10 + 20 * p // (N_REP - 1)) * hash_prime // 1000).astype(jnp.int32).reshape(1) for p in (subset, subset ^ 1)
    ]

    block = to_all(features.astype(jnp.bfloat16), "zh", N_Z_HI)
    block, rows, other_rows, columns, mask = lax.optimization_barrier((block, rows, other_rows, columns, mask))
    up, down = along_z(block, -1), along_z(block, 1)
    far_low, far_high = along_z(block[: BLOCK // 2], -2), along_z(block[BLOCK // 2 :], 2)
    own, own_degree = build_adjacency(thresholds[0], rows, columns[0], mask[0])
    other, other_degree = build_adjacency(thresholds[1], rows, columns[1], mask[1])
    degree = (own_degree + other_degree)[0].reshape(N_XY, 1, RPD).astype(jnp.float16)
    degree = jnp.pad(degree, ((0, 0), (0, 7), (0, F - RPD)))
    gathered = jnp.concatenate([block, up, down, far_low, far_high], axis=0)
    gathered, own, other, degree = lax.optimization_barrier((gathered, own, other, degree))
    aggregate = jnp.dot(own, gathered, preferred_element_type=jnp.float32)
    aggregate, gathered = lax.optimization_barrier((aggregate, to_other_core(gathered)))
    aggregate += jnp.dot(other, gathered, preferred_element_type=jnp.float32)
    sent = jnp.concatenate([aggregate.astype(jnp.float16).reshape(N_XY, RPD, F), degree], axis=1)
    arrived = lax.all_to_all(sent, XY, 0, 0).astype(jnp.float32).sum(axis=0)
    degree = arrived[RPD, :RPD][:, None]
    aggregate = arrived[:RPD]

    row_scale = lax.rsqrt(1.0 + degree)
    hidden = (features + aggregate) * row_scale
    pre_act = jnp.dot(hidden, weight, precision=HIGH, preferred_element_type=jnp.float32)
    activated = jax.nn.softplus(pre_act)
    pulled = cotangent * jax.nn.sigmoid(pre_act) * row_scale

    pulled_block = to_all(pulled.astype(jnp.bfloat16), XY, N_XY)
    contract = (((0,), (0,)), ((), ()))
    cross, _ = build_adjacency(thresholds[0], other_rows, columns[0], mask[0])
    term = lax.dot_general(own, pulled_block, contract, preferred_element_type=jnp.float32)
    term, cross, pulled_block = lax.optimization_barrier((term, cross, to_other_core(pulled_block)))
    term += lax.dot_general(cross, pulled_block, contract, preferred_element_type=jnp.float32)
    low = term[BLOCK:].astype(jnp.bfloat16)
    up, down = along_z(low[:BLOCK], 1), along_z(low[BLOCK : 2 * BLOCK], -1)
    far_low = along_z(low[2 * BLOCK : 2 * BLOCK + BLOCK // 2], 2)
    far_high = along_z(low[2 * BLOCK + BLOCK // 2 :], -2)
    far = jnp.concatenate([far_low, far_high], axis=0)
    term = term[:BLOCK] + up.astype(jnp.float32) + down.astype(jnp.float32) + far.astype(jnp.float32)
    term = exchange(term.astype(jnp.bfloat16), "zh").reshape(N_Z_HI, RPD, F).astype(jnp.float32).sum(axis=0)
    grad_input = lax.dot_general(
        pulled + term, weight, (((1,), (1,)), ((), ())), precision=HIGH, preferred_element_type=jnp.float32
    )
    return (activated, grad_input)


def solution(mesh):
    inner = Mesh(mesh.devices.reshape(N_Z_HI, N_Z_LO, N_X_HI, N_X_LO, N_Y, N_CORE), AXES)
    row, rep = ("zh", "zl", "xh"), ("xl", "y", "c")
    in_specs = (
        P(row + rep, None),
        P(),
        P(row + rep, None),
        P(row, rep),
        P(None, row),
        P(None, rep),
    )
    out_specs = (P(row + rep, None), P(row + rep, None))
    return jax.shard_map(per_device, mesh=inner, in_specs=in_specs, out_specs=out_specs, check_vma=False)
```

time: 194 us -> 168 us (0.87)
  the two profiles are of different devices: /device:TPU:32 before, /device:TPU:64 now
where the time goes in v2:
time: 168 us
  blocking collectives  75.5 us (45%)
  starting transfers between devices  43 us (26%)
  waiting for transfers between devices  21 us (12%)
  local copies, waits for them, and re-layouts  10.7 us (6%)
  matrix products  7.52 us (4%)
  Pallas kernels  5.64 us (3%)
  other arithmetic  2.95 us (2%)
    all_to_all x2, blocking collectives, exchange(): return lax.all_to_all(values, axis, 0, 0, tiled=True)  43.2 us
    ppermute x8, starting transfers between devices, along_z(): return lax.ppermute(values, Z, [(z, (z + step) % N_Z) for z in range(N_Z)])  25.7 us
    all_to_all x1, blocking collectives, per_device(): arrived = lax.all_to_all(sent, XY, 0, 0).astype(jnp.float32).sum(axis=0)  25.6 us
    all_to_all x1, starting transfers between devices, exchange(): return lax.all_to_all(values, axis, 0, 0, tiled=True)  13.3 us
    all_to_all x1, waiting for transfers between devices, exchange(): return lax.all_to_all(values, axis, 0, 0, tiled=True)  9.97 us
    ppermute x8, waiting for transfers between devices, along_z(): return lax.ppermute(values, Z, [(z, (z + step) % N_Z) for z in range(N_Z)])  9.73 us
    all_gather x1, blocking collectives, per_device(): lax.all_gather(small, ('xh', 'c'), axis=0).reshape(N_X_HI, N_CORE, -1)  6.74 us
    pallas_call x3, Pallas kernels, build_adjacency(): pl.pallas_call(adjacency_kernel, in_specs=[pl.BlockSpec(memory_space=pltp...  5.64 us
  transfers between devices with their start and end apart: 11, of which 5 were waited for; matrix products, arithmetic and copies ran while one was open for 6% of the time, Pallas kernels for 3%

profile of v2, /device:TPU:64, one launch (start us, length us, event | category | flops | bytes accessed | tf_op | source)
XLA Modules:
  0.0 167.5 jit_solution(7713379084830115908)
XLA Ops:
  0.6 1.0 convert_element_type.42
  1.7 0.7 broadcast_in_dim.4
  2.4 13.3 %all-to-all-start = ((bf16[4,64,512]{2,1,0:T(8,128)(2,1)}), bf16[4,64,512]{2,1,0:T(8,128)(2,1)S(1)}, u32[]{:S(2)}, u32[]{:S(2)}) async-start(bf16[4,64,512]{2,1,0:T(8,128)(2,1)} %broadcast_in_dim.4), calls=%async_computation | async-start | bytes 524288 | tf_op jit(solution)/shard_map/all_to_all | solution.py:114
  15.7 0.8 copy.22
  16.5 0.8 reshape.92
  17.5 0.1 reshape.95
  17.6 0.8 reshape.90
  18.6 6.7 %all-gather.1 = s32[4,1,3200]{2,1,0:T(1,128)S(1)} all-gather(s32[1,1,3200]{2,1,0:T(1,128)S(1)} %reshape.107), channel_id=2, replica_groups=mesh['zh'=4,'zl'=4,'xh'=2,'xl'=2,'y'=4,'c'=2] {'xh','c'}, dimensions={0}, use_global_device_ids=true | all-gather | bytes 64000 | tf_op jit(solution)/shard_map/all_gather | solution.py:136
  25.4 0.1 reduce.1
  25.5 0.7 rev.3
  26.6 10.0 %all-to-all-done = bf16[4,64,512]{2,1,0:T(8,128)(2,1)S(1)} async-done(((bf16[4,64,512]{2,1,0:T(8,128)(2,1)}), bf16[4,64,512]{2,1,0:T(8,128)(2,1)S(1)}, u32[]{:S(2)}, u32[]{:S(2)}) %all-to-all-start) | async-done | bytes 262176 | tf_op jit(solution)/shard_map/all_to_all | solution.py:114
  36.6 0.7 fusion.19
  37.3 1.9 %collective-permute-start.1 = (bf16[256,512]{1,0:T(8,128)(2,1)S(1)}, bf16[256,512]{1,0:T(8,128)(2,1)}, u32[]{:S(2)}, u32[]{:S(2)}) collective-permute-start(bf16[256,512]{1,0:T(8,128)(2,1)S(1)} %bitcast.54), channel_id=1, source_target_pairs={{0,32},{32,64},{64,96},{96,128},{128,160},{160,192},{192,224},{224... | collective-permute-start | bytes 786440 | tf_op jit(solution)/shard_map/ppermute | solution.py:110
  39.2 3.9 %collective-permute-start = (bf16[256,512]{1,0:T(8,128)(2,1)S(1)}, bf16[256,512]{1,0:T(8,128)(2,1)}, u32[]{:S(2)}, u32[]{:S(2)}) collective-permute-start(bf16[256,512]{1,0:T(8,128)(2,1)S(1)} %bitcast.55), channel_id=1, source_target_pairs={{0,480},{32,0},{64,32},{96,64},{128,96},{160,128},{192,160},{224,1... | collective-permute-start | bytes 786440 | tf_op jit(solution)/shard_map/ppermute | solution.py:110
  43.2 4.1 %collective-permute-start.3 = (bf16[128,512]{1,0:T(8,128)(2,1)}, bf16[128,512]{1,0:T(8,128)(2,1)}, u32[]{:S(2)}, u32[]{:S(2)}) collective-permute-start(bf16[128,512]{1,0:T(8,128)(2,1)} %get-tuple-element.48), channel_id=1, source_target_pairs={{0,64},{32,96},{64,128},{96,160},{128,192},{160,224},{192,256},{22... | collective-permute-start | bytes 393224 | tf_op jit(solution)/shard_map/ppermute | solution.py:110
  47.3 2.6 %collective-permute-start.2 = (bf16[128,512]{1,0:T(8,128)(2,1)}, bf16[128,512]{1,0:T(8,128)(2,1)}, u32[]{:S(2)}, u32[]{:S(2)}) collective-permute-start(bf16[128,512]{1,0:T(8,128)(2,1)} %get-tuple-element.49), channel_id=1, source_target_pairs={{0,448},{32,480},{64,0},{96,32},{128,64},{160,96},{192,128},{224,1... | collective-permute-start | bytes 393224 | tf_op jit(solution)/shard_map/ppermute | solution.py:110
  50.0 1.7 shard_map.78
  51.6 1.3 copy-done.1
  53.0 1.7 shard_map.77
  54.8 1.0 constant_dynamic-update-slice_fusion.3
  55.8 1.0 constant_dynamic-update-slice_fusion.2
  56.8 1.1 collective-permute-done.2
  57.9 0.9 constant_dynamic-update-slice_fusion.1
  58.9 0.9 constant_dynamic-update-slice_fusion
  59.8 1.9 %collective-permute-start.4 = (bf16[1024,512]{1,0:T(8,128)(2,1)S(1)}, bf16[1024,512]{1,0:T(8,128)(2,1)S(1)}, u32[]{:S(2)}, u32[]{:S(2)}) collective-permute-start(bf16[1024,512]{1,0:T(8,128)(2,1)S(1)} %constant_dynamic-update-slice_fusion), channel_id=1, source_target_pairs={{0,1},{1,0},{2,3},{3,2},{4,5},{5,4},{6,7},{7,6},{8,9},{9,8},{10,11... | collective-permute-start | bytes 3145736 | tf_op jit(solution)/shard_map/ppermute | solution.py:106
  61.8 1.2 fusion.22
  63.0 1.3 collective-permute-done.4
  64.3 1.2 fusion.23
  65.6 0.6 add_convert_fusion
  66.1 0.3 pad_maximum_fusion
  66.5 25.6 %all_to_all.32 = f16[16,72,512]{2,1,0:T(8,128)(2,1)S(1)} all-to-all(f16[16,72,512]{2,1,0:T(8,128)(2,1)S(1)} %pad_maximum_fusion), channel_id=1, replica_groups=mesh['zh'=4,'zl'=4,'xh'=2,'xl'=2,'y'=4,'c'=2] {'xh','xl','y'}, dimensions={0} | all-to-all | bytes 2359296 | tf_op jit(solution)/shard_map/all_to_all | solution.py:163
  92.1 0.2 convert_reduce_fusion
  92.3 1.2 fusion.15
  93.6 19.7 %all_to_all.33 = bf16[16,64,512]{2,1,0:T(8,128)(2,1)S(1)} all-to-all(bf16[16,64,512]{2,1,0:T(8,128)(2,1)S(1)} %broadcast_in_dim.5), channel_id=1, replica_groups=mesh['zh'=4,'zl'=4,'xh'=2,'xl'=2,'y'=4,'c'=2] {'xh','xl','y'}, dimensions={0} | all-to-all | bytes 2097152 | tf_op jit(solution)/shard_map/all_to_all | solution.py:114
  113.2 2.1 %collective-permute-start.5 = (bf16[1024,512]{1,0:T(8,128)(2,1)S(1)}, bf16[1024,512]{1,0:T(8,128)(2,1)S(1)}, u32[]{:S(2)}, u32[]{:S(2)}) collective-permute-start(bf16[1024,512]{1,0:T(8,128)(2,1)S(1)} %bitcast.57), channel_id=1, source_target_pairs={{0,1},{1,0},{2,3},{3,2},{4,5},{5,4},{6,7},{7,6},{8,9},{9,8},{10,11... | collective-permute-start | bytes 3145736 | tf_op jit(solution)/shard_map/ppermute | solution.py:106
  115.3 2.3 %shard_map.79 = (bf16[1024,1024]{1,0:T(8,128)(2,1)S(1)}, f32[8,1024]{1,0:T(8,128)}) custom-call(s32[1]{0:T(128)} %bitcast.9.threshold_ref, s32[2,1024]{1,0:T(2,128)S(1)} %bitcast.49, s32[2,1024]{1,0:T(2,128)S(1)} %get-tuple-element.55.columns_ref, s32[16,16]{1,0:T(8,128)S(1)} %get-tuple-element.53.mask_ref), custom_call_target="tpu_custom_call" | custom-call | flops 33554432 | bytes 2097152 | tf_op jit(solution)/shard_map/pallas_call | solution.py:91
  117.6 1.3 fusion.24
  118.9 1.3 fusion.25
  120.2 0.5 fusion.16
  120.8 1.9 %collective-permute-start.6 = (bf16[256,512]{1,0:T(8,128)(2,1)S(1)}, bf16[256,512]{1,0:T(8,128)(2,1)S(1)}, u32[]{:S(2)}, u32[]{:S(2)}) collective-permute-start(bf16[256,512]{1,0:T(8,128)(2,1)S(1)} %get-tuple-element.46), channel_id=1, source_target_pairs={{0,32},{32,64},{64,96},{96,128},{128,160},{160,192},{192,224},{224... | collective-permute-start | bytes 786440 | tf_op jit(solution)/shard_map/ppermute | solution.py:110
  122.7 3.9 %collective-permute-start.7 = (bf16[256,512]{1,0:T(8,128)(2,1)S(1)}, bf16[256,512]{1,0:T(8,128)(2,1)S(1)}, u32[]{:S(2)}, u32[]{:S(2)}) collective-permute-start(bf16[256,512]{1,0:T(8,128)(2,1)S(1)} %get-tuple-element.47), channel_id=1, source_target_pairs={{0,480},{32,0},{64,32},{96,64},{128,96},{160,128},{192,160},{224,1... | collective-permute-start | bytes 786440 | tf_op jit(solution)/shard_map/ppermute | solution.py:110
  126.6 5.4 %collective-permute-start.8 = (bf16[128,512]{1,0:T(8,128)(2,1)S(1)}, bf16[128,512]{1,0:T(8,128)(2,1)S(1)}, u32[]{:S(2)}, u32[]{:S(2)}) collective-permute-start(bf16[128,512]{1,0:T(8,128)(2,1)S(1)} %get-tuple-element.44), channel_id=1, source_target_pairs={{0,64},{32,96},{64,128},{96,160},{128,192},{160,224},{192,256},{22... | collective-permute-start | bytes 393224 | tf_op jit(solution)/shard_map/ppermute | solution.py:110
  132.1 1.9 %collective-permute-start.9 = (bf16[128,512]{1,0:T(8,128)(2,1)S(1)}, bf16[128,512]{1,0:T(8,128)(2,1)S(1)}, u32[]{:S(2)}, u32[]{:S(2)}) collective-permute-start(bf16[128,512]{1,0:T(8,128)(2,1)S(1)} %get-tuple-element.45), channel_id=1, source_target_pairs={{0,448},{32,480},{64,0},{96,32},{128,64},{160,96},{192,128},{224,1... | collective-permute-start | bytes 393224 | tf_op jit(solution)/shard_map/ppermute | solution.py:110
  134.0 3.7 %collective-permute-done.8 = bf16[128,512]{1,0:T(8,128)(2,1)S(1)} collective-permute-done((bf16[128,512]{1,0:T(8,128)(2,1)S(1)}, bf16[128,512]{1,0:T(8,128)(2,1)S(1)}, u32[]{:S(2)}, u32[]{:S(2)}) %collective-permute-start.8) | collective-permute-done | bytes 131104 | tf_op jit(solution)/shard_map/ppermute | solution.py:110
  137.6 4.9 %collective-permute-done.9 = bf16[128,512]{1,0:T(8,128)(2,1)S(1)} collective-permute-done((bf16[128,512]{1,0:T(8,128)(2,1)S(1)}, bf16[128,512]{1,0:T(8,128)(2,1)S(1)}, u32[]{:S(2)}, u32[]{:S(2)}) %collective-permute-start.9) | collective-permute-done | bytes 131104 | tf_op jit(solution)/shard_map/ppermute | solution.py:110
  142.6 0.1 fusion.2
  142.7 23.5 %all_to_all.34 = bf16[4,64,512]{2,1,0:T(8,128)(2,1)S(1)} all-to-all(bf16[4,64,512]{2,1,0:T(8,128)(2,1)S(1)} %bitcast.59), channel_id=1, replica_groups=mesh['zh'=4,'zl'=4,'xh'=2,'xl'=2,'y'=4,'c'=2] {'zh'}, dimensions={0} | all-to-all | bytes 524288 | tf_op jit(solution)/shard_map/all_to_all | solution.py:114
  166.2 1.3 fusion.6
  (54 shorter events, 1.1 us)
Async XLA Ops:
  0.6 91.6 %copy-start = (f32[512,512]{1,0:T(8,128)S(1)}, f32[512,512]{1,0:T(8,128)}, u32[]{:S(2)}) copy-start(f32[512,512]{1,0:T(8,128)} %param.7) | copy-start | bytes 3145732
  2.4 34.2 %all-to-all-start = ((bf16[4,64,512]{2,1,0:T(8,128)(2,1)}), bf16[4,64,512]{2,1,0:T(8,128)(2,1)S(1)}, u32[]{:S(2)}, u32[]{:S(2)}) async-start(bf16[4,64,512]{2,1,0:T(8,128)(2,1)} %broadcast_in_dim.4), calls=%async_computation | async-start | bytes 524288 | tf_op jit(solution)/shard_map/all_to_all | solution.py:114
  37.3 18.5 %collective-permute-start.1 = (bf16[256,512]{1,0:T(8,128)(2,1)S(1)}, bf16[256,512]{1,0:T(8,128)(2,1)}, u32[]{:S(2)}, u32[]{:S(2)}) collective-permute-start(bf16[256,512]{1,0:T(8,128)(2,1)S(1)} %bitcast.54), channel_id=1, source_target_pairs={{0,32},{32,64},{64,96},{96,128},{128,160},{160,192},{192,224},{224... | collective-permute-start | bytes 786440 | tf_op jit(solution)/shard_map/ppermute | solution.py:110
  39.2 15.6 %collective-permute-start = (bf16[256,512]{1,0:T(8,128)(2,1)S(1)}, bf16[256,512]{1,0:T(8,128)(2,1)}, u32[]{:S(2)}, u32[]{:S(2)}) collective-permute-start(bf16[256,512]{1,0:T(8,128)(2,1)S(1)} %bitcast.55), channel_id=1, source_target_pairs={{0,480},{32,0},{64,32},{96,64},{128,96},{160,128},{192,160},{224,1... | collective-permute-start | bytes 786440 | tf_op jit(solution)/shard_map/ppermute | solution.py:110
  43.2 15.7 %collective-permute-start.3 = (bf16[128,512]{1,0:T(8,128)(2,1)}, bf16[128,512]{1,0:T(8,128)(2,1)}, u32[]{:S(2)}, u32[]{:S(2)}) collective-permute-start(bf16[128,512]{1,0:T(8,128)(2,1)} %get-tuple-element.48), channel_id=1, source_target_pairs={{0,64},{32,96},{64,128},{96,160},{128,192},{160,224},{192,256},{22... | collective-permute-start | bytes 393224 | tf_op jit(solution)/shard_map/ppermute | solution.py:110
  47.3 10.6 %collective-permute-start.2 = (bf16[128,512]{1,0:T(8,128)(2,1)}, bf16[128,512]{1,0:T(8,128)(2,1)}, u32[]{:S(2)}, u32[]{:S(2)}) collective-permute-start(bf16[128,512]{1,0:T(8,128)(2,1)} %get-tuple-element.49), channel_id=1, source_target_pairs={{0,448},{32,480},{64,0},{96,32},{128,64},{160,96},{192,128},{224,1... | collective-permute-start | bytes 393224 | tf_op jit(solution)/shard_map/ppermute | solution.py:110
  51.6 1.3 copy-start.1
  59.8 4.6 %collective-permute-start.4 = (bf16[1024,512]{1,0:T(8,128)(2,1)S(1)}, bf16[1024,512]{1,0:T(8,128)(2,1)S(1)}, u32[]{:S(2)}, u32[]{:S(2)}) collective-permute-start(bf16[1024,512]{1,0:T(8,128)(2,1)S(1)} %constant_dynamic-update-slice_fusion), channel_id=1, source_target_pairs={{0,1},{1,0},{2,3},{3,2},{4,5},{5,4},{6,7},{7,6},{8,9},{9,8},{10,11... | collective-permute-start | bytes 3145736 | tf_op jit(solution)/shard_map/ppermute | solution.py:106
  61.8 2.5 %copy-start.2 = (bf16[1024,1024]{1,0:T(8,128)(2,1)S(1)}, bf16[1024,1024]{1,0:T(8,128)(2,1)}, u32[]{:S(2)}) copy-start(bf16[1024,1024]{1,0:T(8,128)(2,1)} %copy-done.1) | copy-start | bytes 6291460
  66.4 25.8 %copy-start.3 = (f32[64,512]{1,0:T(8,128)S(1)}, f32[64,512]{1,0:T(8,128)}, u32[]{:S(2)}) copy-start(f32[64,512]{1,0:T(8,128)} %param.8) | copy-start | bytes 393220
  66.4 25.8 %copy-start.4 = (f32[64,512]{1,0:T(8,128)S(1)}, f32[64,512]{1,0:T(8,128)}, u32[]{:S(2)}) copy-start(f32[64,512]{1,0:T(8,128)} %param.6) | copy-start | bytes 393220
  113.2 5.7 %collective-permute-start.5 = (bf16[1024,512]{1,0:T(8,128)(2,1)S(1)}, bf16[1024,512]{1,0:T(8,128)(2,1)S(1)}, u32[]{:S(2)}, u32[]{:S(2)}) collective-permute-start(bf16[1024,512]{1,0:T(8,128)(2,1)S(1)} %bitcast.57), channel_id=1, source_target_pairs={{0,1},{1,0},{2,3},{3,2},{4,5},{5,4},{6,7},{7,6},{8,9},{9,8},{10,11... | collective-permute-start | bytes 3145736 | tf_op jit(solution)/shard_map/ppermute | solution.py:106
  120.8 21.8 %collective-permute-start.6 = (bf16[256,512]{1,0:T(8,128)(2,1)S(1)}, bf16[256,512]{1,0:T(8,128)(2,1)S(1)}, u32[]{:S(2)}, u32[]{:S(2)}) collective-permute-start(bf16[256,512]{1,0:T(8,128)(2,1)S(1)} %get-tuple-element.46), channel_id=1, source_target_pairs={{0,32},{32,64},{64,96},{96,128},{128,160},{160,192},{192,224},{224... | collective-permute-start | bytes 786440 | tf_op jit(solution)/shard_map/ppermute | solution.py:110
  122.7 19.9 %collective-permute-start.7 = (bf16[256,512]{1,0:T(8,128)(2,1)S(1)}, bf16[256,512]{1,0:T(8,128)(2,1)S(1)}, u32[]{:S(2)}, u32[]{:S(2)}) collective-permute-start(bf16[256,512]{1,0:T(8,128)(2,1)S(1)} %get-tuple-element.47), channel_id=1, source_target_pairs={{0,480},{32,0},{64,32},{96,64},{128,96},{160,128},{192,160},{224,1... | collective-permute-start | bytes 786440 | tf_op jit(solution)/shard_map/ppermute | solution.py:110
  126.6 11.0 %collective-permute-start.8 = (bf16[128,512]{1,0:T(8,128)(2,1)S(1)}, bf16[128,512]{1,0:T(8,128)(2,1)S(1)}, u32[]{:S(2)}, u32[]{:S(2)}) collective-permute-start(bf16[128,512]{1,0:T(8,128)(2,1)S(1)} %get-tuple-element.44), channel_id=1, source_target_pairs={{0,64},{32,96},{64,128},{96,160},{128,192},{160,224},{192,256},{22... | collective-permute-start | bytes 393224 | tf_op jit(solution)/shard_map/ppermute | solution.py:110
  132.1 10.5 %collective-permute-start.9 = (bf16[128,512]{1,0:T(8,128)(2,1)S(1)}, bf16[128,512]{1,0:T(8,128)(2,1)S(1)}, u32[]{:S(2)}, u32[]{:S(2)}) collective-permute-start(bf16[128,512]{1,0:T(8,128)(2,1)S(1)} %get-tuple-element.45), channel_id=1, source_target_pairs={{0,448},{32,480},{64,0},{96,32},{128,64},{160,96},{192,128},{224,1... | collective-permute-start | bytes 393224 | tf_op jit(solution)/shard_map/ppermute | solution.py:110

commit v3 on v2

v3 whole, which is shorter than its diff:
```python
import functools

import jax
import jax.numpy as jnp
from jax import lax
from jax.experimental import pallas as pl
from jax.experimental.pallas import tpu as pltpu
from jax.sharding import Mesh, PartitionSpec as P

HIGH = lax.Precision.HIGH
hash_prime = 65521
N_Z_HI, N_Z_LO, N_X_HI, N_X_LO, N_Y, N_CORE = 4, 4, 2, 2, 4, 2
N_Z = N_Z_HI * N_Z_LO
N_XY = N_X_HI * N_X_LO * N_Y
N_REP = N_X_LO * N_Y * N_CORE
RPD = 64
F = 512
R = N_XY * RPD
COLS = N_CORE * N_Z * RPD
HALF = COLS // 2
BLOCK = N_Z_HI * RPD
DIGITS = 16
AXES = ("zh", "zl", "xh", "xl", "y", "c")
Z = ("zh", "zl")
XY = ("xh", "xl", "y")


def centred(value):
    return value - jnp.round(value * (1.0 / hash_prime)) * float(hash_prime)


def two_digits(value):
    high = jnp.floor((value + 128.0) * (1.0 / 256.0))
    return value - 256.0 * high, high


def stack_rows(rows, width):
    row_index = lax.broadcasted_iota(jnp.int32, (DIGITS, width), 0)
    stacked = jnp.zeros((DIGITS, width), jnp.float32)
    for k, row in enumerate(rows):
        stacked = jnp.where(row_index == k, row, stacked)
    return stacked.astype(jnp.bfloat16)


def row_digits(first_code, second_code):
    digits = []
    for code in (first_code, second_code):
        for value in (code, centred(code * 256.0)):
            low, high = two_digits(value)
            digits.extend((low, 256.0 * high))
    low, high = two_digits(centred(centred((first_code + second_code) * 128.0) * 128.0))
    return digits + [low, 256.0 * high]


def column_digits(first_code, second_code):
    digits = []
    for code in (first_code, second_code):
        low, high = two_digits(code - 16384.0)
        digits.extend((low, low, high, high))
    return digits + [jnp.ones_like(first_code)] * 2


def halves(first, second, upper):
    lane = lax.broadcasted_iota(jnp.int32, first.shape, 1)
    lower_halves = jnp.where(lane < RPD, first, pltpu.roll(second, RPD, 1))
    upper_halves = jnp.where(lane < RPD, pltpu.roll(first, RPD, 1), second)
    return jnp.where(upper == 1, upper_halves, lower_halves)


def class_of(place, z_lo):
    return (z_lo + place + jnp.where(place == 2, 1, 0) - jnp.where(place == 3, 1, 0)) & (N_Z_LO - 1)


def adjacency_kernel(crossed, place_ref, codes_ref, *outs):
    own_ref, *others, picked_ref, left_ref = outs
    core, x_hi, z_lo = place_ref[0], place_ref[1], place_ref[2]

    for x in range(N_X_HI):
        for t in range(R // N_X_HI // 128):
            pieces = [codes_ref[N_CORE * x, :2, pl.ds(256 * t + 128 * k, 128)] for k in range(2)]
            picked_ref[:, pl.ds(R // N_X_HI * x + 128 * t, 128)] = halves(*pieces, core ^ 1 if crossed else core)
    rows = picked_ref[...].astype(jnp.float32)
    left_ref[...] = stack_rows(row_digits(rows[:1], rows[1:]), R)

    groups = (N_Z, HALF)
    column = lax.broadcasted_iota(jnp.int32, groups, 1)
    tile = ((column // RPD) & (N_Z_HI - 1)) * N_Z_LO + class_of(column // BLOCK, z_lo)
    spread = jnp.where(lax.broadcasted_iota(jnp.int32, groups, 0) == tile, 1.0, 0.0).astype(jnp.bfloat16)
    ones = jnp.ones((8, HALF), jnp.bfloat16)
    lane = lax.broadcasted_iota(jnp.int32, (8, 128), 1)
    for side in range(1 if crossed else 2):
        for place in range(N_Z_LO):
            for h in range(N_Z_HI // 2):
                pieces = []
                for k in range(2):
                    at = R + ((2 * h + k) * N_Z_LO + class_of(jnp.int32(place), z_lo)) * 128
                    pieces.append(codes_ref[core ^ side, :2, pl.ds(pl.multiple_of(at, 128), 128)])
                picked_ref[:, pl.ds(BLOCK * place + 128 * h, 128)] = halves(*pieces, x_hi)
        columns = picked_ref[...].astype(jnp.float32)
        right = stack_rows(column_digits(columns[:1], columns[1:]), HALF)
        masks = [codes_ref[N_CORE * x + (core ^ side), :, R + COLS : R + COLS + N_Z] for x in range(N_X_HI)]
        mask = jnp.concatenate(masks, axis=0).astype(jnp.float32).astype(jnp.bfloat16)
        limit = jnp.dot(mask, spread, preferred_element_type=jnp.float32) * place_ref[3 + side].astype(jnp.float32)
        for pair in range(N_XY // 2):
            at = pl.ds(2 * RPD * pair, 2 * RPD)
            contract = (((0,), (0,)), ((), ()))
            value = lax.dot_general(left_ref[:, at], right, contract, preferred_element_type=jnp.float32)
            nearest = jnp.round(value * (1.0 / hash_prime))
            residue = value - nearest * float(hash_prime)
            kept = []
            for k in range(2):
                part = residue[k * RPD : (k + 1) * RPD]
                inside = jnp.logical_and(part >= 0.0, part < limit[2 * pair + k][None, :])
                kept.append(jnp.where(inside, 1.0, 0.0))
            low = jnp.concatenate(kept, axis=0).astype(jnp.bfloat16)
            if crossed:
                own_ref[at, :] = low
                continue
            other_ref, degree_ref = others
            contract = (((1,), (1,)), ((), ()))
            count = lax.dot_general(ones, low, contract, preferred_element_type=jnp.float32)
            if side == 0:
                own_ref[at, :] = low
                degree_ref[2 * pair : 2 * pair + 2] = jnp.zeros((2, 8, 128), jnp.float32)
            else:
                other_ref[at, :] = low
            for k in range(2):
                part = pltpu.roll(count, RPD, 1) if k else count
                degree_ref[2 * pair + k] += jnp.where(lane < RPD, part, 0.0)


def build_adjacency(crossed, place, codes):
    vmem = pl.BlockSpec(memory_space=pltpu.VMEM)
    block = jax.ShapeDtypeStruct((R, HALF), jnp.bfloat16)
    outs = [block] if crossed else [block, block, jax.ShapeDtypeStruct((N_XY, 8, 128), jnp.float32)]
    return pl.pallas_call(
        functools.partial(adjacency_kernel, crossed),
        in_specs=[pl.BlockSpec(memory_space=pltpu.SMEM), vmem],
        out_specs=[vmem] * len(outs),
        out_shape=outs,
        scratch_shapes=[pltpu.VMEM((2, R), jnp.int32), pltpu.VMEM((DIGITS, R), jnp.bfloat16)],
        compiler_params=pltpu.CompilerParams(vmem_limit_bytes=6 * 1024 * 1024),
        cost_estimate=pl.CostEstimate(
            flops=2 * R * HALF * 16 * len(outs), bytes_accessed=2 * R * HALF * len(outs), transcendentals=0
        ),
    )(place, codes)


def prepare_kernel(features_ref, rows_ref, columns_ref, mask_ref, low_ref, codes_ref, values_ref, *scratch):
    *held, sems = scratch
    copies = [
        pltpu.make_async_copy(source, target, sems.at[k])
        for k, (source, target) in enumerate(zip((features_ref, rows_ref, columns_ref, mask_ref), (values_ref, *held)))
    ]
    for copy in copies:
        copy.start()
    codes_ref[...] = jnp.zeros_like(codes_ref)
    for copy in copies:
        copy.wait()
    rows, columns, mask = held
    for k in range(N_X_HI * N_CORE):
        codes_ref[k, :2, :R] = rows[...]
        codes_ref[k, :2, R : R + COLS] = columns[...]
        codes_ref[k, :, R + COLS : R + COLS + N_Z] = mask[...]
    low_ref[...] = values_ref[...].astype(jnp.bfloat16)


def prepare(features, row_codes, col_codes, tile_mask):
    vmem = pl.BlockSpec(memory_space=pltpu.VMEM)
    arrays = (features, row_codes, col_codes, tile_mask)
    return pl.pallas_call(
        prepare_kernel,
        in_specs=[pl.BlockSpec(memory_space=pl.ANY)] * 4,
        out_specs=[vmem, vmem],
        out_shape=[
            jax.ShapeDtypeStruct(features.shape, jnp.bfloat16),
            jax.ShapeDtypeStruct((N_X_HI * N_CORE, 8, R + COLS + 128), jnp.int32),
        ],
        scratch_shapes=[pltpu.VMEM(array.shape, array.dtype) for array in arrays] + [pltpu.SemaphoreType.DMA((4,))],
        compiler_params=pltpu.CompilerParams(vmem_limit_bytes=56 * 1024 * 1024),
    )(*arrays)


def multiply(left, right):
    return jnp.dot(left, right, preferred_element_type=jnp.float32)


def multiply_transposed(left, right):
    return lax.dot_general(left, right, (((0,), (0,)), ((), ())), preferred_element_type=jnp.float32)


def to_other_core(values):
    return lax.ppermute(values, "c", [(0, 1), (1, 0)])


def along_z(values, step):
    return lax.ppermute(values, Z, [(z, (z + step) % N_Z) for z in range(N_Z)])


def exchange(values, axis):
    return lax.all_to_all(values, axis, 0, 0, tiled=True)


def to_all(values, axis, count):
    return exchange(jnp.broadcast_to(values[None], (count,) + values.shape).reshape(-1, values.shape[1]), axis)


def per_device(features, weight, cotangent, tile_mask, row_codes, col_codes):
    x_hi, z_lo, core = lax.axis_index("xh"), lax.axis_index("zl"), lax.axis_index("c")
    subset = (lax.axis_index("xl") * N_Y + lax.axis_index("y")) * N_CORE + core

    thresholds = [(10 + 20 * p // (N_REP - 1)) * hash_prime // 1000 for p in (subset, subset ^ 1)]
    place = jnp.stack([core, x_hi, z_lo, *thresholds]).astype(jnp.int32)

    low, codes = prepare(features, row_codes, col_codes, tile_mask)
    codes = lax.all_to_all(codes, ("xh", "c"), 0, 0, tiled=True)
    block = lax.all_gather(low, "zh", axis=0, tiled=True)
    up, down = along_z(block, -1), along_z(block, 1)
    far = along_z(up, -1)
    own, other, degree = build_adjacency(False, place, codes)
    degree = jnp.pad(degree, ((0, 0), (0, 0), (0, F - 128))).astype(jnp.float16)
    gathered = jnp.concatenate([block, up, down, far], axis=0)
    gathered, own, other, degree = lax.optimization_barrier((gathered, own, other, degree))
    aggregate = multiply(own, gathered)
    aggregate, gathered = lax.optimization_barrier((aggregate, to_other_core(gathered)))
    aggregate += multiply(other, gathered)
    sent = jnp.concatenate([aggregate.astype(jnp.float16).reshape(N_XY, RPD, F), degree], axis=1)
    arrived = lax.all_to_all(sent, XY, 0, 0).astype(jnp.float32).sum(axis=0)
    degree = arrived[RPD, :RPD][:, None]
    aggregate = arrived[:RPD]

    row_scale = lax.rsqrt(1.0 + degree)
    hidden = (features + aggregate) * row_scale
    pre_act = jnp.dot(hidden, weight, precision=HIGH, preferred_element_type=jnp.float32)
    activated = jax.nn.softplus(pre_act)
    pulled = cotangent * jax.nn.sigmoid(pre_act) * row_scale

    pulled_block = to_all(pulled.astype(jnp.bfloat16), XY, N_XY)
    pulled_block, codes = lax.optimization_barrier((pulled_block, codes))
    (cross,) = build_adjacency(True, place, codes)
    far_term = multiply_transposed(own[:, 3 * BLOCK :], pulled_block)
    term = multiply_transposed(own[:, : 3 * BLOCK], pulled_block)
    far_term, term, pulled_other = lax.optimization_barrier((far_term, term, to_other_core(pulled_block)))
    far_term += multiply_transposed(cross[:, 3 * BLOCK :], pulled_other)
    passed = along_z(far_term.astype(jnp.bfloat16), 1)
    term += multiply_transposed(cross[:, : 3 * BLOCK], pulled_other)
    down = along_z(term[2 * BLOCK :].astype(jnp.bfloat16), -1)
    up = along_z((term[BLOCK : 2 * BLOCK] + passed.astype(jnp.float32)).astype(jnp.bfloat16), 1)
    term = term[:BLOCK] + up.astype(jnp.float32) + down.astype(jnp.float32)
    term = exchange(term.astype(jnp.bfloat16), "zh").reshape(N_Z_HI, RPD, F).astype(jnp.float32).sum(axis=0)
    grad_input = lax.dot_general(
        pulled + term, weight, (((1,), (1,)), ((), ())), precision=HIGH, preferred_element_type=jnp.float32
    )
    return (activated, grad_input)


def solution(mesh):
    inner = Mesh(mesh.devices.reshape(N_Z_HI, N_Z_LO, N_X_HI, N_X_LO, N_Y, N_CORE), AXES)
    row, rep = ("zh", "zl", "xh"), ("xl", "y", "c")
    in_specs = (
        P(row + rep, None),
        P(),
        P(row + rep, None),
        P(row, rep),
        P(None, row),
        P(None, rep),
    )
    out_specs = (P(row + rep, None), P(row + rep, None))
    return jax.shard_map(per_device, mesh=inner, in_specs=in_specs, out_specs=out_specs, check_vma=False)
```

time: 168 us -> 161 us (0.958)
  the two profiles are of different devices: /device:TPU:64 before, /device:TPU:32 now
where the time goes in v3:
time: 161 us; the launch traced here: 160 us
  blocking collectives  98.7 us (61%)
  starting transfers between devices  27 us (17%)
  waiting for transfers between devices  15.6 us (10%)
  Pallas kernels  8.04 us (5%)
  matrix products  7.9 us (5%)
  other arithmetic  1.76 us (1%)
    all_to_all x2, blocking collectives, exchange(): return lax.all_to_all(values, axis, 0, 0, tiled=True)  46.7 us
    all_gather x1, blocking collectives, per_device(): block = lax.all_gather(low, 'zh', axis=0, tiled=True)  26.2 us
    all_to_all x1, blocking collectives, per_device(): arrived = lax.all_to_all(sent, XY, 0, 0).astype(jnp.float32).sum(axis=0)  25.7 us
    ppermute x6, starting transfers between devices, along_z(): return lax.ppermute(values, Z, [(z, (z + step) % N_Z) for z in range(N_Z)])  18.8 us
    ppermute x6, waiting for transfers between devices, along_z(): return lax.ppermute(values, Z, [(z, (z + step) % N_Z) for z in range(N_Z)])  11.2 us
    pallas_call x2, Pallas kernels, build_adjacency(): pl.pallas_call(functools.partial(adjacency_kernel, crossed), in_specs=[pl...  6.21 us
    all_to_all x1, starting transfers between devices, per_device(): codes = lax.all_to_all(codes, ('xh', 'c'), 0, 0, tiled=True)  4.3 us
    ppermute x2, starting transfers between devices, to_other_core(): return lax.ppermute(values, 'c', [(0, 1), (1, 0)])  3.83 us
  transfers between devices with their start and end apart: 9, of which 5 were waited for; matrix products, arithmetic and copies ran while one was open for 3% of the time, Pallas kernels for 4%

profile of v3, /device:TPU:32, one launch (start us, length us, event | category | flops | bytes accessed | tf_op | source)
XLA Modules:
  0.0 160.2 jit_solution(17285780880004744550)
XLA Ops:
  0.6 0.0 copy-start
  0.6 1.8 %shard_map.77 = (bf16[64,512]{1,0:T(8,128)(2,1)}, s32[4,8,3200]{2,1,0:T(8,128)}) custom-call(f32[64,512]{1,0:T(8,128)} %features_ref.1, s32[2,1024]{1,0:T(2,128)} %rows_ref.1, s32[2,2048]{1,0:T(2,128)} %columns_ref.1, s32[8,16]{1,0:T(8,128)} %mask_ref.1), custom_call_target="tpu_custom_call" | custom-call | tf_op jit(solution)/shard_map/pallas_call | solution.py:171
  2.5 26.2 %all_gather.3 = bf16[256,512]{1,0:T(8,128)(2,1)S(1)} all-gather(bf16[64,512]{1,0:T(8,128)(2,1)} %get-tuple-element.18), channel_id=1, replica_groups=mesh['zh'=4,'zl'=4,'xh'=2,'xl'=2,'y'=4,'c'=2] {'zh'}, dimensions={0}, use_global_device_ids=true | all-gather | bytes 327680 | tf_op jit(solution)/shard_map/all_gather | solution.py:217
  28.7 2.9 %collective-permute-start = (bf16[256,512]{1,0:T(8,128)(2,1)S(1)}, bf16[256,512]{1,0:T(8,128)(2,1)S(1)}, u32[]{:S(2)}, u32[]{:S(2)}) collective-permute-start(bf16[256,512]{1,0:T(8,128)(2,1)S(1)} %all_gather.3), channel_id=1, source_target_pairs={{0,480},{32,0},{64,32},{96,64},{128,96},{160,128},{192,160},{224,1... | collective-permute-start | bytes 786440 | tf_op jit(solution)/shard_map/ppermute | solution.py:197
  31.6 4.3 %all-to-all-start = ((s32[4,8,3200]{2,1,0:T(8,128)}), s32[4,8,3200]{2,1,0:T(8,128)S(1)}, u32[]{:S(2)}, u32[]{:S(2)}) async-start(s32[4,8,3200]{2,1,0:T(8,128)} %get-tuple-element.19), calls=%async_computation | async-start | bytes 819200 | tf_op jit(solution)/shard_map/all_to_all | solution.py:216
  35.9 2.9 %collective-permute-start.1 = (bf16[256,512]{1,0:T(8,128)(2,1)S(1)}, bf16[256,512]{1,0:T(8,128)(2,1)S(1)}, u32[]{:S(2)}, u32[]{:S(2)}) collective-permute-start(bf16[256,512]{1,0:T(8,128)(2,1)S(1)} %all_gather.3), channel_id=1, source_target_pairs={{0,32},{32,64},{64,96},{96,128},{128,160},{160,192},{192,224},{224... | collective-permute-start | bytes 786440 | tf_op jit(solution)/shard_map/ppermute | solution.py:197
  38.8 0.0 collective-permute-done
  38.8 3.0 %collective-permute-start.2 = (bf16[256,512]{1,0:T(8,128)(2,1)S(1)}, bf16[256,512]{1,0:T(8,128)(2,1)S(1)}, u32[]{:S(2)}, u32[]{:S(2)}) collective-permute-start(bf16[256,512]{1,0:T(8,128)(2,1)S(1)} %collective-permute-done), channel_id=1, source_target_pairs={{0,480},{32,0},{64,32},{96,64},{128,96},{160,128},{192,160},{224,1... | collective-permute-start | bytes 786440 | tf_op jit(solution)/shard_map/ppermute | solution.py:197
  41.9 0.1 stack.23.place_ref
  42.0 3.0 %all-to-all-done.codes_ref = s32[4,8,3200]{2,1,0:T(8,128)S(1)} async-done(((s32[4,8,3200]{2,1,0:T(8,128)}), s32[4,8,3200]{2,1,0:T(8,128)S(1)}, u32[]{:S(2)}, u32[]{:S(2)}) %all-to-all-start) | async-done | bytes 409632 | tf_op jit(solution)/shard_map/all_to_all | solution.py:216
  45.0 4.1 %shard_map.78 = (bf16[1024,1024]{1,0:T(8,128)(2,1)S(1)}, bf16[1024,1024]{1,0:T(8,128)(2,1)S(1)}, f32[16,8,128]{2,1,0:T(8,128)S(1)}) custom-call(s32[5]{0:T(128)S(1)} %stack.23.place_ref, s32[4,8,3200]{2,1,0:T(8,128)S(1)} %all-to-all-done.codes_ref), custom_call_target="tpu_custom_call" | custom-call | flops 100663296 | bytes 6291456 | tf_op jit(solution)/shard_map/pallas_call | solution.py:136
  49.2 0.0 collective-permute-done.1
  49.2 0.0 collective-permute-done.2
  49.2 0.1 pad_maximum_fusion.1
  49.3 1.9 %collective-permute-start.3 = (bf16[1024,512]{1,0:T(8,128)(2,1)S(1)}, bf16[1024,512]{1,0:T(8,128)(2,1)S(1)}, u32[]{:S(2)}, u32[]{:S(2)}) collective-permute-start(bf16[1024,512]{1,0:T(8,128)(2,1)S(1)} %pad_maximum_fusion.1), channel_id=1, source_target_pairs={{0,1},{1,0},{2,3},{3,2},{4,5},{5,4},{6,7},{7,6},{8,9},{9,8},{10,11... | collective-permute-start | bytes 3145736 | tf_op jit(solution)/shard_map/ppermute | solution.py:193
  51.2 1.2 fusion.20
  52.5 1.4 collective-permute-done.3
  53.8 1.2 fusion.21
  55.1 0.6 add_convert_fusion
  55.7 0.3 pad_maximum_fusion
  56.0 0.0 copy-start.1
  56.0 0.0 copy-start.2
  56.0 25.7 %all_to_all.28 = f16[16,72,512]{2,1,0:T(8,128)(2,1)S(1)} all-to-all(f16[16,72,512]{2,1,0:T(8,128)(2,1)S(1)} %pad_maximum_fusion), channel_id=1, replica_groups=mesh['zh'=4,'zl'=4,'xh'=2,'xl'=2,'y'=4,'c'=2] {'xh','xl','y'}, dimensions={0} | all-to-all | bytes 2359296 | tf_op jit(solution)/shard_map/all_to_all | solution.py:228
  81.7 0.2 convert_reduce_fusion
  81.9 0.0 copy-done
  81.9 0.0 copy-done.1
  81.9 1.2 fusion.19
  83.1 0.1 broadcast_in_dim.2
  83.2 19.6 %all_to_all.29 = bf16[16,64,512]{2,1,0:T(8,128)(2,1)S(1)} all-to-all(bf16[16,64,512]{2,1,0:T(8,128)(2,1)S(1)} %broadcast_in_dim.2), channel_id=1, replica_groups=mesh['zh'=4,'zl'=4,'xh'=2,'xl'=2,'y'=4,'c'=2] {'xh','xl','y'}, dimensions={0} | all-to-all | bytes 2097152 | tf_op jit(solution)/shard_map/all_to_all | solution.py:201
  102.8 1.9 %collective-permute-start.4 = (bf16[1024,512]{1,0:T(8,128)(2,1)S(1)}, bf16[1024,512]{1,0:T(8,128)(2,1)S(1)}, u32[]{:S(2)}, u32[]{:S(2)}) collective-permute-start(bf16[1024,512]{1,0:T(8,128)(2,1)S(1)} %bitcast.22), channel_id=1, source_target_pairs={{0,1},{1,0},{2,3},{3,2},{4,5},{5,4},{6,7},{7,6},{8,9},{9,8},{10,11... | collective-permute-start | bytes 3145736 | tf_op jit(solution)/shard_map/ppermute | solution.py:193
  104.7 2.1 %shard_map.79 = bf16[1024,1024]{1,0:T(8,128)(2,1)S(1)} custom-call(s32[5]{0:T(128)S(1)} %stack.23.place_ref, s32[4,8,3200]{2,1,0:T(8,128)S(1)} %all-to-all-done.codes_ref), custom_call_target="tpu_custom_call" | custom-call | flops 33554432 | bytes 2097152 | tf_op jit(solution)/shard_map/pallas_call | solution.py:136
  106.8 0.5 fusion.9
  107.3 1.0 fusion.2
  108.3 0.0 collective-permute-done.4
  108.3 0.5 fusion.4
  108.8 0.1 add_convert_fusion.1
  108.9 3.8 %collective-permute-start.5 = (bf16[256,512]{1,0:T(8,128)(2,1)S(1)}, bf16[256,512]{1,0:T(8,128)(2,1)S(1)}, u32[]{:S(2)}, u32[]{:S(2)}) collective-permute-start(bf16[256,512]{1,0:T(8,128)(2,1)S(1)} %add_convert_fusion.1), channel_id=1, source_target_pairs={{0,32},{32,64},{64,96},{96,128},{128,160},{160,192},{192,224},{224... | collective-permute-start | bytes 786440 | tf_op jit(solution)/shard_map/ppermute | solution.py:197
  112.7 1.0 fusion
  113.7 0.3 add.71
  114.1 2.0 %collective-permute-start.7 = (bf16[256,512]{1,0:T(8,128)(2,1)S(1)}, bf16[256,512]{1,0:T(8,128)(2,1)S(1)}, u32[]{:S(2)}, u32[]{:S(2)}) collective-permute-start(bf16[256,512]{1,0:T(8,128)(2,1)S(1)} %slice.70), channel_id=1, source_target_pairs={{0,480},{32,0},{64,32},{96,64},{128,96},{160,128},{192,160},{224,1... | collective-permute-start | bytes 786440 | tf_op jit(solution)/shard_map/ppermute | solution.py:197
  116.2 3.4 %collective-permute-done.5 = bf16[256,512]{1,0:T(8,128)(2,1)S(1)} collective-permute-done((bf16[256,512]{1,0:T(8,128)(2,1)S(1)}, bf16[256,512]{1,0:T(8,128)(2,1)S(1)}, u32[]{:S(2)}, u32[]{:S(2)}) %collective-permute-start.5) | collective-permute-done | bytes 262176 | tf_op jit(solution)/shard_map/ppermute | solution.py:197
  119.6 0.1 fusion.6
  119.7 4.2 %collective-permute-start.6 = (bf16[256,512]{1,0:T(8,128)(2,1)S(1)}, bf16[256,512]{1,0:T(8,128)(2,1)S(1)}, u32[]{:S(2)}, u32[]{:S(2)}) collective-permute-start(bf16[256,512]{1,0:T(8,128)(2,1)S(1)} %fusion.6), channel_id=1, source_target_pairs={{0,32},{32,64},{64,96},{96,128},{128,160},{160,192},{192,224},{224... | collective-permute-start | bytes 786440 | tf_op jit(solution)/shard_map/ppermute | solution.py:197
  123.9 1.8 %collective-permute-done.7 = bf16[256,512]{1,0:T(8,128)(2,1)S(1)} collective-permute-done((bf16[256,512]{1,0:T(8,128)(2,1)S(1)}, bf16[256,512]{1,0:T(8,128)(2,1)S(1)}, u32[]{:S(2)}, u32[]{:S(2)}) %collective-permute-start.7) | collective-permute-done | bytes 262176 | tf_op jit(solution)/shard_map/ppermute | solution.py:197
  125.7 6.0 %collective-permute-done.6 = bf16[256,512]{1,0:T(8,128)(2,1)S(1)} collective-permute-done((bf16[256,512]{1,0:T(8,128)(2,1)S(1)}, bf16[256,512]{1,0:T(8,128)(2,1)S(1)}, u32[]{:S(2)}, u32[]{:S(2)}) %collective-permute-start.6) | collective-permute-done | bytes 262176 | tf_op jit(solution)/shard_map/ppermute | solution.py:197
  131.7 0.1 fusion.8
  131.8 27.1 %all_to_all.30 = bf16[4,64,512]{2,1,0:T(8,128)(2,1)S(1)} all-to-all(bf16[4,64,512]{2,1,0:T(8,128)(2,1)S(1)} %bitcast.21), channel_id=1, replica_groups=mesh['zh'=4,'zl'=4,'xh'=2,'xl'=2,'y'=4,'c'=2] {'zh'}, dimensions={0} | all-to-all | bytes 524288 | tf_op jit(solution)/shard_map/all_to_all | solution.py:201
  159.0 1.3 fusion.14
  (6 shorter events, 0.1 us)
Async XLA Ops:
  0.6 81.2 %copy-start = (f32[512,512]{1,0:T(8,128)S(1)}, f32[512,512]{1,0:T(8,128)}, u32[]{:S(2)}) copy-start(f32[512,512]{1,0:T(8,128)} %param.7) | copy-start | bytes 3145732
  28.7 10.1 %collective-permute-start = (bf16[256,512]{1,0:T(8,128)(2,1)S(1)}, bf16[256,512]{1,0:T(8,128)(2,1)S(1)}, u32[]{:S(2)}, u32[]{:S(2)}) collective-permute-start(bf16[256,512]{1,0:T(8,128)(2,1)S(1)} %all_gather.3), channel_id=1, source_target_pairs={{0,480},{32,0},{64,32},{96,64},{128,96},{160,128},{192,160},{224,1... | collective-permute-start | bytes 786440 | tf_op jit(solution)/shard_map/ppermute | solution.py:197
  31.6 13.4 %all-to-all-start = ((s32[4,8,3200]{2,1,0:T(8,128)}), s32[4,8,3200]{2,1,0:T(8,128)S(1)}, u32[]{:S(2)}, u32[]{:S(2)}) async-start(s32[4,8,3200]{2,1,0:T(8,128)} %get-tuple-element.19), calls=%async_computation | async-start | bytes 819200 | tf_op jit(solution)/shard_map/all_to_all | solution.py:216
  35.9 13.3 %collective-permute-start.1 = (bf16[256,512]{1,0:T(8,128)(2,1)S(1)}, bf16[256,512]{1,0:T(8,128)(2,1)S(1)}, u32[]{:S(2)}, u32[]{:S(2)}) collective-permute-start(bf16[256,512]{1,0:T(8,128)(2,1)S(1)} %all_gather.3), channel_id=1, source_target_pairs={{0,32},{32,64},{64,96},{96,128},{128,160},{160,192},{192,224},{224... | collective-permute-start | bytes 786440 | tf_op jit(solution)/shard_map/ppermute | solution.py:197
  38.8 10.4 %collective-permute-start.2 = (bf16[256,512]{1,0:T(8,128)(2,1)S(1)}, bf16[256,512]{1,0:T(8,128)(2,1)S(1)}, u32[]{:S(2)}, u32[]{:S(2)}) collective-permute-start(bf16[256,512]{1,0:T(8,128)(2,1)S(1)} %collective-permute-done), channel_id=1, source_target_pairs={{0,480},{32,0},{64,32},{96,64},{128,96},{160,128},{192,160},{224,1... | collective-permute-start | bytes 786440 | tf_op jit(solution)/shard_map/ppermute | solution.py:197
  49.3 4.6 %collective-permute-start.3 = (bf16[1024,512]{1,0:T(8,128)(2,1)S(1)}, bf16[1024,512]{1,0:T(8,128)(2,1)S(1)}, u32[]{:S(2)}, u32[]{:S(2)}) collective-permute-start(bf16[1024,512]{1,0:T(8,128)(2,1)S(1)} %pad_maximum_fusion.1), channel_id=1, source_target_pairs={{0,1},{1,0},{2,3},{3,2},{4,5},{5,4},{6,7},{7,6},{8,9},{9,8},{10,11... | collective-permute-start | bytes 3145736 | tf_op jit(solution)/shard_map/ppermute | solution.py:193
  56.0 25.9 %copy-start.1 = (f32[64,512]{1,0:T(8,128)S(1)}, f32[64,512]{1,0:T(8,128)}, u32[]{:S(2)}) copy-start(f32[64,512]{1,0:T(8,128)} %param.8) | copy-start | bytes 393220
  56.0 25.9 %copy-start.2 = (f32[64,512]{1,0:T(8,128)S(1)}, f32[64,512]{1,0:T(8,128)}, u32[]{:S(2)}) copy-start(f32[64,512]{1,0:T(8,128)} %features_ref.1) | copy-start | bytes 393220
  102.8 5.5 %collective-permute-start.4 = (bf16[1024,512]{1,0:T(8,128)(2,1)S(1)}, bf16[1024,512]{1,0:T(8,128)(2,1)S(1)}, u32[]{:S(2)}, u32[]{:S(2)}) collective-permute-start(bf16[1024,512]{1,0:T(8,128)(2,1)S(1)} %bitcast.22), channel_id=1, source_target_pairs={{0,1},{1,0},{2,3},{3,2},{4,5},{5,4},{6,7},{7,6},{8,9},{9,8},{10,11... | collective-permute-start | bytes 3145736 | tf_op jit(solution)/shard_map/ppermute | solution.py:193
  108.9 10.7 %collective-permute-start.5 = (bf16[256,512]{1,0:T(8,128)(2,1)S(1)}, bf16[256,512]{1,0:T(8,128)(2,1)S(1)}, u32[]{:S(2)}, u32[]{:S(2)}) collective-permute-start(bf16[256,512]{1,0:T(8,128)(2,1)S(1)} %add_convert_fusion.1), channel_id=1, source_target_pairs={{0,32},{32,64},{64,96},{96,128},{128,160},{160,192},{192,224},{224... | collective-permute-start | bytes 786440 | tf_op jit(solution)/shard_map/ppermute | solution.py:197
  114.1 11.5 %collective-permute-start.7 = (bf16[256,512]{1,0:T(8,128)(2,1)S(1)}, bf16[256,512]{1,0:T(8,128)(2,1)S(1)}, u32[]{:S(2)}, u32[]{:S(2)}) collective-permute-start(bf16[256,512]{1,0:T(8,128)(2,1)S(1)} %slice.70), channel_id=1, source_target_pairs={{0,480},{32,0},{64,32},{96,64},{128,96},{160,128},{192,160},{224,1... | collective-permute-start | bytes 786440 | tf_op jit(solution)/shard_map/ppermute | solution.py:197
  119.7 12.0 %collective-permute-start.6 = (bf16[256,512]{1,0:T(8,128)(2,1)S(1)}, bf16[256,512]{1,0:T(8,128)(2,1)S(1)}, u32[]{:S(2)}, u32[]{:S(2)}) collective-permute-start(bf16[256,512]{1,0:T(8,128)(2,1)S(1)} %fusion.6), channel_id=1, source_target_pairs={{0,32},{32,64},{64,96},{96,128},{128,160},{160,192},{192,224},{224... | collective-permute-start | bytes 786440 | tf_op jit(solution)/shard_map/ppermute | solution.py:197

commit v4 on v3

--- a/solution.py
+++ b/solution.py
@@ -1,5 +1,3 @@
-import functools
-
 import jax
 import jax.numpy as jnp
 from jax import lax
@@ -71,16 +69,20 @@
     return (z_lo + place + jnp.where(place == 2, 1, 0) - jnp.where(place == 3, 1, 0)) & (N_Z_LO - 1)
 
 
-def adjacency_kernel(crossed, place_ref, codes_ref, *outs):
-    own_ref, *others, picked_ref, left_ref = outs
+def adjacency_kernel(place_ref, codes_ref, from_x_ref, *refs):
+    own_ref, cross_ref, own_degree_ref, cross_degree_ref, picked_ref, left_ref = refs
     core, x_hi, z_lo = place_ref[0], place_ref[1], place_ref[2]
 
-    for x in range(N_X_HI):
-        for t in range(R // N_X_HI // 128):
-            pieces = [codes_ref[N_CORE * x, :2, pl.ds(256 * t + 128 * k, 128)] for k in range(2)]
-            picked_ref[:, pl.ds(R // N_X_HI * x + 128 * t, 128)] = halves(*pieces, core ^ 1 if crossed else core)
-    rows = picked_ref[...].astype(jnp.float32)
-    left_ref[...] = stack_rows(row_digits(rows[:1], rows[1:]), R)
+    for crossed in range(2):
+        for x in range(N_X_HI):
+            for t in range(R // N_X_HI // 128):
+                pieces = []
+                for k in range(2):
+                    at = pl.ds(256 * t + 128 * k, 128)
+                    pieces.append(jnp.where(x_hi == x, codes_ref[:2, at], from_x_ref[:2, at]))
+                picked_ref[:, pl.ds(R // N_X_HI * x + 128 * t, 128)] = halves(*pieces, core ^ crossed)
+        rows = picked_ref[...].astype(jnp.float32)
+        left_ref[crossed] = stack_rows(row_digits(rows[:1], rows[1:]), R)
 
     groups = (N_Z, HALF)
     column = lax.broadcasted_iota(jnp.int32, groups, 1)
@@ -88,23 +90,25 @@
     spread = jnp.where(lax.broadcasted_iota(jnp.int32, groups, 0) == tile, 1.0, 0.0).astype(jnp.bfloat16)
     ones = jnp.ones((8, HALF), jnp.bfloat16)
     lane = lax.broadcasted_iota(jnp.int32, (8, 128), 1)
-    for side in range(1 if crossed else 2):
-        for place in range(N_Z_LO):
-            for h in range(N_Z_HI // 2):
-                pieces = []
-                for k in range(2):
-                    at = R + ((2 * h + k) * N_Z_LO + class_of(jnp.int32(place), z_lo)) * 128
-                    pieces.append(codes_ref[core ^ side, :2, pl.ds(pl.multiple_of(at, 128), 128)])
-                picked_ref[:, pl.ds(BLOCK * place + 128 * h, 128)] = halves(*pieces, x_hi)
-        columns = picked_ref[...].astype(jnp.float32)
-        right = stack_rows(column_digits(columns[:1], columns[1:]), HALF)
-        masks = [codes_ref[N_CORE * x + (core ^ side), :, R + COLS : R + COLS + N_Z] for x in range(N_X_HI)]
-        mask = jnp.concatenate(masks, axis=0).astype(jnp.float32).astype(jnp.bfloat16)
-        limit = jnp.dot(mask, spread, preferred_element_type=jnp.float32) * place_ref[3 + side].astype(jnp.float32)
+    for place in range(N_Z_LO):
+        for h in range(N_Z_HI // 2):
+            pieces = []
+            for k in range(2):
+                at = R + ((2 * h + k) * N_Z_LO + class_of(jnp.int32(place), z_lo)) * 128
+                pieces.append(codes_ref[:2, pl.ds(pl.multiple_of(at, 128), 128)])
+            picked_ref[:, pl.ds(BLOCK * place + 128 * h, 128)] = halves(*pieces, x_hi)
+    columns = picked_ref[...].astype(jnp.float32)
+    right = stack_rows(column_digits(columns[:1], columns[1:]), HALF)
+    masks = (codes_ref[:, R + COLS : R + COLS + N_Z], from_x_ref[:, R : R + N_Z])
+    mask = jnp.concatenate([jnp.where(x_hi == x, *masks) for x in range(N_X_HI)], axis=0)
+    mask = mask.astype(jnp.float32).astype(jnp.bfloat16)
+    limit = jnp.dot(mask, spread, preferred_element_type=jnp.float32) * place_ref[3].astype(jnp.float32)
+
+    for crossed, (block_ref, degree_ref) in enumerate(((own_ref, own_degree_ref), (cross_ref, cross_degree_ref))):
         for pair in range(N_XY // 2):
             at = pl.ds(2 * RPD * pair, 2 * RPD)
             contract = (((0,), (0,)), ((), ()))
-            value = lax.dot_general(left_ref[:, at], right, contract, preferred_element_type=jnp.float32)
+            value = lax.dot_general(left_ref[crossed, :, at], right, contract, preferred_element_type=jnp.float32)
             nearest = jnp.round(value * (1.0 / hash_prime))
             residue = value - nearest * float(hash_prime)
             kept = []
@@ -113,41 +117,31 @@
                 inside = jnp.logical_and(part >= 0.0, part < limit[2 * pair + k][None, :])
                 kept.append(jnp.where(inside, 1.0, 0.0))
             low = jnp.concatenate(kept, axis=0).astype(jnp.bfloat16)
-            if crossed:
-                own_ref[at, :] = low
-                continue
-            other_ref, degree_ref = others
+            block_ref[at, :] = low
             contract = (((1,), (1,)), ((), ()))
             count = lax.dot_general(ones, low, contract, preferred_element_type=jnp.float32)
-            if side == 0:
-                own_ref[at, :] = low
-                degree_ref[2 * pair : 2 * pair + 2] = jnp.zeros((2, 8, 128), jnp.float32)
-            else:
-                other_ref[at, :] = low
             for k in range(2):
                 part = pltpu.roll(count, RPD, 1) if k else count
-                degree_ref[2 * pair + k] += jnp.where(lane < RPD, part, 0.0)
-
-
-def build_adjacency(crossed, place, codes):
+                degree_ref[2 * pair + k] = jnp.where(lane < RPD, part, 0.0)
+
+
+def build_adjacency(place, codes, from_x):
     vmem = pl.BlockSpec(memory_space=pltpu.VMEM)
     block = jax.ShapeDtypeStruct((R, HALF), jnp.bfloat16)
-    outs = [block] if crossed else [block, block, jax.ShapeDtypeStruct((N_XY, 8, 128), jnp.float32)]
+    degree = jax.ShapeDtypeStruct((N_XY, 8, 128), jnp.float32)
     return pl.pallas_call(
-        functools.partial(adjacency_kernel, crossed),
-        in_specs=[pl.BlockSpec(memory_space=pltpu.SMEM), vmem],
-        out_specs=[vmem] * len(outs),
-        out_shape=outs,
-        scratch_shapes=[pltpu.VMEM((2, R), jnp.int32), pltpu.VMEM((DIGITS, R), jnp.bfloat16)],
+        adjacency_kernel,
+        in_specs=[pl.BlockSpec(memory_space=pltpu.SMEM), vmem, vmem],
+        out_specs=[vmem] * 4,
+        out_shape=[block, block, degree, degree],
+        scratch_shapes=[pltpu.VMEM((2, R), jnp.int32), pltpu.VMEM((2, DIGITS, R), jnp.bfloat16)],
         compiler_params=pltpu.CompilerParams(vmem_limit_bytes=6 * 1024 * 1024),
-        cost_estimate=pl.CostEstimate(
-            flops=2 * R * HALF * 16 * len(outs), bytes_accessed=2 * R * HALF * len(outs), transcendentals=0
-        ),
-    )(place, codes)
-
-
-def prepare_kernel(features_ref, rows_ref, columns_ref, mask_ref, low_ref, codes_ref, values_ref, *scratch):
-    *held, sems = scratch
+        cost_estimate=pl.CostEstimate(flops=4 * R * HALF * 16, bytes_accessed=4 * R * HALF, transcendentals=0),
+    )(place, codes, from_x)
+
+
+def prepare_kernel(features_ref, rows_ref, columns_ref, mask_ref, low_ref, codes_ref, shared_ref, *scratch):
+    values_ref, *held, sems = scratch
     copies = [
         pltpu.make_async_copy(source, target, sems.at[k])
         for k, (source, target) in enumerate(zip((features_ref, rows_ref, columns_ref, mask_ref), (values_ref, *held)))
@@ -155,13 +149,15 @@
     for copy in copies:
         copy.start()
     codes_ref[...] = jnp.zeros_like(codes_ref)
+    shared_ref[...] = jnp.zeros_like(shared_ref)
     for copy in copies:
         copy.wait()
     rows, columns, mask = held
-    for k in range(N_X_HI * N_CORE):
-        codes_ref[k, :2, :R] = rows[...]
-        codes_ref[k, :2, R : R + COLS] = columns[...]
-        codes_ref[k, :, R + COLS : R + COLS + N_Z] = mask[...]
+    codes_ref[:2, :R] = rows[...]
+    codes_ref[:2, R : R + COLS] = columns[...]
+    codes_ref[:, R + COLS : R + COLS + N_Z] = mask[...]
+    shared_ref[:2, :R] = rows[...]
+    shared_ref[:, R : R + N_Z] = mask[...]
     low_ref[...] = values_ref[...].astype(jnp.bfloat16)
 
 
@@ -171,10 +167,11 @@
     return pl.pallas_call(
         prepare_kernel,
         in_specs=[pl.BlockSpec(memory_space=pl.ANY)] * 4,
-        out_specs=[vmem, vmem],
+        out_specs=[vmem, vmem, vmem],
         out_shape=[
             jax.ShapeDtypeStruct(features.shape, jnp.bfloat16),
-            jax.ShapeDtypeStruct((N_X_HI * N_CORE, 8, R + COLS + 128), jnp.int32),
+            jax.ShapeDtypeStruct((8, R + COLS + 128), jnp.int32),
+            jax.ShapeDtypeStruct((8, R + 128), jnp.int32),
         ],
         scratch_shapes=[pltpu.VMEM(array.shape, array.dtype) for array in arrays] + [pltpu.SemaphoreType.DMA((4,))],
         compiler_params=pltpu.CompilerParams(vmem_limit_bytes=56 * 1024 * 1024),
@@ -209,22 +206,28 @@
     x_hi, z_lo, core = lax.axis_index("xh"), lax.axis_index("zl"), lax.axis_index("c")
     subset = (lax.axis_index("xl") * N_Y + lax.axis_index("y")) * N_CORE + core
 
-    thresholds = [(10 + 20 * p // (N_REP - 1)) * hash_prime // 1000 for p in (subset, subset ^ 1)]
-    place = jnp.stack([core, x_hi, z_lo, *thresholds]).astype(jnp.int32)
-
-    low, codes = prepare(features, row_codes, col_codes, tile_mask)
-    codes = lax.all_to_all(codes, ("xh", "c"), 0, 0, tiled=True)
+    threshold = (10 + 20 * subset // (N_REP - 1)) * hash_prime // 1000
+    place = jnp.stack([core, x_hi, z_lo, threshold]).astype(jnp.int32)
+
+    low, codes, shared = prepare(features, row_codes, col_codes, tile_mask)
+    from_x = lax.ppermute(shared, "xh", [(0, 1), (1, 0)])
     block = lax.all_gather(low, "zh", axis=0, tiled=True)
     up, down = along_z(block, -1), along_z(block, 1)
+    up, from_x = lax.optimization_barrier((up, from_x))
     far = along_z(up, -1)
-    own, other, degree = build_adjacency(False, place, codes)
-    degree = jnp.pad(degree, ((0, 0), (0, 0), (0, F - 128))).astype(jnp.float16)
+    own, cross, own_degree, cross_degree = build_adjacency(place, codes, from_x)
     gathered = jnp.concatenate([block, up, down, far], axis=0)
-    gathered, own, other, degree = lax.optimization_barrier((gathered, own, other, degree))
-    aggregate = multiply(own, gathered)
-    aggregate, gathered = lax.optimization_barrier((aggregate, to_other_core(gathered)))
-    aggregate += multiply(other, gathered)
-    sent = jnp.concatenate([aggregate.astype(jnp.float16).reshape(N_XY, RPD, F), degree], axis=1)
+    gathered, own, cross, own_degree, cross_degree = lax.optimization_barrier(
+        (gathered, own, cross, own_degree, cross_degree)
+    )
+
+    def with_degree(aggregate, degree):
+        degree = jnp.pad(degree, ((0, 0), (0, 0), (0, F - 128)))
+        return jnp.concatenate([aggregate.reshape(N_XY, RPD, F), degree], axis=1)
+
+    crossing = to_other_core(with_degree(multiply(cross, gathered), cross_degree).astype(jnp.float16))
+    aggregate, crossing = lax.optimization_barrier((multiply(own, gathered), crossing))
+    sent = (with_degree(aggregate, own_degree) + crossing.astype(jnp.float32)).astype(jnp.float16)
     arrived = lax.all_to_all(sent, XY, 0, 0).astype(jnp.float32).sum(axis=0)
     degree = arrived[RPD, :RPD][:, None]
     aggregate = arrived[:RPD]
@@ -236,8 +239,6 @@
     pulled = cotangent * jax.nn.sigmoid(pre_act) * row_scale
 
     pulled_block = to_all(pulled.astype(jnp.bfloat16), XY, N_XY)
-    pulled_block, codes = lax.optimization_barrier((pulled_block, codes))
-    (cross,) = build_adjacency(True, place, codes)
     far_term = multiply_transposed(own[:, 3 * BLOCK :], pulled_block)
     term = multiply_transposed(own[:, : 3 * BLOCK], pulled_block)
     far_term, term, pulled_other = lax.optimization_barrier((far_term, term, to_other_core(pulled_block)))

time: 161 us -> 156 us (0.969)
  Pallas kernels: 8.04 us -> 5.23 us
  waiting for transfers between devices: 15.6 us -> 13.8 us
    ppermute x0 -> x1, starting transfers between devices: none -> 4.93 us  [per_device(): from_x = lax.ppermute(shared, 'xh', [(0, 1), (1, 0)])]
    all_to_all x1 -> x0, starting transfers between devices: 4.3 us -> none  [per_device(): codes = lax.all_to_all(codes, ('xh', 'c'), 0, 0, tiled=True)]
    all_to_all x1 -> x0, waiting for transfers between devices: 3.04 us -> none  [per_device(): codes = lax.all_to_all(codes, ('xh', 'c'), 0, 0, tiled=True)]
    pallas_call x2 -> x1, Pallas kernels: 6.21 us -> 3.51 us  [build_adjacency(): pl.pallas_call(adjacency_kernel, in_specs=[pl.BlockSpec(memory_space=pltp...]
  transfers between devices with their start and end apart: 9 -> 9, of which waited for: 5 -> 6; matrix products, arithmetic and copies ran while one was open for 3% -> 3% of each run, Pallas kernels for 4% -> 2%
where the time goes in v4:
time: 156 us; the launch traced here: 155 us
  blocking collectives  98 us (63%)
  starting transfers between devices  26.7 us (17%)
  waiting for transfers between devices  13.8 us (9%)
  matrix products  7.91 us (5%)
  Pallas kernels  5.23 us (3%)
  other arithmetic  1.67 us (1%)
    all_to_all x2, blocking collectives, exchange(): return lax.all_to_all(values, axis, 0, 0, tiled=True)  46.3 us
    all_gather x1, blocking collectives, per_device(): block = lax.all_gather(low, 'zh', axis=0, tiled=True)  26.2 us
    all_to_all x1, blocking collectives, per_device(): arrived = lax.all_to_all(sent, XY, 0, 0).astype(jnp.float32).sum(axis=0)  25.6 us
    ppermute x6, starting transfers between devices, along_z(): return lax.ppermute(values, Z, [(z, (z + step) % N_Z) for z in range(N_Z)])  17.9 us
    ppermute x6, waiting for transfers between devices, along_z(): return lax.ppermute(values, Z, [(z, (z + step) % N_Z) for z in range(N_Z)])  11.1 us
    ppermute x1, starting transfers between devices, per_device(): from_x = lax.ppermute(shared, 'xh', [(0, 1), (1, 0)])  4.93 us
    ppermute x2, starting transfers between devices, to_other_core(): return lax.ppermute(values, 'c', [(0, 1), (1, 0)])  3.83 us
    pallas_call x1, Pallas kernels, build_adjacency(): pl.pallas_call(adjacency_kernel, in_specs=[pl.BlockSpec(memory_space=pltp...  3.51 us
  transfers between devices with their start and end apart: 9, of which 6 were waited for; matrix products, arithmetic and copies ran while one was open for 3% of the time, Pallas kernels for 2%

profile of v4, /device:TPU:32, one launch (start us, length us, event | category | flops | bytes accessed | tf_op | source)
XLA Modules:
  0.0 155.3 jit_solution(17935055398165272414)
XLA Ops:
  0.6 0.0 copy-start
  0.6 1.7 %shard_map.77 = (bf16[64,512]{1,0:T(8,128)(2,1)}, s32[8,3200]{1,0:T(8,128)}, s32[8,1152]{1,0:T(8,128)}) custom-call(f32[64,512]{1,0:T(8,128)} %features_ref.1, s32[2,1024]{1,0:T(2,128)} %rows_ref.1, s32[2,2048]{1,0:T(2,128)} %columns_ref.1, s32[8,16]{1,0:T(8,128)} %mask_ref.1), custom_call_target="tpu_custom_call" | custom-call | tf_op jit(solution)/shard_map/pallas_call | solution.py:167
  2.4 26.2 %all_gather.3 = bf16[256,512]{1,0:T(8,128)(2,1)S(1)} all-gather(bf16[64,512]{1,0:T(8,128)(2,1)} %get-tuple-element.21), channel_id=1, replica_groups=mesh['zh'=4,'zl'=4,'xh'=2,'xl'=2,'y'=4,'c'=2] {'zh'}, dimensions={0}, use_global_device_ids=true | all-gather | bytes 327680 | tf_op jit(solution)/shard_map/all_gather | solution.py:214
  28.6 2.9 %collective-permute-start = (bf16[256,512]{1,0:T(8,128)(2,1)S(1)}, bf16[256,512]{1,0:T(8,128)(2,1)S(1)}, u32[]{:S(2)}, u32[]{:S(2)}) collective-permute-start(bf16[256,512]{1,0:T(8,128)(2,1)S(1)} %all_gather.3), channel_id=1, source_target_pairs={{0,480},{32,0},{64,32},{96,64},{128,96},{160,128},{192,160},{224,1... | collective-permute-start | bytes 786440 | tf_op jit(solution)/shard_map/ppermute | solution.py:194
  31.5 4.9 %collective-permute-start.1 = (s32[8,1152]{1,0:T(8,128)}, s32[8,1152]{1,0:T(8,128)S(1)}, u32[]{:S(2)}, u32[]{:S(2)}) collective-permute-start(s32[8,1152]{1,0:T(8,128)} %get-tuple-element.22), channel_id=1, source_target_pairs={{0,16},{16,0},{1,17},{17,1},{2,18},{18,2},{3,19},{19,3},{4,20},{20... | collective-permute-start | bytes 110600 | tf_op jit(solution)/shard_map/ppermute | solution.py:213
  36.4 2.9 %collective-permute-start.2 = (bf16[256,512]{1,0:T(8,128)(2,1)S(1)}, bf16[256,512]{1,0:T(8,128)(2,1)S(1)}, u32[]{:S(2)}, u32[]{:S(2)}) collective-permute-start(bf16[256,512]{1,0:T(8,128)(2,1)S(1)} %all_gather.3), channel_id=1, source_target_pairs={{0,32},{32,64},{64,96},{96,128},{128,160},{160,192},{192,224},{224... | collective-permute-start | bytes 786440 | tf_op jit(solution)/shard_map/ppermute | solution.py:194
  39.4 0.0 collective-permute-done.1.from_x_ref
  39.4 0.0 collective-permute-done
  39.4 3.6 %collective-permute-start.3 = (bf16[256,512]{1,0:T(8,128)(2,1)S(1)}, bf16[256,512]{1,0:T(8,128)(2,1)S(1)}, u32[]{:S(2)}, u32[]{:S(2)}) collective-permute-start(bf16[256,512]{1,0:T(8,128)(2,1)S(1)} %collective-permute-done), channel_id=1, source_target_pairs={{0,480},{32,0},{64,32},{96,64},{128,96},{160,128},{192,160},{224,1... | collective-permute-start | bytes 786440 | tf_op jit(solution)/shard_map/ppermute | solution.py:194
  43.1 0.1 pad_add_fusion.place_ref
  43.2 0.9 copy-done.1
  44.1 3.5 %shard_map.78 = (bf16[1024,1024]{1,0:T(8,128)(2,1)S(1)}, bf16[1024,1024]{1,0:T(8,128)(2,1)S(1)}, f32[16,8,128]{2,1,0:T(8,128)S(1)}, f32[16,8,128]{2,1,0:T(8,128)S(1)}) custom-call(s32[4]{0:T(128)S(1)} %pad_add_fusion.place_ref, s32[8,3200]{1,0:T(8,128)S(1)} %copy-done.1, s32[8,1152]{1,0:T(8,128)S(1)} %collective-permute-done.1.from_x_ref), custom_call_target="tpu_custom_call" | custom-call | flops 67108864 | bytes 4194304 | tf_op jit(solution)/shard_map/pallas_call | solution.py:132
  47.6 0.0 collective-permute-done.2
  47.6 0.1 collective-permute-done.3
  47.6 0.1 pad_maximum_fusion
  47.7 1.2 convolution_convert_fusion
  49.0 0.3 fusion.7
  49.3 1.9 %collective-permute-start.4 = (f16[16,72,512]{2,1,0:T(8,128)(2,1)S(1)}, f16[16,72,512]{2,1,0:T(8,128)(2,1)S(1)}, u32[]{:S(2)}, u32[]{:S(2)}) collective-permute-start(f16[16,72,512]{2,1,0:T(8,128)(2,1)S(1)} %fusion.7), channel_id=1, source_target_pairs={{0,1},{1,0},{2,3},{3,2},{4,5},{5,4},{6,7},{7,6},{8,9},{9,8},{10,11... | collective-permute-start | bytes 3538952 | tf_op jit(solution)/shard_map/ppermute | solution.py:190
  51.2 1.3 fusion.24
  52.4 1.6 %collective-permute-done.4 = f16[16,72,512]{2,1,0:T(8,128)(2,1)S(1)} collective-permute-done((f16[16,72,512]{2,1,0:T(8,128)(2,1)S(1)}, f16[16,72,512]{2,1,0:T(8,128)(2,1)S(1)}, u32[]{:S(2)}, u32[]{:S(2)}) %collective-permute-start.4) | collective-permute-done | bytes 1179680 | tf_op jit(solution)/shard_map/ppermute | solution.py:190
  54.0 0.4 fusion.1
  54.4 0.0 copy-start.2
  54.4 0.0 copy-start.3
  54.4 25.6 %all_to_all.23 = f16[16,72,512]{2,1,0:T(8,128)(2,1)S(1)} all-to-all(f16[16,72,512]{2,1,0:T(8,128)(2,1)S(1)} %fusion.1), channel_id=1, replica_groups=mesh['zh'=4,'zl'=4,'xh'=2,'xl'=2,'y'=4,'c'=2] {'xh','xl','y'}, dimensions={0} | all-to-all | bytes 2359296 | tf_op jit(solution)/shard_map/all_to_all | solution.py:231
  80.0 0.2 convert_reduce_fusion
  80.2 0.0 copy-done
  80.2 0.0 copy-done.2
  80.2 1.2 fusion.23
  81.4 0.1 broadcast_in_dim.2
  81.5 19.7 %all_to_all.24 = bf16[16,64,512]{2,1,0:T(8,128)(2,1)S(1)} all-to-all(bf16[16,64,512]{2,1,0:T(8,128)(2,1)S(1)} %broadcast_in_dim.2), channel_id=1, replica_groups=mesh['zh'=4,'zl'=4,'xh'=2,'xl'=2,'y'=4,'c'=2] {'xh','xl','y'}, dimensions={0} | all-to-all | bytes 2097152 | tf_op jit(solution)/shard_map/all_to_all | solution.py:198
  101.2 1.9 %collective-permute-start.5 = (bf16[1024,512]{1,0:T(8,128)(2,1)S(1)}, bf16[1024,512]{1,0:T(8,128)(2,1)S(1)}, u32[]{:S(2)}, u32[]{:S(2)}) collective-permute-start(bf16[1024,512]{1,0:T(8,128)(2,1)S(1)} %bitcast.22), channel_id=1, source_target_pairs={{0,1},{1,0},{2,3},{3,2},{4,5},{5,4},{6,7},{7,6},{8,9},{9,8},{10,11... | collective-permute-start | bytes 3145736 | tf_op jit(solution)/shard_map/ppermute | solution.py:190
  103.1 0.5 fusion.13
  103.6 1.0 fusion.5
  104.6 1.1 collective-permute-done.5
  105.7 0.5 fusion.11
  106.2 0.1 add_convert_fusion
  106.3 2.6 %collective-permute-start.6 = (bf16[256,512]{1,0:T(8,128)(2,1)S(1)}, bf16[256,512]{1,0:T(8,128)(2,1)S(1)}, u32[]{:S(2)}, u32[]{:S(2)}) collective-permute-start(bf16[256,512]{1,0:T(8,128)(2,1)S(1)} %add_convert_fusion), channel_id=1, source_target_pairs={{0,32},{32,64},{64,96},{96,128},{128,160},{160,192},{192,224},{224... | collective-permute-start | bytes 786440 | tf_op jit(solution)/shard_map/ppermute | solution.py:194
  108.9 1.0 fusion.3
  109.9 0.3 add.63
  110.3 3.2 %collective-permute-start.8 = (bf16[256,512]{1,0:T(8,128)(2,1)S(1)}, bf16[256,512]{1,0:T(8,128)(2,1)S(1)}, u32[]{:S(2)}, u32[]{:S(2)}) collective-permute-start(bf16[256,512]{1,0:T(8,128)(2,1)S(1)} %slice.68), channel_id=1, source_target_pairs={{0,480},{32,0},{64,32},{96,64},{128,96},{160,128},{192,160},{224,1... | collective-permute-start | bytes 786440 | tf_op jit(solution)/shard_map/ppermute | solution.py:194
  113.6 3.0 %collective-permute-done.6 = bf16[256,512]{1,0:T(8,128)(2,1)S(1)} collective-permute-done((bf16[256,512]{1,0:T(8,128)(2,1)S(1)}, bf16[256,512]{1,0:T(8,128)(2,1)S(1)}, u32[]{:S(2)}, u32[]{:S(2)}) %collective-permute-start.6) | collective-permute-done | bytes 262176 | tf_op jit(solution)/shard_map/ppermute | solution.py:194
  116.6 0.1 fusion.8
  116.7 2.6 %collective-permute-start.7 = (bf16[256,512]{1,0:T(8,128)(2,1)S(1)}, bf16[256,512]{1,0:T(8,128)(2,1)S(1)}, u32[]{:S(2)}, u32[]{:S(2)}) collective-permute-start(bf16[256,512]{1,0:T(8,128)(2,1)S(1)} %fusion.8), channel_id=1, source_target_pairs={{0,32},{32,64},{64,96},{96,128},{128,160},{160,192},{192,224},{224... | collective-permute-start | bytes 786440 | tf_op jit(solution)/shard_map/ppermute | solution.py:194
  119.3 1.6 %collective-permute-done.8 = bf16[256,512]{1,0:T(8,128)(2,1)S(1)} collective-permute-done((bf16[256,512]{1,0:T(8,128)(2,1)S(1)}, bf16[256,512]{1,0:T(8,128)(2,1)S(1)}, u32[]{:S(2)}, u32[]{:S(2)}) %collective-permute-start.8) | collective-permute-done | bytes 262176 | tf_op jit(solution)/shard_map/ppermute | solution.py:194
  120.8 6.4 %collective-permute-done.7 = bf16[256,512]{1,0:T(8,128)(2,1)S(1)} collective-permute-done((bf16[256,512]{1,0:T(8,128)(2,1)S(1)}, bf16[256,512]{1,0:T(8,128)(2,1)S(1)}, u32[]{:S(2)}, u32[]{:S(2)}) %collective-permute-start.7) | collective-permute-done | bytes 262176 | tf_op jit(solution)/shard_map/ppermute | solution.py:194
  127.3 0.1 fusion.10
  127.4 26.6 %all_to_all.25 = bf16[4,64,512]{2,1,0:T(8,128)(2,1)S(1)} all-to-all(bf16[4,64,512]{2,1,0:T(8,128)(2,1)S(1)} %bitcast.21), channel_id=1, replica_groups=mesh['zh'=4,'zl'=4,'xh'=2,'xl'=2,'y'=4,'c'=2] {'zh'}, dimensions={0} | all-to-all | bytes 524288 | tf_op jit(solution)/shard_map/all_to_all | solution.py:198
  154.0 1.3 fusion.18
  (6 shorter events, 0.1 us)
Async XLA Ops:
  0.6 79.6 %copy-start = (f32[512,512]{1,0:T(8,128)S(1)}, f32[512,512]{1,0:T(8,128)}, u32[]{:S(2)}) copy-start(f32[512,512]{1,0:T(8,128)} %param.7) | copy-start | bytes 3145732
  28.6 10.8 %collective-permute-start = (bf16[256,512]{1,0:T(8,128)(2,1)S(1)}, bf16[256,512]{1,0:T(8,128)(2,1)S(1)}, u32[]{:S(2)}, u32[]{:S(2)}) collective-permute-start(bf16[256,512]{1,0:T(8,128)(2,1)S(1)} %all_gather.3), channel_id=1, source_target_pairs={{0,480},{32,0},{64,32},{96,64},{128,96},{160,128},{192,160},{224,1... | collective-permute-start | bytes 786440 | tf_op jit(solution)/shard_map/ppermute | solution.py:194
  31.5 7.9 %collective-permute-start.1 = (s32[8,1152]{1,0:T(8,128)}, s32[8,1152]{1,0:T(8,128)S(1)}, u32[]{:S(2)}, u32[]{:S(2)}) collective-permute-start(s32[8,1152]{1,0:T(8,128)} %get-tuple-element.22), channel_id=1, source_target_pairs={{0,16},{16,0},{1,17},{17,1},{2,18},{18,2},{3,19},{19,3},{4,20},{20... | collective-permute-start | bytes 110600 | tf_op jit(solution)/shard_map/ppermute | solution.py:213
  36.4 11.1 %collective-permute-start.2 = (bf16[256,512]{1,0:T(8,128)(2,1)S(1)}, bf16[256,512]{1,0:T(8,128)(2,1)S(1)}, u32[]{:S(2)}, u32[]{:S(2)}) collective-permute-start(bf16[256,512]{1,0:T(8,128)(2,1)S(1)} %all_gather.3), channel_id=1, source_target_pairs={{0,32},{32,64},{64,96},{96,128},{128,160},{160,192},{192,224},{224... | collective-permute-start | bytes 786440 | tf_op jit(solution)/shard_map/ppermute | solution.py:194
  39.4 8.3 %collective-permute-start.3 = (bf16[256,512]{1,0:T(8,128)(2,1)S(1)}, bf16[256,512]{1,0:T(8,128)(2,1)S(1)}, u32[]{:S(2)}, u32[]{:S(2)}) collective-permute-start(bf16[256,512]{1,0:T(8,128)(2,1)S(1)} %collective-permute-done), channel_id=1, source_target_pairs={{0,480},{32,0},{64,32},{96,64},{128,96},{160,128},{192,160},{224,1... | collective-permute-start | bytes 786440 | tf_op jit(solution)/shard_map/ppermute | solution.py:194
  43.2 0.9 copy-start.1
  49.3 4.7 %collective-permute-start.4 = (f16[16,72,512]{2,1,0:T(8,128)(2,1)S(1)}, f16[16,72,512]{2,1,0:T(8,128)(2,1)S(1)}, u32[]{:S(2)}, u32[]{:S(2)}) collective-permute-start(f16[16,72,512]{2,1,0:T(8,128)(2,1)S(1)} %fusion.7), channel_id=1, source_target_pairs={{0,1},{1,0},{2,3},{3,2},{4,5},{5,4},{6,7},{7,6},{8,9},{9,8},{10,11... | collective-permute-start | bytes 3538952 | tf_op jit(solution)/shard_map/ppermute | solution.py:190
  54.4 25.8 %copy-start.2 = (f32[64,512]{1,0:T(8,128)S(1)}, f32[64,512]{1,0:T(8,128)}, u32[]{:S(2)}) copy-start(f32[64,512]{1,0:T(8,128)} %param.8) | copy-start | bytes 393220
  54.4 25.8 %copy-start.3 = (f32[64,512]{1,0:T(8,128)S(1)}, f32[64,512]{1,0:T(8,128)}, u32[]{:S(2)}) copy-start(f32[64,512]{1,0:T(8,128)} %features_ref.1) | copy-start | bytes 393220
  101.2 4.5 %collective-permute-start.5 = (bf16[1024,512]{1,0:T(8,128)(2,1)S(1)}, bf16[1024,512]{1,0:T(8,128)(2,1)S(1)}, u32[]{:S(2)}, u32[]{:S(2)}) collective-permute-start(bf16[1024,512]{1,0:T(8,128)(2,1)S(1)} %bitcast.22), channel_id=1, source_target_pairs={{0,1},{1,0},{2,3},{3,2},{4,5},{5,4},{6,7},{7,6},{8,9},{9,8},{10,11... | collective-permute-start | bytes 3145736 | tf_op jit(solution)/shard_map/ppermute | solution.py:190
  106.3 10.3 %collective-permute-start.6 = (bf16[256,512]{1,0:T(8,128)(2,1)S(1)}, bf16[256,512]{1,0:T(8,128)(2,1)S(1)}, u32[]{:S(2)}, u32[]{:S(2)}) collective-permute-start(bf16[256,512]{1,0:T(8,128)(2,1)S(1)} %add_convert_fusion), channel_id=1, source_target_pairs={{0,32},{32,64},{64,96},{96,128},{128,160},{160,192},{192,224},{224... | collective-permute-start | bytes 786440 | tf_op jit(solution)/shard_map/ppermute | solution.py:194
  110.3 10.5 %collective-permute-start.8 = (bf16[256,512]{1,0:T(8,128)(2,1)S(1)}, bf16[256,512]{1,0:T(8,128)(2,1)S(1)}, u32[]{:S(2)}, u32[]{:S(2)}) collective-permute-start(bf16[256,512]{1,0:T(8,128)(2,1)S(1)} %slice.68), channel_id=1, source_target_pairs={{0,480},{32,0},{64,32},{96,64},{128,96},{160,128},{192,160},{224,1... | collective-permute-start | bytes 786440 | tf_op jit(solution)/shard_map/ppermute | solution.py:194
  116.7 10.6 %collective-permute-start.7 = (bf16[256,512]{1,0:T(8,128)(2,1)S(1)}, bf16[256,512]{1,0:T(8,128)(2,1)S(1)}, u32[]{:S(2)}, u32[]{:S(2)}) collective-permute-start(bf16[256,512]{1,0:T(8,128)(2,1)S(1)} %fusion.8), channel_id=1, source_target_pairs={{0,32},{32,64},{64,96},{96,128},{128,160},{160,192},{192,224},{224... | collective-permute-start | bytes 786440 | tf_op jit(solution)/shard_map/ppermute | solution.py:194

commit v5 on v4

--- a/solution.py
+++ b/solution.py
@@ -178,6 +178,26 @@
     )(*arrays)
 
 
+def class_sums_kernel(z_hi_ref, term_ref, up_ref, down_ref, *sum_refs):
+    for step, sum_ref in enumerate(sum_refs):
+        start = ((z_hi_ref[0] + step) & (N_Z_HI - 1)) * RPD
+        at = pl.ds(pl.multiple_of(start, RPD), RPD)
+        total = term_ref[at, :] + up_ref[at, :].astype(jnp.float32) + down_ref[at, :].astype(jnp.float32)
+        sum_ref[...] = total.astype(sum_ref.dtype)
+
+
+def class_sums(z_hi, term, up, down):
+    vmem = pl.BlockSpec(memory_space=pltpu.VMEM)
+    kinds = (jnp.float32, jnp.float32, jnp.bfloat16, jnp.bfloat16)
+    return pl.pallas_call(
+        class_sums_kernel,
+        in_specs=[pl.BlockSpec(memory_space=pltpu.SMEM), vmem, vmem, vmem],
+        out_specs=[vmem] * N_Z_HI,
+        out_shape=[jax.ShapeDtypeStruct((RPD, F), kind) for kind in kinds],
+        compiler_params=pltpu.CompilerParams(vmem_limit_bytes=4 * 1024 * 1024),
+    )(z_hi.reshape(1).astype(jnp.int32), term, up, down)
+
+
 def multiply(left, right):
     return jnp.dot(left, right, preferred_element_type=jnp.float32)
 
@@ -247,8 +267,11 @@
     term += multiply_transposed(cross[:, : 3 * BLOCK], pulled_other)
     down = along_z(term[2 * BLOCK :].astype(jnp.bfloat16), -1)
     up = along_z((term[BLOCK : 2 * BLOCK] + passed.astype(jnp.float32)).astype(jnp.bfloat16), 1)
-    term = term[:BLOCK] + up.astype(jnp.float32) + down.astype(jnp.float32)
-    term = exchange(term.astype(jnp.bfloat16), "zh").reshape(N_Z_HI, RPD, F).astype(jnp.float32).sum(axis=0)
+    kept, ahead, opposite, behind = class_sums(lax.axis_index("zh"), term, up, down)
+    passed = along_z(opposite, N_Z_LO)
+    down = along_z(behind, -N_Z_LO)
+    up = along_z((ahead + passed.astype(jnp.float32)).astype(jnp.bfloat16), N_Z_LO)
+    term = kept + up.astype(jnp.float32) + down.astype(jnp.float32)
     grad_input = lax.dot_general(
         pulled + term, weight, (((1,), (1,)), ((), ())), precision=HIGH, preferred_element_type=jnp.float32
     )

time: 156 us -> 154 us (0.987)
  blocking collectives: 98 us -> 71.4 us
  starting transfers between devices: 26.7 us -> 40.9 us
  waiting for transfers between devices: 13.8 us -> 22.9 us
    all_to_all x2 -> x1, blocking collectives: 46.3 us -> 19.7 us  [exchange(): return lax.all_to_all(values, axis, 0, 0, tiled=True)]
    ppermute x6 -> x9, starting transfers between devices: 17.9 us -> 32.2 us  [along_z(): return lax.ppermute(values, Z, [(z, (z + step) % N_Z) for z in range(N_Z)])]
    ppermute x6 -> x9, waiting for transfers between devices: 11.1 us -> 20.2 us  [along_z(): return lax.ppermute(values, Z, [(z, (z + step) % N_Z) for z in range(N_Z)])]
  transfers between devices with their start and end apart: 9 -> 12, of which waited for: 6 -> 8; matrix products, arithmetic and copies ran while one was open for 3% -> 4% of each run, Pallas kernels for 2% -> 2%
where the time goes in v5:
time: 154 us; the launch traced here: 153 us
  blocking collectives  71.4 us (46%)
  starting transfers between devices  40.9 us (27%)
  waiting for transfers between devices  22.9 us (15%)
  matrix products  7.96 us (5%)
  Pallas kernels  5.31 us (3%)
  other arithmetic  2.22 us (1%)
  local copies, waits for them, and re-layouts  1.73 us (1%)
    ppermute x9, starting transfers between devices, along_z(): return lax.ppermute(values, Z, [(z, (z + step) % N_Z) for z in range(N_Z)])  32.2 us
    all_gather x1, blocking collectives, per_device(): block = lax.all_gather(low, 'zh', axis=0, tiled=True)  26.2 us
    all_to_all x1, blocking collectives, per_device(): arrived = lax.all_to_all(sent, XY, 0, 0).astype(jnp.float32).sum(axis=0)  25.6 us
    ppermute x9, waiting for transfers between devices, along_z(): return lax.ppermute(values, Z, [(z, (z + step) % N_Z) for z in range(N_Z)])  20.2 us
    all_to_all x1, blocking collectives, exchange(): return lax.all_to_all(values, axis, 0, 0, tiled=True)  19.7 us
    ppermute x1, starting transfers between devices, per_device(): from_x = lax.ppermute(shared, 'xh', [(0, 1), (1, 0)])  4.93 us
    ppermute x2, starting transfers between devices, to_other_core(): return lax.ppermute(values, 'c', [(0, 1), (1, 0)])  3.83 us
    pallas_call x1, Pallas kernels, build_adjacency(): pl.pallas_call(adjacency_kernel, in_specs=[pl.BlockSpec(memory_space=pltp...  3.51 us
  transfers between devices with their start and end apart: 12, of which 8 were waited for; matrix products, arithmetic and copies ran while one was open for 4% of the time, Pallas kernels for 2%

profile of v5, /device:TPU:32, one launch (start us, length us, event | category | flops | bytes accessed | tf_op | source)
XLA Modules:
  0.0 153.4 jit_solution(11784963331890727909)
XLA Ops:
  0.6 0.0 copy-start
  0.6 1.7 %shard_map.77 = (bf16[64,512]{1,0:T(8,128)(2,1)}, s32[8,3200]{1,0:T(8,128)}, s32[8,1152]{1,0:T(8,128)}) custom-call(f32[64,512]{1,0:T(8,128)} %features_ref.1, s32[2,1024]{1,0:T(2,128)} %rows_ref.1, s32[2,2048]{1,0:T(2,128)} %columns_ref.1, s32[8,16]{1,0:T(8,128)} %mask_ref.1), custom_call_target="tpu_custom_call" | custom-call | tf_op jit(solution)/shard_map/pallas_call | solution.py:167
  2.4 26.2 %all_gather.3 = bf16[256,512]{1,0:T(8,128)(2,1)S(1)} all-gather(bf16[64,512]{1,0:T(8,128)(2,1)} %get-tuple-element.25), channel_id=1, replica_groups=mesh['zh'=4,'zl'=4,'xh'=2,'xl'=2,'y'=4,'c'=2] {'zh'}, dimensions={0}, use_global_device_ids=true | all-gather | bytes 327680 | tf_op jit(solution)/shard_map/all_gather | solution.py:234
  28.6 2.9 %collective-permute-start = (bf16[256,512]{1,0:T(8,128)(2,1)S(1)}, bf16[256,512]{1,0:T(8,128)(2,1)S(1)}, u32[]{:S(2)}, u32[]{:S(2)}) collective-permute-start(bf16[256,512]{1,0:T(8,128)(2,1)S(1)} %all_gather.3), channel_id=1, source_target_pairs={{0,480},{32,0},{64,32},{96,64},{128,96},{160,128},{192,160},{224,1... | collective-permute-start | bytes 786440 | tf_op jit(solution)/shard_map/ppermute | solution.py:214
  31.5 4.9 %collective-permute-start.1 = (s32[8,1152]{1,0:T(8,128)}, s32[8,1152]{1,0:T(8,128)S(1)}, u32[]{:S(2)}, u32[]{:S(2)}) collective-permute-start(s32[8,1152]{1,0:T(8,128)} %get-tuple-element.26), channel_id=1, source_target_pairs={{0,16},{16,0},{1,17},{17,1},{2,18},{18,2},{3,19},{19,3},{4,20},{20... | collective-permute-start | bytes 110600 | tf_op jit(solution)/shard_map/ppermute | solution.py:233
  36.4 2.9 %collective-permute-start.2 = (bf16[256,512]{1,0:T(8,128)(2,1)S(1)}, bf16[256,512]{1,0:T(8,128)(2,1)S(1)}, u32[]{:S(2)}, u32[]{:S(2)}) collective-permute-start(bf16[256,512]{1,0:T(8,128)(2,1)S(1)} %all_gather.3), channel_id=1, source_target_pairs={{0,32},{32,64},{64,96},{96,128},{128,160},{160,192},{192,224},{224... | collective-permute-start | bytes 786440 | tf_op jit(solution)/shard_map/ppermute | solution.py:214
  39.4 3.6 %collective-permute-start.3 = (bf16[256,512]{1,0:T(8,128)(2,1)S(1)}, bf16[256,512]{1,0:T(8,128)(2,1)S(1)}, u32[]{:S(2)}, u32[]{:S(2)}) collective-permute-start(bf16[256,512]{1,0:T(8,128)(2,1)S(1)} %collective-permute-done), channel_id=1, source_target_pairs={{0,480},{32,0},{64,32},{96,64},{128,96},{160,128},{192,160},{224,1... | collective-permute-start | bytes 786440 | tf_op jit(solution)/shard_map/ppermute | solution.py:214
  43.1 0.1 pad_add_fusion.place_ref
  43.2 0.9 copy-done.1
  44.1 3.5 %shard_map.78 = (bf16[1024,1024]{1,0:T(8,128)(2,1)S(1)}, bf16[1024,1024]{1,0:T(8,128)(2,1)S(1)}, f32[16,8,128]{2,1,0:T(8,128)S(1)}, f32[16,8,128]{2,1,0:T(8,128)S(1)}) custom-call(s32[4]{0:T(128)S(1)} %pad_add_fusion.place_ref, s32[8,3200]{1,0:T(8,128)S(1)} %copy-done.1, s32[8,1152]{1,0:T(8,128)S(1)} %collective-permute-done.1.from_x_ref), custom_call_target="tpu_custom_call" | custom-call | flops 67108864 | bytes 4194304 | tf_op jit(solution)/shard_map/pallas_call | solution.py:132
  47.6 0.1 collective-permute-done.3
  47.6 0.1 pad_maximum_fusion
  47.7 1.2 convolution_convert_fusion
  49.0 0.3 fusion.7
  49.3 1.9 %collective-permute-start.4 = (f16[16,72,512]{2,1,0:T(8,128)(2,1)S(1)}, f16[16,72,512]{2,1,0:T(8,128)(2,1)S(1)}, u32[]{:S(2)}, u32[]{:S(2)}) collective-permute-start(f16[16,72,512]{2,1,0:T(8,128)(2,1)S(1)} %fusion.7), channel_id=1, source_target_pairs={{0,1},{1,0},{2,3},{3,2},{4,5},{5,4},{6,7},{7,6},{8,9},{9,8},{10,11... | collective-permute-start | bytes 3538952 | tf_op jit(solution)/shard_map/ppermute | solution.py:210
  51.2 1.3 fusion.26
  52.4 1.6 %collective-permute-done.4 = f16[16,72,512]{2,1,0:T(8,128)(2,1)S(1)} collective-permute-done((f16[16,72,512]{2,1,0:T(8,128)(2,1)S(1)}, f16[16,72,512]{2,1,0:T(8,128)(2,1)S(1)}, u32[]{:S(2)}, u32[]{:S(2)}) %collective-permute-start.4) | collective-permute-done | bytes 1179680 | tf_op jit(solution)/shard_map/ppermute | solution.py:210
  54.0 0.4 fusion.1
  54.4 0.0 copy-start.2
  54.4 0.0 copy-start.3
  54.4 25.6 %all_to_all.14 = f16[16,72,512]{2,1,0:T(8,128)(2,1)S(1)} all-to-all(f16[16,72,512]{2,1,0:T(8,128)(2,1)S(1)} %fusion.1), channel_id=1, replica_groups=mesh['zh'=4,'zl'=4,'xh'=2,'xl'=2,'y'=4,'c'=2] {'xh','xl','y'}, dimensions={0} | all-to-all | bytes 2359296 | tf_op jit(solution)/shard_map/all_to_all | solution.py:251
  80.0 0.2 convert_reduce_fusion
  80.2 1.2 fusion.25
  81.4 0.1 broadcast_in_dim.2
  81.5 19.7 %all_to_all.15 = bf16[16,64,512]{2,1,0:T(8,128)(2,1)S(1)} all-to-all(bf16[16,64,512]{2,1,0:T(8,128)(2,1)S(1)} %broadcast_in_dim.2), channel_id=1, replica_groups=mesh['zh'=4,'zl'=4,'xh'=2,'xl'=2,'y'=4,'c'=2] {'xh','xl','y'}, dimensions={0} | all-to-all | bytes 2097152 | tf_op jit(solution)/shard_map/all_to_all | solution.py:218
  101.2 1.9 %collective-permute-start.5 = (bf16[1024,512]{1,0:T(8,128)(2,1)S(1)}, bf16[1024,512]{1,0:T(8,128)(2,1)S(1)}, u32[]{:S(2)}, u32[]{:S(2)}) collective-permute-start(bf16[1024,512]{1,0:T(8,128)(2,1)S(1)} %bitcast.21), channel_id=1, source_target_pairs={{0,1},{1,0},{2,3},{3,2},{4,5},{5,4},{6,7},{7,6},{8,9},{9,8},{10,11... | collective-permute-start | bytes 3145736 | tf_op jit(solution)/shard_map/ppermute | solution.py:210
  103.1 0.5 fusion.11
  103.6 1.0 fusion.5
  104.6 1.1 collective-permute-done.5
  105.7 0.5 fusion.9
  106.2 0.1 add_convert_fusion
  106.3 2.6 %collective-permute-start.6 = (bf16[256,512]{1,0:T(8,128)(2,1)S(1)}, bf16[256,512]{1,0:T(8,128)(2,1)S(1)}, u32[]{:S(2)}, u32[]{:S(2)}) collective-permute-start(bf16[256,512]{1,0:T(8,128)(2,1)S(1)} %add_convert_fusion), channel_id=1, source_target_pairs={{0,32},{32,64},{64,96},{96,128},{128,160},{160,192},{192,224},{224... | collective-permute-start | bytes 786440 | tf_op jit(solution)/shard_map/ppermute | solution.py:214
  108.9 1.0 fusion.3
  109.9 0.3 add.66.term_ref
  110.3 0.7 slice.58
  111.0 3.2 %collective-permute-start.8 = (bf16[256,512]{1,0:T(8,128)(2,1)}, bf16[256,512]{1,0:T(8,128)(2,1)S(1)}, u32[]{:S(2)}, u32[]{:S(2)}) collective-permute-start(bf16[256,512]{1,0:T(8,128)(2,1)} %slice.58), channel_id=1, source_target_pairs={{0,480},{32,0},{64,32},{96,64},{128,96},{160,128},{192,160},{224,1... | collective-permute-start | bytes 786440 | tf_op jit(solution)/shard_map/ppermute | solution.py:214
  114.2 2.4 %collective-permute-done.6 = bf16[256,512]{1,0:T(8,128)(2,1)S(1)} collective-permute-done((bf16[256,512]{1,0:T(8,128)(2,1)S(1)}, bf16[256,512]{1,0:T(8,128)(2,1)S(1)}, u32[]{:S(2)}, u32[]{:S(2)}) %collective-permute-start.6) | collective-permute-done | bytes 262176 | tf_op jit(solution)/shard_map/ppermute | solution.py:214
  116.6 0.8 fusion.8
  117.4 2.6 %collective-permute-start.7 = (bf16[256,512]{1,0:T(8,128)(2,1)}, bf16[256,512]{1,0:T(8,128)(2,1)S(1)}, u32[]{:S(2)}, u32[]{:S(2)}) collective-permute-start(bf16[256,512]{1,0:T(8,128)(2,1)} %fusion.8), channel_id=1, source_target_pairs={{0,32},{32,64},{64,96},{96,128},{128,160},{160,192},{192,224},{224... | collective-permute-start | bytes 786440 | tf_op jit(solution)/shard_map/ppermute | solution.py:214
  119.9 1.8 %collective-permute-done.8.down_ref = bf16[256,512]{1,0:T(8,128)(2,1)S(1)} collective-permute-done((bf16[256,512]{1,0:T(8,128)(2,1)}, bf16[256,512]{1,0:T(8,128)(2,1)S(1)}, u32[]{:S(2)}, u32[]{:S(2)}) %collective-permute-start.8) | collective-permute-done | bytes 262176 | tf_op jit(solution)/shard_map/ppermute | solution.py:214
  121.7 6.4 %collective-permute-done.7.up_ref = bf16[256,512]{1,0:T(8,128)(2,1)S(1)} collective-permute-done((bf16[256,512]{1,0:T(8,128)(2,1)}, bf16[256,512]{1,0:T(8,128)(2,1)S(1)}, u32[]{:S(2)}, u32[]{:S(2)}) %collective-permute-start.7) | collective-permute-done | bytes 262176 | tf_op jit(solution)/shard_map/ppermute | solution.py:214
  128.2 0.1 shard_map.79
  128.2 4.8 %collective-permute-start.9 = (bf16[64,512]{1,0:T(8,128)(2,1)S(1)}, bf16[64,512]{1,0:T(8,128)(2,1)S(1)}, u32[]{:S(2)}, u32[]{:S(2)}) collective-permute-start(bf16[64,512]{1,0:T(8,128)(2,1)S(1)} %get-tuple-element.46), channel_id=1, source_target_pairs={{0,128},{32,160},{64,192},{96,224},{128,256},{160,288},{192,320},{... | collective-permute-start | bytes 196616 | tf_op jit(solution)/shard_map/ppermute | solution.py:214
  133.1 4.9 %collective-permute-start.11 = (bf16[64,512]{1,0:T(8,128)(2,1)S(1)}, bf16[64,512]{1,0:T(8,128)(2,1)S(1)}, u32[]{:S(2)}, u32[]{:S(2)}) collective-permute-start(bf16[64,512]{1,0:T(8,128)(2,1)S(1)} %get-tuple-element.47), channel_id=1, source_target_pairs={{0,384},{32,416},{64,448},{96,480},{128,0},{160,32},{192,64},{224,... | collective-permute-start | bytes 196616 | tf_op jit(solution)/shard_map/ppermute | solution.py:214
  138.0 2.4 %collective-permute-done.9 = bf16[64,512]{1,0:T(8,128)(2,1)S(1)} collective-permute-done((bf16[64,512]{1,0:T(8,128)(2,1)S(1)}, bf16[64,512]{1,0:T(8,128)(2,1)S(1)}, u32[]{:S(2)}, u32[]{:S(2)}) %collective-permute-start.9) | collective-permute-done | bytes 65568 | tf_op jit(solution)/shard_map/ppermute | solution.py:214
  140.5 4.5 %collective-permute-start.10 = (bf16[64,512]{1,0:T(8,128)(2,1)S(1)}, bf16[64,512]{1,0:T(8,128)(2,1)S(1)}, u32[]{:S(2)}, u32[]{:S(2)}) collective-permute-start(bf16[64,512]{1,0:T(8,128)(2,1)S(1)} %add_convert_fusion.1), channel_id=1, source_target_pairs={{0,128},{32,160},{64,192},{96,224},{128,256},{160,288},{192,320},{... | collective-permute-start | bytes 196616 | tf_op jit(solution)/shard_map/ppermute | solution.py:214
  145.0 7.1 %collective-permute-done.10 = bf16[64,512]{1,0:T(8,128)(2,1)S(1)} collective-permute-done((bf16[64,512]{1,0:T(8,128)(2,1)S(1)}, bf16[64,512]{1,0:T(8,128)(2,1)S(1)}, u32[]{:S(2)}, u32[]{:S(2)}) %collective-permute-start.10) | collective-permute-done | bytes 65568 | tf_op jit(solution)/shard_map/ppermute | solution.py:214
  152.1 1.3 fusion.16
  (11 shorter events, 0.0 us)
Async XLA Ops:
  0.6 79.6 %copy-start = (f32[512,512]{1,0:T(8,128)S(1)}, f32[512,512]{1,0:T(8,128)}, u32[]{:S(2)}) copy-start(f32[512,512]{1,0:T(8,128)} %param.7) | copy-start | bytes 3145732
  28.6 10.8 %collective-permute-start = (bf16[256,512]{1,0:T(8,128)(2,1)S(1)}, bf16[256,512]{1,0:T(8,128)(2,1)S(1)}, u32[]{:S(2)}, u32[]{:S(2)}) collective-permute-start(bf16[256,512]{1,0:T(8,128)(2,1)S(1)} %all_gather.3), channel_id=1, source_target_pairs={{0,480},{32,0},{64,32},{96,64},{128,96},{160,128},{192,160},{224,1... | collective-permute-start | bytes 786440 | tf_op jit(solution)/shard_map/ppermute | solution.py:214
  31.5 7.9 %collective-permute-start.1 = (s32[8,1152]{1,0:T(8,128)}, s32[8,1152]{1,0:T(8,128)S(1)}, u32[]{:S(2)}, u32[]{:S(2)}) collective-permute-start(s32[8,1152]{1,0:T(8,128)} %get-tuple-element.26), channel_id=1, source_target_pairs={{0,16},{16,0},{1,17},{17,1},{2,18},{18,2},{3,19},{19,3},{4,20},{20... | collective-permute-start | bytes 110600 | tf_op jit(solution)/shard_map/ppermute | solution.py:233
  36.4 11.1 %collective-permute-start.2 = (bf16[256,512]{1,0:T(8,128)(2,1)S(1)}, bf16[256,512]{1,0:T(8,128)(2,1)S(1)}, u32[]{:S(2)}, u32[]{:S(2)}) collective-permute-start(bf16[256,512]{1,0:T(8,128)(2,1)S(1)} %all_gather.3), channel_id=1, source_target_pairs={{0,32},{32,64},{64,96},{96,128},{128,160},{160,192},{192,224},{224... | collective-permute-start | bytes 786440 | tf_op jit(solution)/shard_map/ppermute | solution.py:214
  39.4 8.3 %collective-permute-start.3 = (bf16[256,512]{1,0:T(8,128)(2,1)S(1)}, bf16[256,512]{1,0:T(8,128)(2,1)S(1)}, u32[]{:S(2)}, u32[]{:S(2)}) collective-permute-start(bf16[256,512]{1,0:T(8,128)(2,1)S(1)} %collective-permute-done), channel_id=1, source_target_pairs={{0,480},{32,0},{64,32},{96,64},{128,96},{160,128},{192,160},{224,1... | collective-permute-start | bytes 786440 | tf_op jit(solution)/shard_map/ppermute | solution.py:214
  43.2 0.9 copy-start.1
  49.3 4.7 %collective-permute-start.4 = (f16[16,72,512]{2,1,0:T(8,128)(2,1)S(1)}, f16[16,72,512]{2,1,0:T(8,128)(2,1)S(1)}, u32[]{:S(2)}, u32[]{:S(2)}) collective-permute-start(f16[16,72,512]{2,1,0:T(8,128)(2,1)S(1)} %fusion.7), channel_id=1, source_target_pairs={{0,1},{1,0},{2,3},{3,2},{4,5},{5,4},{6,7},{7,6},{8,9},{9,8},{10,11... | collective-permute-start | bytes 3538952 | tf_op jit(solution)/shard_map/ppermute | solution.py:210
  54.4 25.8 %copy-start.2 = (f32[64,512]{1,0:T(8,128)S(1)}, f32[64,512]{1,0:T(8,128)}, u32[]{:S(2)}) copy-start(f32[64,512]{1,0:T(8,128)} %param.8) | copy-start | bytes 393220
  54.4 25.8 %copy-start.3 = (f32[64,512]{1,0:T(8,128)S(1)}, f32[64,512]{1,0:T(8,128)}, u32[]{:S(2)}) copy-start(f32[64,512]{1,0:T(8,128)} %features_ref.1) | copy-start | bytes 393220
  101.2 4.5 %collective-permute-start.5 = (bf16[1024,512]{1,0:T(8,128)(2,1)S(1)}, bf16[1024,512]{1,0:T(8,128)(2,1)S(1)}, u32[]{:S(2)}, u32[]{:S(2)}) collective-permute-start(bf16[1024,512]{1,0:T(8,128)(2,1)S(1)} %bitcast.21), channel_id=1, source_target_pairs={{0,1},{1,0},{2,3},{3,2},{4,5},{5,4},{6,7},{7,6},{8,9},{9,8},{10,11... | collective-permute-start | bytes 3145736 | tf_op jit(solution)/shard_map/ppermute | solution.py:210
  106.3 10.3 %collective-permute-start.6 = (bf16[256,512]{1,0:T(8,128)(2,1)S(1)}, bf16[256,512]{1,0:T(8,128)(2,1)S(1)}, u32[]{:S(2)}, u32[]{:S(2)}) collective-permute-start(bf16[256,512]{1,0:T(8,128)(2,1)S(1)} %add_convert_fusion), channel_id=1, source_target_pairs={{0,32},{32,64},{64,96},{96,128},{128,160},{160,192},{192,224},{224... | collective-permute-start | bytes 786440 | tf_op jit(solution)/shard_map/ppermute | solution.py:214
  111.0 10.7 %collective-permute-start.8 = (bf16[256,512]{1,0:T(8,128)(2,1)}, bf16[256,512]{1,0:T(8,128)(2,1)S(1)}, u32[]{:S(2)}, u32[]{:S(2)}) collective-permute-start(bf16[256,512]{1,0:T(8,128)(2,1)} %slice.58), channel_id=1, source_target_pairs={{0,480},{32,0},{64,32},{96,64},{128,96},{160,128},{192,160},{224,1... | collective-permute-start | bytes 786440 | tf_op jit(solution)/shard_map/ppermute | solution.py:214
  117.4 10.8 %collective-permute-start.7 = (bf16[256,512]{1,0:T(8,128)(2,1)}, bf16[256,512]{1,0:T(8,128)(2,1)S(1)}, u32[]{:S(2)}, u32[]{:S(2)}) collective-permute-start(bf16[256,512]{1,0:T(8,128)(2,1)} %fusion.8), channel_id=1, source_target_pairs={{0,32},{32,64},{64,96},{96,128},{128,160},{160,192},{192,224},{224... | collective-permute-start | bytes 786440 | tf_op jit(solution)/shard_map/ppermute | solution.py:214
  128.2 12.2 %collective-permute-start.9 = (bf16[64,512]{1,0:T(8,128)(2,1)S(1)}, bf16[64,512]{1,0:T(8,128)(2,1)S(1)}, u32[]{:S(2)}, u32[]{:S(2)}) collective-permute-start(bf16[64,512]{1,0:T(8,128)(2,1)S(1)} %get-tuple-element.46), channel_id=1, source_target_pairs={{0,128},{32,160},{64,192},{96,224},{128,256},{160,288},{192,320},{... | collective-permute-start | bytes 196616 | tf_op jit(solution)/shard_map/ppermute | solution.py:214
  133.1 11.9 %collective-permute-start.11 = (bf16[64,512]{1,0:T(8,128)(2,1)S(1)}, bf16[64,512]{1,0:T(8,128)(2,1)S(1)}, u32[]{:S(2)}, u32[]{:S(2)}) collective-permute-start(bf16[64,512]{1,0:T(8,128)(2,1)S(1)} %get-tuple-element.47), channel_id=1, source_target_pairs={{0,384},{32,416},{64,448},{96,480},{128,0},{160,32},{192,64},{224,... | collective-permute-start | bytes 196616 | tf_op jit(solution)/shard_map/ppermute | solution.py:214
  140.5 11.7 %collective-permute-start.10 = (bf16[64,512]{1,0:T(8,128)(2,1)S(1)}, bf16[64,512]{1,0:T(8,128)(2,1)S(1)}, u32[]{:S(2)}, u32[]{:S(2)}) collective-permute-start(bf16[64,512]{1,0:T(8,128)(2,1)S(1)} %add_convert_fusion.1), channel_id=1, source_target_pairs={{0,128},{32,160},{64,192},{96,224},{128,256},{160,288},{192,320},{... | collective-permute-start | bytes 196616 | tf_op jit(solution)/shard_map/ppermute | solution.py:214

commit v6 on v5

--- a/solution.py
+++ b/solution.py
@@ -267,7 +267,7 @@
     term += multiply_transposed(cross[:, : 3 * BLOCK], pulled_other)
     down = along_z(term[2 * BLOCK :].astype(jnp.bfloat16), -1)
     up = along_z((term[BLOCK : 2 * BLOCK] + passed.astype(jnp.float32)).astype(jnp.bfloat16), 1)
-    kept, ahead, opposite, behind = class_sums(lax.axis_index("zh"), term, up, down)
+    kept, ahead, opposite, behind = class_sums(lax.axis_index("zh"), term[:BLOCK], up, down)
     passed = along_z(opposite, N_Z_LO)
     down = along_z(behind, -N_Z_LO)
     up = along_z((ahead + passed.astype(jnp.float32)).astype(jnp.bfloat16), N_Z_LO)

time: 154 us -> 153 us (level)
  the two profiles are of different devices: /device:TPU:32 before, /device:TPU:8 now
where the time goes in v6:
time: 153 us; the launch traced here: 152 us
  blocking collectives  70.6 us (46%)
  starting transfers between devices  42.3 us (28%)
  waiting for transfers between devices  22.7 us (15%)
  matrix products  7.91 us (5%)
  Pallas kernels  5.31 us (3%)
  other arithmetic  1.59 us (1%)
    ppermute x9, starting transfers between devices, along_z(): return lax.ppermute(values, Z, [(z, (z + step) % N_Z) for z in range(N_Z)])  33.5 us
    all_gather x1, blocking collectives, per_device(): block = lax.all_gather(low, 'zh', axis=0, tiled=True)  27.1 us
    all_to_all x1, blocking collectives, per_device(): arrived = lax.all_to_all(sent, XY, 0, 0).astype(jnp.float32).sum(axis=0)  23.8 us
    all_to_all x1, blocking collectives, exchange(): return lax.all_to_all(values, axis, 0, 0, tiled=True)  19.7 us
    ppermute x9, waiting for transfers between devices, along_z(): return lax.ppermute(values, Z, [(z, (z + step) % N_Z) for z in range(N_Z)])  19.3 us
    ppermute x1, starting transfers between devices, per_device(): from_x = lax.ppermute(shared, 'xh', [(0, 1), (1, 0)])  4.93 us
    ppermute x2, starting transfers between devices, to_other_core(): return lax.ppermute(values, 'c', [(0, 1), (1, 0)])  3.83 us
    pallas_call x1, Pallas kernels, build_adjacency(): pl.pallas_call(adjacency_kernel, in_specs=[pl.BlockSpec(memory_space=pltp...  3.51 us
  transfers between devices with their start and end apart: 12, of which 8 were waited for; matrix products, arithmetic and copies ran while one was open for 3% of the time, Pallas kernels for 2%

profile of v6, /device:TPU:8, one launch (start us, length us, event | category | flops | bytes accessed | tf_op | source)
XLA Modules:
  0.0 152.5 jit_solution(6644948495802038830)
XLA Ops:
  0.6 0.0 copy-start
  0.6 1.7 %shard_map.77 = (bf16[64,512]{1,0:T(8,128)(2,1)}, s32[8,3200]{1,0:T(8,128)}, s32[8,1152]{1,0:T(8,128)}) custom-call(f32[64,512]{1,0:T(8,128)} %features_ref.1, s32[2,1024]{1,0:T(2,128)} %rows_ref.1, s32[2,2048]{1,0:T(2,128)} %columns_ref.1, s32[8,16]{1,0:T(8,128)} %mask_ref.1), custom_call_target="tpu_custom_call" | custom-call | tf_op jit(solution)/shard_map/pallas_call | solution.py:167
  2.4 27.1 %all_gather.3 = bf16[256,512]{1,0:T(8,128)(2,1)S(1)} all-gather(bf16[64,512]{1,0:T(8,128)(2,1)} %get-tuple-element.25), channel_id=1, replica_groups=mesh['zh'=4,'zl'=4,'xh'=2,'xl'=2,'y'=4,'c'=2] {'zh'}, dimensions={0}, use_global_device_ids=true | all-gather | bytes 327680 | tf_op jit(solution)/shard_map/all_gather | solution.py:234
  29.5 4.0 %collective-permute-start = (bf16[256,512]{1,0:T(8,128)(2,1)S(1)}, bf16[256,512]{1,0:T(8,128)(2,1)S(1)}, u32[]{:S(2)}, u32[]{:S(2)}) collective-permute-start(bf16[256,512]{1,0:T(8,128)(2,1)S(1)} %all_gather.3), channel_id=1, source_target_pairs={{0,480},{32,0},{64,32},{96,64},{128,96},{160,128},{192,160},{224,1... | collective-permute-start | bytes 786440 | tf_op jit(solution)/shard_map/ppermute | solution.py:214
  33.5 4.9 %collective-permute-start.1 = (s32[8,1152]{1,0:T(8,128)}, s32[8,1152]{1,0:T(8,128)S(1)}, u32[]{:S(2)}, u32[]{:S(2)}) collective-permute-start(s32[8,1152]{1,0:T(8,128)} %get-tuple-element.26), channel_id=1, source_target_pairs={{0,16},{16,0},{1,17},{17,1},{2,18},{18,2},{3,19},{19,3},{4,20},{20... | collective-permute-start | bytes 110600 | tf_op jit(solution)/shard_map/ppermute | solution.py:233
  38.4 1.9 %collective-permute-start.2 = (bf16[256,512]{1,0:T(8,128)(2,1)S(1)}, bf16[256,512]{1,0:T(8,128)(2,1)S(1)}, u32[]{:S(2)}, u32[]{:S(2)}) collective-permute-start(bf16[256,512]{1,0:T(8,128)(2,1)S(1)} %all_gather.3), channel_id=1, source_target_pairs={{0,32},{32,64},{64,96},{96,128},{128,160},{160,192},{192,224},{224... | collective-permute-start | bytes 786440 | tf_op jit(solution)/shard_map/ppermute | solution.py:214
  40.3 0.7 collective-permute-done.1.from_x_ref
  41.0 4.5 %collective-permute-start.3 = (bf16[256,512]{1,0:T(8,128)(2,1)S(1)}, bf16[256,512]{1,0:T(8,128)(2,1)S(1)}, u32[]{:S(2)}, u32[]{:S(2)}) collective-permute-start(bf16[256,512]{1,0:T(8,128)(2,1)S(1)} %collective-permute-done), channel_id=1, source_target_pairs={{0,480},{32,0},{64,32},{96,64},{128,96},{160,128},{192,160},{224,1... | collective-permute-start | bytes 786440 | tf_op jit(solution)/shard_map/ppermute | solution.py:214
  45.5 0.1 pad_add_fusion.place_ref
  45.6 0.9 copy-done.1
  46.5 3.5 %shard_map.78 = (bf16[1024,1024]{1,0:T(8,128)(2,1)S(1)}, bf16[1024,1024]{1,0:T(8,128)(2,1)S(1)}, f32[16,8,128]{2,1,0:T(8,128)S(1)}, f32[16,8,128]{2,1,0:T(8,128)S(1)}) custom-call(s32[4]{0:T(128)S(1)} %pad_add_fusion.place_ref, s32[8,3200]{1,0:T(8,128)S(1)} %copy-done.1, s32[8,1152]{1,0:T(8,128)S(1)} %collective-permute-done.1.from_x_ref), custom_call_target="tpu_custom_call" | custom-call | flops 67108864 | bytes 4194304 | tf_op jit(solution)/shard_map/pallas_call | solution.py:132
  50.0 0.1 pad_maximum_fusion
  50.1 1.3 convolution_convert_fusion
  51.4 0.3 fusion.7
  51.7 1.9 %collective-permute-start.4 = (f16[16,72,512]{2,1,0:T(8,128)(2,1)S(1)}, f16[16,72,512]{2,1,0:T(8,128)(2,1)S(1)}, u32[]{:S(2)}, u32[]{:S(2)}) collective-permute-start(f16[16,72,512]{2,1,0:T(8,128)(2,1)S(1)} %fusion.7), channel_id=1, source_target_pairs={{0,1},{1,0},{2,3},{3,2},{4,5},{5,4},{6,7},{7,6},{8,9},{9,8},{10,11... | collective-permute-start | bytes 3538952 | tf_op jit(solution)/shard_map/ppermute | solution.py:210
  53.6 1.3 fusion.26
  54.8 1.6 %collective-permute-done.4 = f16[16,72,512]{2,1,0:T(8,128)(2,1)S(1)} collective-permute-done((f16[16,72,512]{2,1,0:T(8,128)(2,1)S(1)}, f16[16,72,512]{2,1,0:T(8,128)(2,1)S(1)}, u32[]{:S(2)}, u32[]{:S(2)}) %collective-permute-start.4) | collective-permute-done | bytes 1179680 | tf_op jit(solution)/shard_map/ppermute | solution.py:210
  56.4 0.4 fusion.1
  56.8 0.0 copy-start.2
  56.8 0.0 copy-start.3
  56.8 23.8 %all_to_all.14 = f16[16,72,512]{2,1,0:T(8,128)(2,1)S(1)} all-to-all(f16[16,72,512]{2,1,0:T(8,128)(2,1)S(1)} %fusion.1), channel_id=1, replica_groups=mesh['zh'=4,'zl'=4,'xh'=2,'xl'=2,'y'=4,'c'=2] {'xh','xl','y'}, dimensions={0} | all-to-all | bytes 2359296 | tf_op jit(solution)/shard_map/all_to_all | solution.py:251
  80.6 0.2 convert_reduce_fusion
  80.8 1.2 fusion.25
  82.0 0.1 broadcast_in_dim.2
  82.1 19.7 %all_to_all.15 = bf16[16,64,512]{2,1,0:T(8,128)(2,1)S(1)} all-to-all(bf16[16,64,512]{2,1,0:T(8,128)(2,1)S(1)} %broadcast_in_dim.2), channel_id=1, replica_groups=mesh['zh'=4,'zl'=4,'xh'=2,'xl'=2,'y'=4,'c'=2] {'xh','xl','y'}, dimensions={0} | all-to-all | bytes 2097152 | tf_op jit(solution)/shard_map/all_to_all | solution.py:218
  101.8 1.9 %collective-permute-start.5 = (bf16[1024,512]{1,0:T(8,128)(2,1)S(1)}, bf16[1024,512]{1,0:T(8,128)(2,1)S(1)}, u32[]{:S(2)}, u32[]{:S(2)}) collective-permute-start(bf16[1024,512]{1,0:T(8,128)(2,1)S(1)} %bitcast.21), channel_id=1, source_target_pairs={{0,1},{1,0},{2,3},{3,2},{4,5},{5,4},{6,7},{7,6},{8,9},{9,8},{10,11... | collective-permute-start | bytes 3145736 | tf_op jit(solution)/shard_map/ppermute | solution.py:210
  103.8 0.5 fusion.11
  104.2 1.0 fusion.5
  105.2 1.1 collective-permute-done.5
  106.4 0.5 fusion.9
  106.9 0.1 add_convert_fusion
  107.0 2.1 %collective-permute-start.6 = (bf16[256,512]{1,0:T(8,128)(2,1)S(1)}, bf16[256,512]{1,0:T(8,128)(2,1)S(1)}, u32[]{:S(2)}, u32[]{:S(2)}) collective-permute-start(bf16[256,512]{1,0:T(8,128)(2,1)S(1)} %add_convert_fusion), channel_id=1, source_target_pairs={{0,32},{32,64},{64,96},{96,128},{128,160},{160,192},{192,224},{224... | collective-permute-start | bytes 786440 | tf_op jit(solution)/shard_map/ppermute | solution.py:214
  109.1 1.0 fusion.3
  110.1 0.3 add.66
  110.5 4.9 %collective-permute-start.8 = (bf16[256,512]{1,0:T(8,128)(2,1)S(1)}, bf16[256,512]{1,0:T(8,128)(2,1)S(1)}, u32[]{:S(2)}, u32[]{:S(2)}) collective-permute-start(bf16[256,512]{1,0:T(8,128)(2,1)S(1)} %slice.63), channel_id=1, source_target_pairs={{0,480},{32,0},{64,32},{96,64},{128,96},{160,128},{192,160},{224,1... | collective-permute-start | bytes 786440 | tf_op jit(solution)/shard_map/ppermute | solution.py:214
  115.4 3.0 %collective-permute-done.6 = bf16[256,512]{1,0:T(8,128)(2,1)S(1)} collective-permute-done((bf16[256,512]{1,0:T(8,128)(2,1)S(1)}, bf16[256,512]{1,0:T(8,128)(2,1)S(1)}, u32[]{:S(2)}, u32[]{:S(2)}) %collective-permute-start.6) | collective-permute-done | bytes 262176 | tf_op jit(solution)/shard_map/ppermute | solution.py:214
  118.4 0.1 fusion.8
  118.5 1.9 %collective-permute-start.7 = (bf16[256,512]{1,0:T(8,128)(2,1)S(1)}, bf16[256,512]{1,0:T(8,128)(2,1)S(1)}, u32[]{:S(2)}, u32[]{:S(2)}) collective-permute-start(bf16[256,512]{1,0:T(8,128)(2,1)S(1)} %get-tuple-element.48), channel_id=1, source_target_pairs={{0,32},{32,64},{64,96},{96,128},{128,160},{160,192},{192,224},{224... | collective-permute-start | bytes 786440 | tf_op jit(solution)/shard_map/ppermute | solution.py:214
  120.5 0.5 collective-permute-done.8.down_ref
  121.0 8.2 %collective-permute-done.7.up_ref = bf16[256,512]{1,0:T(8,128)(2,1)S(1)} collective-permute-done((bf16[256,512]{1,0:T(8,128)(2,1)S(1)}, bf16[256,512]{1,0:T(8,128)(2,1)S(1)}, u32[]{:S(2)}, u32[]{:S(2)}) %collective-permute-start.7) | collective-permute-done | bytes 262176 | tf_op jit(solution)/shard_map/ppermute | solution.py:214
  129.2 0.1 shard_map.79
  129.2 4.8 %collective-permute-start.9 = (bf16[64,512]{1,0:T(8,128)(2,1)S(1)}, bf16[64,512]{1,0:T(8,128)(2,1)S(1)}, u32[]{:S(2)}, u32[]{:S(2)}) collective-permute-start(bf16[64,512]{1,0:T(8,128)(2,1)S(1)} %get-tuple-element.46), channel_id=1, source_target_pairs={{0,128},{32,160},{64,192},{96,224},{128,256},{160,288},{192,320},{... | collective-permute-start | bytes 196616 | tf_op jit(solution)/shard_map/ppermute | solution.py:214
  134.1 4.9 %collective-permute-start.11 = (bf16[64,512]{1,0:T(8,128)(2,1)S(1)}, bf16[64,512]{1,0:T(8,128)(2,1)S(1)}, u32[]{:S(2)}, u32[]{:S(2)}) collective-permute-start(bf16[64,512]{1,0:T(8,128)(2,1)S(1)} %get-tuple-element.47), channel_id=1, source_target_pairs={{0,384},{32,416},{64,448},{96,480},{128,0},{160,32},{192,64},{224,... | collective-permute-start | bytes 196616 | tf_op jit(solution)/shard_map/ppermute | solution.py:214
  139.0 1.2 collective-permute-done.9
  140.2 4.5 %collective-permute-start.10 = (bf16[64,512]{1,0:T(8,128)(2,1)S(1)}, bf16[64,512]{1,0:T(8,128)(2,1)S(1)}, u32[]{:S(2)}, u32[]{:S(2)}) collective-permute-start(bf16[64,512]{1,0:T(8,128)(2,1)S(1)} %add_convert_fusion.1), channel_id=1, source_target_pairs={{0,128},{32,160},{64,192},{96,224},{128,256},{160,288},{192,320},{... | collective-permute-start | bytes 196616 | tf_op jit(solution)/shard_map/ppermute | solution.py:214
  144.7 0.0 collective-permute-done.11
  144.7 6.5 %collective-permute-done.10 = bf16[64,512]{1,0:T(8,128)(2,1)S(1)} collective-permute-done((bf16[64,512]{1,0:T(8,128)(2,1)S(1)}, bf16[64,512]{1,0:T(8,128)(2,1)S(1)}, u32[]{:S(2)}, u32[]{:S(2)}) %collective-permute-start.10) | collective-permute-done | bytes 65568 | tf_op jit(solution)/shard_map/ppermute | solution.py:214
  151.2 1.3 fusion.16
  (11 shorter events, 0.1 us)
Async XLA Ops:
  0.6 80.2 %copy-start = (f32[512,512]{1,0:T(8,128)S(1)}, f32[512,512]{1,0:T(8,128)}, u32[]{:S(2)}) copy-start(f32[512,512]{1,0:T(8,128)} %param.7) | copy-start | bytes 3145732
  29.5 11.5 %collective-permute-start = (bf16[256,512]{1,0:T(8,128)(2,1)S(1)}, bf16[256,512]{1,0:T(8,128)(2,1)S(1)}, u32[]{:S(2)}, u32[]{:S(2)}) collective-permute-start(bf16[256,512]{1,0:T(8,128)(2,1)S(1)} %all_gather.3), channel_id=1, source_target_pairs={{0,480},{32,0},{64,32},{96,64},{128,96},{160,128},{192,160},{224,1... | collective-permute-start | bytes 786440 | tf_op jit(solution)/shard_map/ppermute | solution.py:214
  33.5 7.6 %collective-permute-start.1 = (s32[8,1152]{1,0:T(8,128)}, s32[8,1152]{1,0:T(8,128)S(1)}, u32[]{:S(2)}, u32[]{:S(2)}) collective-permute-start(s32[8,1152]{1,0:T(8,128)} %get-tuple-element.26), channel_id=1, source_target_pairs={{0,16},{16,0},{1,17},{17,1},{2,18},{18,2},{3,19},{19,3},{4,20},{20... | collective-permute-start | bytes 110600 | tf_op jit(solution)/shard_map/ppermute | solution.py:233
  38.4 11.6 %collective-permute-start.2 = (bf16[256,512]{1,0:T(8,128)(2,1)S(1)}, bf16[256,512]{1,0:T(8,128)(2,1)S(1)}, u32[]{:S(2)}, u32[]{:S(2)}) collective-permute-start(bf16[256,512]{1,0:T(8,128)(2,1)S(1)} %all_gather.3), channel_id=1, source_target_pairs={{0,32},{32,64},{64,96},{96,128},{128,160},{160,192},{192,224},{224... | collective-permute-start | bytes 786440 | tf_op jit(solution)/shard_map/ppermute | solution.py:214
  41.0 9.0 %collective-permute-start.3 = (bf16[256,512]{1,0:T(8,128)(2,1)S(1)}, bf16[256,512]{1,0:T(8,128)(2,1)S(1)}, u32[]{:S(2)}, u32[]{:S(2)}) collective-permute-start(bf16[256,512]{1,0:T(8,128)(2,1)S(1)} %collective-permute-done), channel_id=1, source_target_pairs={{0,480},{32,0},{64,32},{96,64},{128,96},{160,128},{192,160},{224,1... | collective-permute-start | bytes 786440 | tf_op jit(solution)/shard_map/ppermute | solution.py:214
  45.6 0.9 copy-start.1
  51.7 4.7 %collective-permute-start.4 = (f16[16,72,512]{2,1,0:T(8,128)(2,1)S(1)}, f16[16,72,512]{2,1,0:T(8,128)(2,1)S(1)}, u32[]{:S(2)}, u32[]{:S(2)}) collective-permute-start(f16[16,72,512]{2,1,0:T(8,128)(2,1)S(1)} %fusion.7), channel_id=1, source_target_pairs={{0,1},{1,0},{2,3},{3,2},{4,5},{5,4},{6,7},{7,6},{8,9},{9,8},{10,11... | collective-permute-start | bytes 3538952 | tf_op jit(solution)/shard_map/ppermute | solution.py:210
  56.8 24.0 %copy-start.2 = (f32[64,512]{1,0:T(8,128)S(1)}, f32[64,512]{1,0:T(8,128)}, u32[]{:S(2)}) copy-start(f32[64,512]{1,0:T(8,128)} %param.8) | copy-start | bytes 393220
  56.8 24.0 %copy-start.3 = (f32[64,512]{1,0:T(8,128)S(1)}, f32[64,512]{1,0:T(8,128)}, u32[]{:S(2)}) copy-start(f32[64,512]{1,0:T(8,128)} %features_ref.1) | copy-start | bytes 393220
  101.8 4.5 %collective-permute-start.5 = (bf16[1024,512]{1,0:T(8,128)(2,1)S(1)}, bf16[1024,512]{1,0:T(8,128)(2,1)S(1)}, u32[]{:S(2)}, u32[]{:S(2)}) collective-permute-start(bf16[1024,512]{1,0:T(8,128)(2,1)S(1)} %bitcast.21), channel_id=1, source_target_pairs={{0,1},{1,0},{2,3},{3,2},{4,5},{5,4},{6,7},{7,6},{8,9},{9,8},{10,11... | collective-permute-start | bytes 3145736 | tf_op jit(solution)/shard_map/ppermute | solution.py:210
  107.0 11.5 %collective-permute-start.6 = (bf16[256,512]{1,0:T(8,128)(2,1)S(1)}, bf16[256,512]{1,0:T(8,128)(2,1)S(1)}, u32[]{:S(2)}, u32[]{:S(2)}) collective-permute-start(bf16[256,512]{1,0:T(8,128)(2,1)S(1)} %add_convert_fusion), channel_id=1, source_target_pairs={{0,32},{32,64},{64,96},{96,128},{128,160},{160,192},{192,224},{224... | collective-permute-start | bytes 786440 | tf_op jit(solution)/shard_map/ppermute | solution.py:214
  110.5 10.5 %collective-permute-start.8 = (bf16[256,512]{1,0:T(8,128)(2,1)S(1)}, bf16[256,512]{1,0:T(8,128)(2,1)S(1)}, u32[]{:S(2)}, u32[]{:S(2)}) collective-permute-start(bf16[256,512]{1,0:T(8,128)(2,1)S(1)} %slice.63), channel_id=1, source_target_pairs={{0,480},{32,0},{64,32},{96,64},{128,96},{160,128},{192,160},{224,1... | collective-permute-start | bytes 786440 | tf_op jit(solution)/shard_map/ppermute | solution.py:214
  118.5 10.6 %collective-permute-start.7 = (bf16[256,512]{1,0:T(8,128)(2,1)S(1)}, bf16[256,512]{1,0:T(8,128)(2,1)S(1)}, u32[]{:S(2)}, u32[]{:S(2)}) collective-permute-start(bf16[256,512]{1,0:T(8,128)(2,1)S(1)} %get-tuple-element.48), channel_id=1, source_target_pairs={{0,32},{32,64},{64,96},{96,128},{128,160},{160,192},{192,224},{224... | collective-permute-start | bytes 786440 | tf_op jit(solution)/shard_map/ppermute | solution.py:214
  129.2 11.0 %collective-permute-start.9 = (bf16[64,512]{1,0:T(8,128)(2,1)S(1)}, bf16[64,512]{1,0:T(8,128)(2,1)S(1)}, u32[]{:S(2)}, u32[]{:S(2)}) collective-permute-start(bf16[64,512]{1,0:T(8,128)(2,1)S(1)} %get-tuple-element.46), channel_id=1, source_target_pairs={{0,128},{32,160},{64,192},{96,224},{128,256},{160,288},{192,320},{... | collective-permute-start | bytes 196616 | tf_op jit(solution)/shard_map/ppermute | solution.py:214
  134.1 10.7 %collective-permute-start.11 = (bf16[64,512]{1,0:T(8,128)(2,1)S(1)}, bf16[64,512]{1,0:T(8,128)(2,1)S(1)}, u32[]{:S(2)}, u32[]{:S(2)}) collective-permute-start(bf16[64,512]{1,0:T(8,128)(2,1)S(1)} %get-tuple-element.47), channel_id=1, source_target_pairs={{0,384},{32,416},{64,448},{96,480},{128,0},{160,32},{192,64},{224,... | collective-permute-start | bytes 196616 | tf_op jit(solution)/shard_map/ppermute | solution.py:214
  140.2 11.0 %collective-permute-start.10 = (bf16[64,512]{1,0:T(8,128)(2,1)S(1)}, bf16[64,512]{1,0:T(8,128)(2,1)S(1)}, u32[]{:S(2)}, u32[]{:S(2)}) collective-permute-start(bf16[64,512]{1,0:T(8,128)(2,1)S(1)} %add_convert_fusion.1), channel_id=1, source_target_pairs={{0,128},{32,160},{64,192},{96,224},{128,256},{160,288},{192,320},{... | collective-permute-start | bytes 196616 | tf_op jit(solution)/shard_map/ppermute | solution.py:214

commit v7 on v6

--- a/solution.py
+++ b/solution.py
@@ -79,9 +79,9 @@
                 pieces = []
                 for k in range(2):
                     at = pl.ds(256 * t + 128 * k, 128)
-                    pieces.append(jnp.where(x_hi == x, codes_ref[:2, at], from_x_ref[:2, at]))
+                    pieces.append(jnp.where(x_hi == x, codes_ref[:2, at], from_x_ref[:2, at].astype(jnp.float32)))
                 picked_ref[:, pl.ds(R // N_X_HI * x + 128 * t, 128)] = halves(*pieces, core ^ crossed)
-        rows = picked_ref[...].astype(jnp.float32)
+        rows = picked_ref[...]
         left_ref[crossed] = stack_rows(row_digits(rows[:1], rows[1:]), R)
 
     groups = (N_Z, HALF)
@@ -97,11 +97,11 @@
                 at = R + ((2 * h + k) * N_Z_LO + class_of(jnp.int32(place), z_lo)) * 128
                 pieces.append(codes_ref[:2, pl.ds(pl.multiple_of(at, 128), 128)])
             picked_ref[:, pl.ds(BLOCK * place + 128 * h, 128)] = halves(*pieces, x_hi)
-    columns = picked_ref[...].astype(jnp.float32)
+    columns = picked_ref[...]
     right = stack_rows(column_digits(columns[:1], columns[1:]), HALF)
-    masks = (codes_ref[:, R + COLS : R + COLS + N_Z], from_x_ref[:, R : R + N_Z])
+    masks = (codes_ref[:, R + COLS : R + COLS + N_Z], from_x_ref[:, R : R + N_Z].astype(jnp.float32))
     mask = jnp.concatenate([jnp.where(x_hi == x, *masks) for x in range(N_X_HI)], axis=0)
-    mask = mask.astype(jnp.float32).astype(jnp.bfloat16)
+    mask = mask.astype(jnp.bfloat16)
     limit = jnp.dot(mask, spread, preferred_element_type=jnp.float32) * place_ref[3].astype(jnp.float32)
 
     for crossed, (block_ref, degree_ref) in enumerate(((own_ref, own_degree_ref), (cross_ref, cross_degree_ref))):
@@ -134,7 +134,7 @@
         in_specs=[pl.BlockSpec(memory_space=pltpu.SMEM), vmem, vmem],
         out_specs=[vmem] * 4,
         out_shape=[block, block, degree, degree],
-        scratch_shapes=[pltpu.VMEM((2, R), jnp.int32), pltpu.VMEM((2, DIGITS, R), jnp.bfloat16)],
+        scratch_shapes=[pltpu.VMEM((2, R), jnp.float32), pltpu.VMEM((2, DIGITS, R), jnp.bfloat16)],
         compiler_params=pltpu.CompilerParams(vmem_limit_bytes=6 * 1024 * 1024),
         cost_estimate=pl.CostEstimate(flops=4 * R * HALF * 16, bytes_accessed=4 * R * HALF, transcendentals=0),
     )(place, codes, from_x)
@@ -233,7 +233,7 @@
     from_x = lax.ppermute(shared, "xh", [(0, 1), (1, 0)])
     block = lax.all_gather(low, "zh", axis=0, tiled=True)
     up, down = along_z(block, -1), along_z(block, 1)
-    up, from_x = lax.optimization_barrier((up, from_x))
+    up, from_x, codes = lax.optimization_barrier((up, from_x, codes.astype(jnp.float32)))
     far = along_z(up, -1)
     own, cross, own_degree, cross_degree = build_adjacency(place, codes, from_x)
     gathered = jnp.concatenate([block, up, down, far], axis=0)

time: 153 us -> 154 us (level)
  no operation moved by 1% of the time
where the time goes in v7:
time: 154 us; the launch traced here: 153 us
  blocking collectives  70.4 us (46%)
  starting transfers between devices  43.2 us (28%)
  waiting for transfers between devices  22.7 us (15%)
  matrix products  7.9 us (5%)
  Pallas kernels  5.32 us (3%)
  other arithmetic  2.49 us (2%)
    ppermute x9, starting transfers between devices, along_z(): return lax.ppermute(values, Z, [(z, (z + step) % N_Z) for z in range(N_Z)])  34.4 us
    all_gather x1, blocking collectives, per_device(): block = lax.all_gather(low, 'zh', axis=0, tiled=True)  27.1 us
    all_to_all x1, blocking collectives, per_device(): arrived = lax.all_to_all(sent, XY, 0, 0).astype(jnp.float32).sum(axis=0)  23.6 us
    ppermute x9, waiting for transfers between devices, along_z(): return lax.ppermute(values, Z, [(z, (z + step) % N_Z) for z in range(N_Z)])  20 us
    all_to_all x1, blocking collectives, exchange(): return lax.all_to_all(values, axis, 0, 0, tiled=True)  19.7 us
    ppermute x1, starting transfers between devices, per_device(): from_x = lax.ppermute(shared, 'xh', [(0, 1), (1, 0)])  4.93 us
    ppermute x2, starting transfers between devices, to_other_core(): return lax.ppermute(values, 'c', [(0, 1), (1, 0)])  3.83 us
    pallas_call x1, Pallas kernels, build_adjacency(): pl.pallas_call(adjacency_kernel, in_specs=[pl.BlockSpec(memory_space=pltp...  3.52 us
  transfers between devices with their start and end apart: 12, of which 8 were waited for; matrix products, arithmetic and copies ran while one was open for 3% of the time, Pallas kernels for 2%

profile of v7, /device:TPU:8, one launch (start us, length us, event | category | flops | bytes accessed | tf_op | source)
XLA Modules:
  0.0 153.1 jit_solution(8970727268074868167)
XLA Ops:
  0.6 0.0 copy-start
  0.6 1.7 %shard_map.77 = (bf16[64,512]{1,0:T(8,128)(2,1)}, s32[8,3200]{1,0:T(8,128)}, s32[8,1152]{1,0:T(8,128)}) custom-call(f32[64,512]{1,0:T(8,128)} %features_ref.1, s32[2,1024]{1,0:T(2,128)} %rows_ref.1, s32[2,2048]{1,0:T(2,128)} %columns_ref.1, s32[8,16]{1,0:T(8,128)} %mask_ref.1), custom_call_target="tpu_custom_call" | custom-call | tf_op jit(solution)/shard_map/pallas_call | solution.py:167
  2.4 27.1 %all_gather.3 = bf16[256,512]{1,0:T(8,128)(2,1)S(1)} all-gather(bf16[64,512]{1,0:T(8,128)(2,1)} %get-tuple-element.26), channel_id=1, replica_groups=mesh['zh'=4,'zl'=4,'xh'=2,'xl'=2,'y'=4,'c'=2] {'zh'}, dimensions={0}, use_global_device_ids=true | all-gather | bytes 327680 | tf_op jit(solution)/shard_map/all_gather | solution.py:234
  29.5 4.0 %collective-permute-start = (bf16[256,512]{1,0:T(8,128)(2,1)S(1)}, bf16[256,512]{1,0:T(8,128)(2,1)S(1)}, u32[]{:S(2)}, u32[]{:S(2)}) collective-permute-start(bf16[256,512]{1,0:T(8,128)(2,1)S(1)} %all_gather.3), channel_id=1, source_target_pairs={{0,480},{32,0},{64,32},{96,64},{128,96},{160,128},{192,160},{224,1... | collective-permute-start | bytes 786440 | tf_op jit(solution)/shard_map/ppermute | solution.py:214
  33.5 4.9 %collective-permute-start.1 = (s32[8,1152]{1,0:T(8,128)}, s32[8,1152]{1,0:T(8,128)S(1)}, u32[]{:S(2)}, u32[]{:S(2)}) collective-permute-start(s32[8,1152]{1,0:T(8,128)} %get-tuple-element.27), channel_id=1, source_target_pairs={{0,16},{16,0},{1,17},{17,1},{2,18},{18,2},{3,19},{19,3},{4,20},{20... | collective-permute-start | bytes 110600 | tf_op jit(solution)/shard_map/ppermute | solution.py:233
  38.4 1.9 %collective-permute-start.2 = (bf16[256,512]{1,0:T(8,128)(2,1)S(1)}, bf16[256,512]{1,0:T(8,128)(2,1)S(1)}, u32[]{:S(2)}, u32[]{:S(2)}) collective-permute-start(bf16[256,512]{1,0:T(8,128)(2,1)S(1)} %all_gather.3), channel_id=1, source_target_pairs={{0,32},{32,64},{64,96},{96,128},{128,160},{160,192},{192,224},{224... | collective-permute-start | bytes 786440 | tf_op jit(solution)/shard_map/ppermute | solution.py:214
  40.3 0.9 convert_element_type.41.codes_ref
  41.2 0.0 collective-permute-done.1.from_x_ref
  41.2 5.1 %collective-permute-start.3 = (bf16[256,512]{1,0:T(8,128)(2,1)S(1)}, bf16[256,512]{1,0:T(8,128)(2,1)S(1)}, u32[]{:S(2)}, u32[]{:S(2)}) collective-permute-start(bf16[256,512]{1,0:T(8,128)(2,1)S(1)} %collective-permute-done), channel_id=1, source_target_pairs={{0,480},{32,0},{64,32},{96,64},{128,96},{160,128},{192,160},{224,1... | collective-permute-start | bytes 786440 | tf_op jit(solution)/shard_map/ppermute | solution.py:214
  46.4 0.1 pad_add_fusion.place_ref
  46.5 3.5 %shard_map.78 = (bf16[1024,1024]{1,0:T(8,128)(2,1)S(1)}, bf16[1024,1024]{1,0:T(8,128)(2,1)S(1)}, f32[16,8,128]{2,1,0:T(8,128)S(1)}, f32[16,8,128]{2,1,0:T(8,128)S(1)}) custom-call(s32[4]{0:T(128)S(1)} %pad_add_fusion.place_ref, f32[8,3200]{1,0:T(8,128)S(1)} %convert_element_type.41.codes_ref, s32[8,1152]{1,0:T(8,128)S(1)} %collective-permute-done.1.from_x_ref), custom_call_target="tpu_custom_call" | custom-call | flops 67108864 | bytes 4194304 | tf_op jit(solution)/shard_map/pallas_call | solution.py:132
  50.0 0.2 collective-permute-done.3
  50.3 0.1 pad_maximum_fusion
  50.3 1.2 convolution_convert_fusion
  51.6 0.3 fusion.7
  51.9 1.9 %collective-permute-start.4 = (f16[16,72,512]{2,1,0:T(8,128)(2,1)S(1)}, f16[16,72,512]{2,1,0:T(8,128)(2,1)S(1)}, u32[]{:S(2)}, u32[]{:S(2)}) collective-permute-start(f16[16,72,512]{2,1,0:T(8,128)(2,1)S(1)} %fusion.7), channel_id=1, source_target_pairs={{0,1},{1,0},{2,3},{3,2},{4,5},{5,4},{6,7},{7,6},{8,9},{9,8},{10,11... | collective-permute-start | bytes 3538952 | tf_op jit(solution)/shard_map/ppermute | solution.py:210
  53.8 1.2 fusion.26
  55.0 1.6 %collective-permute-done.4 = f16[16,72,512]{2,1,0:T(8,128)(2,1)S(1)} collective-permute-done((f16[16,72,512]{2,1,0:T(8,128)(2,1)S(1)}, f16[16,72,512]{2,1,0:T(8,128)(2,1)S(1)}, u32[]{:S(2)}, u32[]{:S(2)}) %collective-permute-start.4) | collective-permute-done | bytes 1179680 | tf_op jit(solution)/shard_map/ppermute | solution.py:210
  56.6 0.4 fusion.1
  57.0 0.0 copy-start.1
  57.0 0.0 copy-start.2
  57.0 23.6 %all_to_all.14 = f16[16,72,512]{2,1,0:T(8,128)(2,1)S(1)} all-to-all(f16[16,72,512]{2,1,0:T(8,128)(2,1)S(1)} %fusion.1), channel_id=1, replica_groups=mesh['zh'=4,'zl'=4,'xh'=2,'xl'=2,'y'=4,'c'=2] {'xh','xl','y'}, dimensions={0} | all-to-all | bytes 2359296 | tf_op jit(solution)/shard_map/all_to_all | solution.py:251
  80.6 0.2 convert_reduce_fusion
  80.8 1.2 fusion.25
  82.0 0.1 broadcast_in_dim.2
  82.1 19.7 %all_to_all.15 = bf16[16,64,512]{2,1,0:T(8,128)(2,1)S(1)} all-to-all(bf16[16,64,512]{2,1,0:T(8,128)(2,1)S(1)} %broadcast_in_dim.2), channel_id=1, replica_groups=mesh['zh'=4,'zl'=4,'xh'=2,'xl'=2,'y'=4,'c'=2] {'xh','xl','y'}, dimensions={0} | all-to-all | bytes 2097152 | tf_op jit(solution)/shard_map/all_to_all | solution.py:218
  101.8 1.9 %collective-permute-start.5 = (bf16[1024,512]{1,0:T(8,128)(2,1)S(1)}, bf16[1024,512]{1,0:T(8,128)(2,1)S(1)}, u32[]{:S(2)}, u32[]{:S(2)}) collective-permute-start(bf16[1024,512]{1,0:T(8,128)(2,1)S(1)} %bitcast.21), channel_id=1, source_target_pairs={{0,1},{1,0},{2,3},{3,2},{4,5},{5,4},{6,7},{7,6},{8,9},{9,8},{10,11... | collective-permute-start | bytes 3145736 | tf_op jit(solution)/shard_map/ppermute | solution.py:210
  103.8 0.5 fusion.11
  104.2 1.0 fusion.5
  105.2 1.1 collective-permute-done.5
  106.4 0.5 fusion.9
  106.9 0.1 add_convert_fusion
  107.0 1.9 %collective-permute-start.6 = (bf16[256,512]{1,0:T(8,128)(2,1)S(1)}, bf16[256,512]{1,0:T(8,128)(2,1)S(1)}, u32[]{:S(2)}, u32[]{:S(2)}) collective-permute-start(bf16[256,512]{1,0:T(8,128)(2,1)S(1)} %add_convert_fusion), channel_id=1, source_target_pairs={{0,32},{32,64},{64,96},{96,128},{128,160},{160,192},{192,224},{224... | collective-permute-start | bytes 786440 | tf_op jit(solution)/shard_map/ppermute | solution.py:214
  108.9 1.0 fusion.3
  109.9 0.3 add.66
  110.3 5.1 %collective-permute-start.8 = (bf16[256,512]{1,0:T(8,128)(2,1)S(1)}, bf16[256,512]{1,0:T(8,128)(2,1)S(1)}, u32[]{:S(2)}, u32[]{:S(2)}) collective-permute-start(bf16[256,512]{1,0:T(8,128)(2,1)S(1)} %slice.63), channel_id=1, source_target_pairs={{0,480},{32,0},{64,32},{96,64},{128,96},{160,128},{192,160},{224,1... | collective-permute-start | bytes 786440 | tf_op jit(solution)/shard_map/ppermute | solution.py:214
  115.4 3.0 %collective-permute-done.6 = bf16[256,512]{1,0:T(8,128)(2,1)S(1)} collective-permute-done((bf16[256,512]{1,0:T(8,128)(2,1)S(1)}, bf16[256,512]{1,0:T(8,128)(2,1)S(1)}, u32[]{:S(2)}, u32[]{:S(2)}) %collective-permute-start.6) | collective-permute-done | bytes 262176 | tf_op jit(solution)/shard_map/ppermute | solution.py:214
  118.4 0.1 fusion.8
  118.5 1.9 %collective-permute-start.7 = (bf16[256,512]{1,0:T(8,128)(2,1)S(1)}, bf16[256,512]{1,0:T(8,128)(2,1)S(1)}, u32[]{:S(2)}, u32[]{:S(2)}) collective-permute-start(bf16[256,512]{1,0:T(8,128)(2,1)S(1)} %get-tuple-element.50), channel_id=1, source_target_pairs={{0,32},{32,64},{64,96},{96,128},{128,160},{160,192},{192,224},{224... | collective-permute-start | bytes 786440 | tf_op jit(solution)/shard_map/ppermute | solution.py:214
  120.5 0.5 collective-permute-done.8.down_ref
  121.0 8.2 %collective-permute-done.7.up_ref = bf16[256,512]{1,0:T(8,128)(2,1)S(1)} collective-permute-done((bf16[256,512]{1,0:T(8,128)(2,1)S(1)}, bf16[256,512]{1,0:T(8,128)(2,1)S(1)}, u32[]{:S(2)}, u32[]{:S(2)}) %collective-permute-start.7) | collective-permute-done | bytes 262176 | tf_op jit(solution)/shard_map/ppermute | solution.py:214
  129.2 0.1 shard_map.79
  129.2 4.8 %collective-permute-start.9 = (bf16[64,512]{1,0:T(8,128)(2,1)S(1)}, bf16[64,512]{1,0:T(8,128)(2,1)S(1)}, u32[]{:S(2)}, u32[]{:S(2)}) collective-permute-start(bf16[64,512]{1,0:T(8,128)(2,1)S(1)} %get-tuple-element.48), channel_id=1, source_target_pairs={{0,128},{32,160},{64,192},{96,224},{128,256},{160,288},{192,320},{... | collective-permute-start | bytes 196616 | tf_op jit(solution)/shard_map/ppermute | solution.py:214
  134.1 4.9 %collective-permute-start.11 = (bf16[64,512]{1,0:T(8,128)(2,1)S(1)}, bf16[64,512]{1,0:T(8,128)(2,1)S(1)}, u32[]{:S(2)}, u32[]{:S(2)}) collective-permute-start(bf16[64,512]{1,0:T(8,128)(2,1)S(1)} %get-tuple-element.49), channel_id=1, source_target_pairs={{0,384},{32,416},{64,448},{96,480},{128,0},{160,32},{192,64},{224,... | collective-permute-start | bytes 196616 | tf_op jit(solution)/shard_map/ppermute | solution.py:214
  139.0 1.8 %collective-permute-done.9 = bf16[64,512]{1,0:T(8,128)(2,1)S(1)} collective-permute-done((bf16[64,512]{1,0:T(8,128)(2,1)S(1)}, bf16[64,512]{1,0:T(8,128)(2,1)S(1)}, u32[]{:S(2)}, u32[]{:S(2)}) %collective-permute-start.9) | collective-permute-done | bytes 65568 | tf_op jit(solution)/shard_map/ppermute | solution.py:214
  140.8 4.7 %collective-permute-start.10 = (bf16[64,512]{1,0:T(8,128)(2,1)S(1)}, bf16[64,512]{1,0:T(8,128)(2,1)S(1)}, u32[]{:S(2)}, u32[]{:S(2)}) collective-permute-start(bf16[64,512]{1,0:T(8,128)(2,1)S(1)} %add_convert_fusion.1), channel_id=1, source_target_pairs={{0,128},{32,160},{64,192},{96,224},{128,256},{160,288},{192,320},{... | collective-permute-start | bytes 196616 | tf_op jit(solution)/shard_map/ppermute | solution.py:214
  145.5 6.3 %collective-permute-done.10 = bf16[64,512]{1,0:T(8,128)(2,1)S(1)} collective-permute-done((bf16[64,512]{1,0:T(8,128)(2,1)S(1)}, bf16[64,512]{1,0:T(8,128)(2,1)S(1)}, u32[]{:S(2)}, u32[]{:S(2)}) %collective-permute-start.10) | collective-permute-done | bytes 65568 | tf_op jit(solution)/shard_map/ppermute | solution.py:214
  151.8 1.3 fusion.16
  (10 shorter events, 0.1 us)
Async XLA Ops:
  0.6 80.2 %copy-start = (f32[512,512]{1,0:T(8,128)S(1)}, f32[512,512]{1,0:T(8,128)}, u32[]{:S(2)}) copy-start(f32[512,512]{1,0:T(8,128)} %param.7) | copy-start | bytes 3145732
  29.5 11.7 %collective-permute-start = (bf16[256,512]{1,0:T(8,128)(2,1)S(1)}, bf16[256,512]{1,0:T(8,128)(2,1)S(1)}, u32[]{:S(2)}, u32[]{:S(2)}) collective-permute-start(bf16[256,512]{1,0:T(8,128)(2,1)S(1)} %all_gather.3), channel_id=1, source_target_pairs={{0,480},{32,0},{64,32},{96,64},{128,96},{160,128},{192,160},{224,1... | collective-permute-start | bytes 786440 | tf_op jit(solution)/shard_map/ppermute | solution.py:214
  33.5 7.8 %collective-permute-start.1 = (s32[8,1152]{1,0:T(8,128)}, s32[8,1152]{1,0:T(8,128)S(1)}, u32[]{:S(2)}, u32[]{:S(2)}) collective-permute-start(s32[8,1152]{1,0:T(8,128)} %get-tuple-element.27), channel_id=1, source_target_pairs={{0,16},{16,0},{1,17},{17,1},{2,18},{18,2},{3,19},{19,3},{4,20},{20... | collective-permute-start | bytes 110600 | tf_op jit(solution)/shard_map/ppermute | solution.py:233
  38.4 11.6 %collective-permute-start.2 = (bf16[256,512]{1,0:T(8,128)(2,1)S(1)}, bf16[256,512]{1,0:T(8,128)(2,1)S(1)}, u32[]{:S(2)}, u32[]{:S(2)}) collective-permute-start(bf16[256,512]{1,0:T(8,128)(2,1)S(1)} %all_gather.3), channel_id=1, source_target_pairs={{0,32},{32,64},{64,96},{96,128},{128,160},{160,192},{192,224},{224... | collective-permute-start | bytes 786440 | tf_op jit(solution)/shard_map/ppermute | solution.py:214
  41.2 9.0 %collective-permute-start.3 = (bf16[256,512]{1,0:T(8,128)(2,1)S(1)}, bf16[256,512]{1,0:T(8,128)(2,1)S(1)}, u32[]{:S(2)}, u32[]{:S(2)}) collective-permute-start(bf16[256,512]{1,0:T(8,128)(2,1)S(1)} %collective-permute-done), channel_id=1, source_target_pairs={{0,480},{32,0},{64,32},{96,64},{128,96},{160,128},{192,160},{224,1... | collective-permute-start | bytes 786440 | tf_op jit(solution)/shard_map/ppermute | solution.py:214
  51.9 4.7 %collective-permute-start.4 = (f16[16,72,512]{2,1,0:T(8,128)(2,1)S(1)}, f16[16,72,512]{2,1,0:T(8,128)(2,1)S(1)}, u32[]{:S(2)}, u32[]{:S(2)}) collective-permute-start(f16[16,72,512]{2,1,0:T(8,128)(2,1)S(1)} %fusion.7), channel_id=1, source_target_pairs={{0,1},{1,0},{2,3},{3,2},{4,5},{5,4},{6,7},{7,6},{8,9},{9,8},{10,11... | collective-permute-start | bytes 3538952 | tf_op jit(solution)/shard_map/ppermute | solution.py:210
  57.0 23.8 %copy-start.1 = (f32[64,512]{1,0:T(8,128)S(1)}, f32[64,512]{1,0:T(8,128)}, u32[]{:S(2)}) copy-start(f32[64,512]{1,0:T(8,128)} %param.8) | copy-start | bytes 393220
  57.0 23.8 %copy-start.2 = (f32[64,512]{1,0:T(8,128)S(1)}, f32[64,512]{1,0:T(8,128)}, u32[]{:S(2)}) copy-start(f32[64,512]{1,0:T(8,128)} %features_ref.1) | copy-start | bytes 393220
  101.8 4.5 %collective-permute-start.5 = (bf16[1024,512]{1,0:T(8,128)(2,1)S(1)}, bf16[1024,512]{1,0:T(8,128)(2,1)S(1)}, u32[]{:S(2)}, u32[]{:S(2)}) collective-permute-start(bf16[1024,512]{1,0:T(8,128)(2,1)S(1)} %bitcast.21), channel_id=1, source_target_pairs={{0,1},{1,0},{2,3},{3,2},{4,5},{5,4},{6,7},{7,6},{8,9},{9,8},{10,11... | collective-permute-start | bytes 3145736 | tf_op jit(solution)/shard_map/ppermute | solution.py:210
  107.0 11.5 %collective-permute-start.6 = (bf16[256,512]{1,0:T(8,128)(2,1)S(1)}, bf16[256,512]{1,0:T(8,128)(2,1)S(1)}, u32[]{:S(2)}, u32[]{:S(2)}) collective-permute-start(bf16[256,512]{1,0:T(8,128)(2,1)S(1)} %add_convert_fusion), channel_id=1, source_target_pairs={{0,32},{32,64},{64,96},{96,128},{128,160},{160,192},{192,224},{224... | collective-permute-start | bytes 786440 | tf_op jit(solution)/shard_map/ppermute | solution.py:214
  110.3 10.7 %collective-permute-start.8 = (bf16[256,512]{1,0:T(8,128)(2,1)S(1)}, bf16[256,512]{1,0:T(8,128)(2,1)S(1)}, u32[]{:S(2)}, u32[]{:S(2)}) collective-permute-start(bf16[256,512]{1,0:T(8,128)(2,1)S(1)} %slice.63), channel_id=1, source_target_pairs={{0,480},{32,0},{64,32},{96,64},{128,96},{160,128},{192,160},{224,1... | collective-permute-start | bytes 786440 | tf_op jit(solution)/shard_map/ppermute | solution.py:214
  118.5 10.6 %collective-permute-start.7 = (bf16[256,512]{1,0:T(8,128)(2,1)S(1)}, bf16[256,512]{1,0:T(8,128)(2,1)S(1)}, u32[]{:S(2)}, u32[]{:S(2)}) collective-permute-start(bf16[256,512]{1,0:T(8,128)(2,1)S(1)} %get-tuple-element.50), channel_id=1, source_target_pairs={{0,32},{32,64},{64,96},{96,128},{128,160},{160,192},{192,224},{224... | collective-permute-start | bytes 786440 | tf_op jit(solution)/shard_map/ppermute | solution.py:214
  129.2 11.5 %collective-permute-start.9 = (bf16[64,512]{1,0:T(8,128)(2,1)S(1)}, bf16[64,512]{1,0:T(8,128)(2,1)S(1)}, u32[]{:S(2)}, u32[]{:S(2)}) collective-permute-start(bf16[64,512]{1,0:T(8,128)(2,1)S(1)} %get-tuple-element.48), channel_id=1, source_target_pairs={{0,128},{32,160},{64,192},{96,224},{128,256},{160,288},{192,320},{... | collective-permute-start | bytes 196616 | tf_op jit(solution)/shard_map/ppermute | solution.py:214
  134.1 11.4 %collective-permute-start.11 = (bf16[64,512]{1,0:T(8,128)(2,1)S(1)}, bf16[64,512]{1,0:T(8,128)(2,1)S(1)}, u32[]{:S(2)}, u32[]{:S(2)}) collective-permute-start(bf16[64,512]{1,0:T(8,128)(2,1)S(1)} %get-tuple-element.49), channel_id=1, source_target_pairs={{0,384},{32,416},{64,448},{96,480},{128,0},{160,32},{192,64},{224,... | collective-permute-start | bytes 196616 | tf_op jit(solution)/shard_map/ppermute | solution.py:214
  140.8 11.0 %collective-permute-start.10 = (bf16[64,512]{1,0:T(8,128)(2,1)S(1)}, bf16[64,512]{1,0:T(8,128)(2,1)S(1)}, u32[]{:S(2)}, u32[]{:S(2)}) collective-permute-start(bf16[64,512]{1,0:T(8,128)(2,1)S(1)} %add_convert_fusion.1), channel_id=1, source_target_pairs={{0,128},{32,160},{64,192},{96,224},{128,256},{160,288},{192,320},{... | collective-permute-start | bytes 196616 | tf_op jit(solution)/shard_map/ppermute | solution.py:214

commit v8 on v6

--- a/solution.py
+++ b/solution.py
@@ -102,7 +102,9 @@
     masks = (codes_ref[:, R + COLS : R + COLS + N_Z], from_x_ref[:, R : R + N_Z])
     mask = jnp.concatenate([jnp.where(x_hi == x, *masks) for x in range(N_X_HI)], axis=0)
     mask = mask.astype(jnp.float32).astype(jnp.bfloat16)
-    limit = jnp.dot(mask, spread, preferred_element_type=jnp.float32) * place_ref[3].astype(jnp.float32)
+    threshold = place_ref[3].astype(jnp.float32)
+    middle = (threshold - 1.0) * 0.5
+    reach = jnp.dot(mask, spread, preferred_element_type=jnp.float32) * (threshold * 0.5)
 
     for crossed, (block_ref, degree_ref) in enumerate(((own_ref, own_degree_ref), (cross_ref, cross_degree_ref))):
         for pair in range(N_XY // 2):
@@ -114,7 +116,7 @@
             kept = []
             for k in range(2):
                 part = residue[k * RPD : (k + 1) * RPD]
-                inside = jnp.logical_and(part >= 0.0, part < limit[2 * pair + k][None, :])
+                inside = jnp.abs(part - middle) < reach[2 * pair + k][None, :]
                 kept.append(jnp.where(inside, 1.0, 0.0))
             low = jnp.concatenate(kept, axis=0).astype(jnp.bfloat16)
             block_ref[at, :] = low

time: 153 us -> 153 us (level)
  no operation moved by 1% of the time
where the time goes in v8:
time: 153 us; the launch traced here: 152 us
  blocking collectives  70.8 us (46%)
  starting transfers between devices  42.3 us (28%)
  waiting for transfers between devices  22.7 us (15%)
  matrix products  7.91 us (5%)
  Pallas kernels  5.18 us (3%)
  other arithmetic  1.59 us (1%)
    ppermute x9, starting transfers between devices, along_z(): return lax.ppermute(values, Z, [(z, (z + step) % N_Z) for z in range(N_Z)])  33.5 us
    all_gather x1, blocking collectives, per_device(): block = lax.all_gather(low, 'zh', axis=0, tiled=True)  27.1 us
    all_to_all x1, blocking collectives, per_device(): arrived = lax.all_to_all(sent, XY, 0, 0).astype(jnp.float32).sum(axis=0)  23.9 us
    all_to_all x1, blocking collectives, exchange(): return lax.all_to_all(values, axis, 0, 0, tiled=True)  19.7 us
    ppermute x9, waiting for transfers between devices, along_z(): return lax.ppermute(values, Z, [(z, (z + step) % N_Z) for z in range(N_Z)])  19.3 us
    ppermute x1, starting transfers between devices, per_device(): from_x = lax.ppermute(shared, 'xh', [(0, 1), (1, 0)])  4.93 us
    ppermute x2, starting transfers between devices, to_other_core(): return lax.ppermute(values, 'c', [(0, 1), (1, 0)])  3.83 us
    pallas_call x1, Pallas kernels, build_adjacency(): pl.pallas_call(adjacency_kernel, in_specs=[pl.BlockSpec(memory_space=pltp...  3.38 us
  transfers between devices with their start and end apart: 12, of which 8 were waited for; matrix products, arithmetic and copies ran while one was open for 3% of the time, Pallas kernels for 2%

profile of v8, /device:TPU:8, one launch (start us, length us, event | category | flops | bytes accessed | tf_op | source)
XLA Modules:
  0.0 152.5 jit_solution(2228739700007494296)
XLA Ops:
  0.6 0.0 copy-start
  0.6 1.7 %shard_map.77 = (bf16[64,512]{1,0:T(8,128)(2,1)}, s32[8,3200]{1,0:T(8,128)}, s32[8,1152]{1,0:T(8,128)}) custom-call(f32[64,512]{1,0:T(8,128)} %features_ref.1, s32[2,1024]{1,0:T(2,128)} %rows_ref.1, s32[2,2048]{1,0:T(2,128)} %columns_ref.1, s32[8,16]{1,0:T(8,128)} %mask_ref.1), custom_call_target="tpu_custom_call" | custom-call | tf_op jit(solution)/shard_map/pallas_call | solution.py:169
  2.4 27.1 %all_gather.3 = bf16[256,512]{1,0:T(8,128)(2,1)S(1)} all-gather(bf16[64,512]{1,0:T(8,128)(2,1)} %get-tuple-element.25), channel_id=1, replica_groups=mesh['zh'=4,'zl'=4,'xh'=2,'xl'=2,'y'=4,'c'=2] {'zh'}, dimensions={0}, use_global_device_ids=true | all-gather | bytes 327680 | tf_op jit(solution)/shard_map/all_gather | solution.py:236
  29.5 4.0 %collective-permute-start = (bf16[256,512]{1,0:T(8,128)(2,1)S(1)}, bf16[256,512]{1,0:T(8,128)(2,1)S(1)}, u32[]{:S(2)}, u32[]{:S(2)}) collective-permute-start(bf16[256,512]{1,0:T(8,128)(2,1)S(1)} %all_gather.3), channel_id=1, source_target_pairs={{0,480},{32,0},{64,32},{96,64},{128,96},{160,128},{192,160},{224,1... | collective-permute-start | bytes 786440 | tf_op jit(solution)/shard_map/ppermute | solution.py:216
  33.5 4.9 %collective-permute-start.1 = (s32[8,1152]{1,0:T(8,128)}, s32[8,1152]{1,0:T(8,128)S(1)}, u32[]{:S(2)}, u32[]{:S(2)}) collective-permute-start(s32[8,1152]{1,0:T(8,128)} %get-tuple-element.26), channel_id=1, source_target_pairs={{0,16},{16,0},{1,17},{17,1},{2,18},{18,2},{3,19},{19,3},{4,20},{20... | collective-permute-start | bytes 110600 | tf_op jit(solution)/shard_map/ppermute | solution.py:235
  38.4 1.9 %collective-permute-start.2 = (bf16[256,512]{1,0:T(8,128)(2,1)S(1)}, bf16[256,512]{1,0:T(8,128)(2,1)S(1)}, u32[]{:S(2)}, u32[]{:S(2)}) collective-permute-start(bf16[256,512]{1,0:T(8,128)(2,1)S(1)} %all_gather.3), channel_id=1, source_target_pairs={{0,32},{32,64},{64,96},{96,128},{128,160},{160,192},{192,224},{224... | collective-permute-start | bytes 786440 | tf_op jit(solution)/shard_map/ppermute | solution.py:216
  40.3 0.7 collective-permute-done.1.from_x_ref
  41.0 0.0 collective-permute-done
  41.0 4.5 %collective-permute-start.3 = (bf16[256,512]{1,0:T(8,128)(2,1)S(1)}, bf16[256,512]{1,0:T(8,128)(2,1)S(1)}, u32[]{:S(2)}, u32[]{:S(2)}) collective-permute-start(bf16[256,512]{1,0:T(8,128)(2,1)S(1)} %collective-permute-done), channel_id=1, source_target_pairs={{0,480},{32,0},{64,32},{96,64},{128,96},{160,128},{192,160},{224,1... | collective-permute-start | bytes 786440 | tf_op jit(solution)/shard_map/ppermute | solution.py:216
  45.5 0.1 pad_add_fusion.place_ref
  45.6 0.9 copy-done.1
  46.5 3.4 %shard_map.78 = (bf16[1024,1024]{1,0:T(8,128)(2,1)S(1)}, bf16[1024,1024]{1,0:T(8,128)(2,1)S(1)}, f32[16,8,128]{2,1,0:T(8,128)S(1)}, f32[16,8,128]{2,1,0:T(8,128)S(1)}) custom-call(s32[4]{0:T(128)S(1)} %pad_add_fusion.place_ref, s32[8,3200]{1,0:T(8,128)S(1)} %copy-done.1, s32[8,1152]{1,0:T(8,128)S(1)} %collective-permute-done.1.from_x_ref), custom_call_target="tpu_custom_call" | custom-call | flops 67108864 | bytes 4194304 | tf_op jit(solution)/shard_map/pallas_call | solution.py:134
  49.9 0.1 pad_maximum_fusion
  50.0 1.2 convolution_convert_fusion
  51.2 0.3 fusion.7
  51.5 1.9 %collective-permute-start.4 = (f16[16,72,512]{2,1,0:T(8,128)(2,1)S(1)}, f16[16,72,512]{2,1,0:T(8,128)(2,1)S(1)}, u32[]{:S(2)}, u32[]{:S(2)}) collective-permute-start(f16[16,72,512]{2,1,0:T(8,128)(2,1)S(1)} %fusion.7), channel_id=1, source_target_pairs={{0,1},{1,0},{2,3},{3,2},{4,5},{5,4},{6,7},{7,6},{8,9},{9,8},{10,11... | collective-permute-start | bytes 3538952 | tf_op jit(solution)/shard_map/ppermute | solution.py:212
  53.4 1.2 fusion.26
  54.7 1.6 %collective-permute-done.4 = f16[16,72,512]{2,1,0:T(8,128)(2,1)S(1)} collective-permute-done((f16[16,72,512]{2,1,0:T(8,128)(2,1)S(1)}, f16[16,72,512]{2,1,0:T(8,128)(2,1)S(1)}, u32[]{:S(2)}, u32[]{:S(2)}) %collective-permute-start.4) | collective-permute-done | bytes 1179680 | tf_op jit(solution)/shard_map/ppermute | solution.py:212
  56.3 0.4 fusion.1
  56.7 0.0 copy-start.2
  56.7 0.0 copy-start.3
  56.7 23.9 %all_to_all.14 = f16[16,72,512]{2,1,0:T(8,128)(2,1)S(1)} all-to-all(f16[16,72,512]{2,1,0:T(8,128)(2,1)S(1)} %fusion.1), channel_id=1, replica_groups=mesh['zh'=4,'zl'=4,'xh'=2,'xl'=2,'y'=4,'c'=2] {'xh','xl','y'}, dimensions={0} | all-to-all | bytes 2359296 | tf_op jit(solution)/shard_map/all_to_all | solution.py:253
  80.6 0.2 convert_reduce_fusion
  80.8 1.2 fusion.25
  82.0 0.1 broadcast_in_dim.2
  82.1 19.7 %all_to_all.15 = bf16[16,64,512]{2,1,0:T(8,128)(2,1)S(1)} all-to-all(bf16[16,64,512]{2,1,0:T(8,128)(2,1)S(1)} %broadcast_in_dim.2), channel_id=1, replica_groups=mesh['zh'=4,'zl'=4,'xh'=2,'xl'=2,'y'=4,'c'=2] {'xh','xl','y'}, dimensions={0} | all-to-all | bytes 2097152 | tf_op jit(solution)/shard_map/all_to_all | solution.py:220
  101.8 1.9 %collective-permute-start.5 = (bf16[1024,512]{1,0:T(8,128)(2,1)S(1)}, bf16[1024,512]{1,0:T(8,128)(2,1)S(1)}, u32[]{:S(2)}, u32[]{:S(2)}) collective-permute-start(bf16[1024,512]{1,0:T(8,128)(2,1)S(1)} %bitcast.21), channel_id=1, source_target_pairs={{0,1},{1,0},{2,3},{3,2},{4,5},{5,4},{6,7},{7,6},{8,9},{9,8},{10,11... | collective-permute-start | bytes 3145736 | tf_op jit(solution)/shard_map/ppermute | solution.py:212
  103.8 0.5 fusion.11
  104.2 1.0 fusion.5
  105.2 1.1 collective-permute-done.5
  106.4 0.5 fusion.9
  106.9 0.1 add_convert_fusion
  107.0 2.0 %collective-permute-start.6 = (bf16[256,512]{1,0:T(8,128)(2,1)S(1)}, bf16[256,512]{1,0:T(8,128)(2,1)S(1)}, u32[]{:S(2)}, u32[]{:S(2)}) collective-permute-start(bf16[256,512]{1,0:T(8,128)(2,1)S(1)} %add_convert_fusion), channel_id=1, source_target_pairs={{0,32},{32,64},{64,96},{96,128},{128,160},{160,192},{192,224},{224... | collective-permute-start | bytes 786440 | tf_op jit(solution)/shard_map/ppermute | solution.py:216
  109.0 1.0 fusion.3
  110.0 0.3 add.66
  110.4 5.0 %collective-permute-start.8 = (bf16[256,512]{1,0:T(8,128)(2,1)S(1)}, bf16[256,512]{1,0:T(8,128)(2,1)S(1)}, u32[]{:S(2)}, u32[]{:S(2)}) collective-permute-start(bf16[256,512]{1,0:T(8,128)(2,1)S(1)} %slice.63), channel_id=1, source_target_pairs={{0,480},{32,0},{64,32},{96,64},{128,96},{160,128},{192,160},{224,1... | collective-permute-start | bytes 786440 | tf_op jit(solution)/shard_map/ppermute | solution.py:216
  115.4 3.0 %collective-permute-done.6 = bf16[256,512]{1,0:T(8,128)(2,1)S(1)} collective-permute-done((bf16[256,512]{1,0:T(8,128)(2,1)S(1)}, bf16[256,512]{1,0:T(8,128)(2,1)S(1)}, u32[]{:S(2)}, u32[]{:S(2)}) %collective-permute-start.6) | collective-permute-done | bytes 262176 | tf_op jit(solution)/shard_map/ppermute | solution.py:216
  118.4 0.1 fusion.8
  118.5 1.9 %collective-permute-start.7 = (bf16[256,512]{1,0:T(8,128)(2,1)S(1)}, bf16[256,512]{1,0:T(8,128)(2,1)S(1)}, u32[]{:S(2)}, u32[]{:S(2)}) collective-permute-start(bf16[256,512]{1,0:T(8,128)(2,1)S(1)} %get-tuple-element.48), channel_id=1, source_target_pairs={{0,32},{32,64},{64,96},{96,128},{128,160},{160,192},{192,224},{224... | collective-permute-start | bytes 786440 | tf_op jit(solution)/shard_map/ppermute | solution.py:216
  120.5 0.5 collective-permute-done.8.down_ref
  121.0 8.2 %collective-permute-done.7.up_ref = bf16[256,512]{1,0:T(8,128)(2,1)S(1)} collective-permute-done((bf16[256,512]{1,0:T(8,128)(2,1)S(1)}, bf16[256,512]{1,0:T(8,128)(2,1)S(1)}, u32[]{:S(2)}, u32[]{:S(2)}) %collective-permute-start.7) | collective-permute-done | bytes 262176 | tf_op jit(solution)/shard_map/ppermute | solution.py:216
  129.2 0.1 shard_map.79
  129.2 4.8 %collective-permute-start.9 = (bf16[64,512]{1,0:T(8,128)(2,1)S(1)}, bf16[64,512]{1,0:T(8,128)(2,1)S(1)}, u32[]{:S(2)}, u32[]{:S(2)}) collective-permute-start(bf16[64,512]{1,0:T(8,128)(2,1)S(1)} %get-tuple-element.46), channel_id=1, source_target_pairs={{0,128},{32,160},{64,192},{96,224},{128,256},{160,288},{192,320},{... | collective-permute-start | bytes 196616 | tf_op jit(solution)/shard_map/ppermute | solution.py:216
  134.1 4.9 %collective-permute-start.11 = (bf16[64,512]{1,0:T(8,128)(2,1)S(1)}, bf16[64,512]{1,0:T(8,128)(2,1)S(1)}, u32[]{:S(2)}, u32[]{:S(2)}) collective-permute-start(bf16[64,512]{1,0:T(8,128)(2,1)S(1)} %get-tuple-element.47), channel_id=1, source_target_pairs={{0,384},{32,416},{64,448},{96,480},{128,0},{160,32},{192,64},{224,... | collective-permute-start | bytes 196616 | tf_op jit(solution)/shard_map/ppermute | solution.py:216
  139.0 1.2 collective-permute-done.9
  140.2 4.5 %collective-permute-start.10 = (bf16[64,512]{1,0:T(8,128)(2,1)S(1)}, bf16[64,512]{1,0:T(8,128)(2,1)S(1)}, u32[]{:S(2)}, u32[]{:S(2)}) collective-permute-start(bf16[64,512]{1,0:T(8,128)(2,1)S(1)} %add_convert_fusion.1), channel_id=1, source_target_pairs={{0,128},{32,160},{64,192},{96,224},{128,256},{160,288},{192,320},{... | collective-permute-start | bytes 196616 | tf_op jit(solution)/shard_map/ppermute | solution.py:216
  144.7 6.5 %collective-permute-done.10 = bf16[64,512]{1,0:T(8,128)(2,1)S(1)} collective-permute-done((bf16[64,512]{1,0:T(8,128)(2,1)S(1)}, bf16[64,512]{1,0:T(8,128)(2,1)S(1)}, u32[]{:S(2)}, u32[]{:S(2)}) %collective-permute-start.10) | collective-permute-done | bytes 65568 | tf_op jit(solution)/shard_map/ppermute | solution.py:216
  151.2 1.3 fusion.16
  (11 shorter events, 0.1 us)
Async XLA Ops:
  0.6 80.2 %copy-start = (f32[512,512]{1,0:T(8,128)S(1)}, f32[512,512]{1,0:T(8,128)}, u32[]{:S(2)}) copy-start(f32[512,512]{1,0:T(8,128)} %param.7) | copy-start | bytes 3145732
  29.5 11.5 %collective-permute-start = (bf16[256,512]{1,0:T(8,128)(2,1)S(1)}, bf16[256,512]{1,0:T(8,128)(2,1)S(1)}, u32[]{:S(2)}, u32[]{:S(2)}) collective-permute-start(bf16[256,512]{1,0:T(8,128)(2,1)S(1)} %all_gather.3), channel_id=1, source_target_pairs={{0,480},{32,0},{64,32},{96,64},{128,96},{160,128},{192,160},{224,1... | collective-permute-start | bytes 786440 | tf_op jit(solution)/shard_map/ppermute | solution.py:216
  33.5 7.6 %collective-permute-start.1 = (s32[8,1152]{1,0:T(8,128)}, s32[8,1152]{1,0:T(8,128)S(1)}, u32[]{:S(2)}, u32[]{:S(2)}) collective-permute-start(s32[8,1152]{1,0:T(8,128)} %get-tuple-element.26), channel_id=1, source_target_pairs={{0,16},{16,0},{1,17},{17,1},{2,18},{18,2},{3,19},{19,3},{4,20},{20... | collective-permute-start | bytes 110600 | tf_op jit(solution)/shard_map/ppermute | solution.py:235
  38.4 11.5 %collective-permute-start.2 = (bf16[256,512]{1,0:T(8,128)(2,1)S(1)}, bf16[256,512]{1,0:T(8,128)(2,1)S(1)}, u32[]{:S(2)}, u32[]{:S(2)}) collective-permute-start(bf16[256,512]{1,0:T(8,128)(2,1)S(1)} %all_gather.3), channel_id=1, source_target_pairs={{0,32},{32,64},{64,96},{96,128},{128,160},{160,192},{192,224},{224... | collective-permute-start | bytes 786440 | tf_op jit(solution)/shard_map/ppermute | solution.py:216
  41.0 8.9 %collective-permute-start.3 = (bf16[256,512]{1,0:T(8,128)(2,1)S(1)}, bf16[256,512]{1,0:T(8,128)(2,1)S(1)}, u32[]{:S(2)}, u32[]{:S(2)}) collective-permute-start(bf16[256,512]{1,0:T(8,128)(2,1)S(1)} %collective-permute-done), channel_id=1, source_target_pairs={{0,480},{32,0},{64,32},{96,64},{128,96},{160,128},{192,160},{224,1... | collective-permute-start | bytes 786440 | tf_op jit(solution)/shard_map/ppermute | solution.py:216
  45.6 0.9 copy-start.1
  51.5 4.7 %collective-permute-start.4 = (f16[16,72,512]{2,1,0:T(8,128)(2,1)S(1)}, f16[16,72,512]{2,1,0:T(8,128)(2,1)S(1)}, u32[]{:S(2)}, u32[]{:S(2)}) collective-permute-start(f16[16,72,512]{2,1,0:T(8,128)(2,1)S(1)} %fusion.7), channel_id=1, source_target_pairs={{0,1},{1,0},{2,3},{3,2},{4,5},{5,4},{6,7},{7,6},{8,9},{9,8},{10,11... | collective-permute-start | bytes 3538952 | tf_op jit(solution)/shard_map/ppermute | solution.py:212
  56.7 24.1 %copy-start.2 = (f32[64,512]{1,0:T(8,128)S(1)}, f32[64,512]{1,0:T(8,128)}, u32[]{:S(2)}) copy-start(f32[64,512]{1,0:T(8,128)} %param.8) | copy-start | bytes 393220
  56.7 24.1 %copy-start.3 = (f32[64,512]{1,0:T(8,128)S(1)}, f32[64,512]{1,0:T(8,128)}, u32[]{:S(2)}) copy-start(f32[64,512]{1,0:T(8,128)} %features_ref.1) | copy-start | bytes 393220
  101.8 4.5 %collective-permute-start.5 = (bf16[1024,512]{1,0:T(8,128)(2,1)S(1)}, bf16[1024,512]{1,0:T(8,128)(2,1)S(1)}, u32[]{:S(2)}, u32[]{:S(2)}) collective-permute-start(bf16[1024,512]{1,0:T(8,128)(2,1)S(1)} %bitcast.21), channel_id=1, source_target_pairs={{0,1},{1,0},{2,3},{3,2},{4,5},{5,4},{6,7},{7,6},{8,9},{9,8},{10,11... | collective-permute-start | bytes 3145736 | tf_op jit(solution)/shard_map/ppermute | solution.py:212
  107.0 11.5 %collective-permute-start.6 = (bf16[256,512]{1,0:T(8,128)(2,1)S(1)}, bf16[256,512]{1,0:T(8,128)(2,1)S(1)}, u32[]{:S(2)}, u32[]{:S(2)}) collective-permute-start(bf16[256,512]{1,0:T(8,128)(2,1)S(1)} %add_convert_fusion), channel_id=1, source_target_pairs={{0,32},{32,64},{64,96},{96,128},{128,160},{160,192},{192,224},{224... | collective-permute-start | bytes 786440 | tf_op jit(solution)/shard_map/ppermute | solution.py:216
  110.4 10.6 %collective-permute-start.8 = (bf16[256,512]{1,0:T(8,128)(2,1)S(1)}, bf16[256,512]{1,0:T(8,128)(2,1)S(1)}, u32[]{:S(2)}, u32[]{:S(2)}) collective-permute-start(bf16[256,512]{1,0:T(8,128)(2,1)S(1)} %slice.63), channel_id=1, source_target_pairs={{0,480},{32,0},{64,32},{96,64},{128,96},{160,128},{192,160},{224,1... | collective-permute-start | bytes 786440 | tf_op jit(solution)/shard_map/ppermute | solution.py:216
  118.5 10.6 %collective-permute-start.7 = (bf16[256,512]{1,0:T(8,128)(2,1)S(1)}, bf16[256,512]{1,0:T(8,128)(2,1)S(1)}, u32[]{:S(2)}, u32[]{:S(2)}) collective-permute-start(bf16[256,512]{1,0:T(8,128)(2,1)S(1)} %get-tuple-element.48), channel_id=1, source_target_pairs={{0,32},{32,64},{64,96},{96,128},{128,160},{160,192},{192,224},{224... | collective-permute-start | bytes 786440 | tf_op jit(solution)/shard_map/ppermute | solution.py:216
  129.2 11.0 %collective-permute-start.9 = (bf16[64,512]{1,0:T(8,128)(2,1)S(1)}, bf16[64,512]{1,0:T(8,128)(2,1)S(1)}, u32[]{:S(2)}, u32[]{:S(2)}) collective-permute-start(bf16[64,512]{1,0:T(8,128)(2,1)S(1)} %get-tuple-element.46), channel_id=1, source_target_pairs={{0,128},{32,160},{64,192},{96,224},{128,256},{160,288},{192,320},{... | collective-permute-start | bytes 196616 | tf_op jit(solution)/shard_map/ppermute | solution.py:216
  134.1 10.7 %collective-permute-start.11 = (bf16[64,512]{1,0:T(8,128)(2,1)S(1)}, bf16[64,512]{1,0:T(8,128)(2,1)S(1)}, u32[]{:S(2)}, u32[]{:S(2)}) collective-permute-start(bf16[64,512]{1,0:T(8,128)(2,1)S(1)} %get-tuple-element.47), channel_id=1, source_target_pairs={{0,384},{32,416},{64,448},{96,480},{128,0},{160,32},{192,64},{224,... | collective-permute-start | bytes 196616 | tf_op jit(solution)/shard_map/ppermute | solution.py:216
  140.2 11.0 %collective-permute-start.10 = (bf16[64,512]{1,0:T(8,128)(2,1)S(1)}, bf16[64,512]{1,0:T(8,128)(2,1)S(1)}, u32[]{:S(2)}, u32[]{:S(2)}) collective-permute-start(bf16[64,512]{1,0:T(8,128)(2,1)S(1)} %add_convert_fusion.1), channel_id=1, source_target_pairs={{0,128},{32,160},{64,192},{96,224},{128,256},{160,288},{192,320},{... | collective-permute-start | bytes 196616 | tf_op jit(solution)/shard_map/ppermute | solution.py:216
